TPU v7x, 128 devices: a whole 4x4x4 slice. The times are simulated.
128 devices in a mesh: rows: 8 (over z_lo, x), seq: 16 (over y, z_hi, core).
Axes of the slice: x: 4, y: 4, z: 4 (z_hi: 2, z_lo: 2; z = z_hi * 2 + z_lo), core: 2. Of those that a mesh axis runs over, the one named last changes fastest.
Arguments:
- tokens: bfloat16 [16, 2048, 768], P('rows', 'seq'), may hold values from -6 to 6
- lengths: int32 [16], P('rows'), may hold values from 1 to 2048, as said below
- cotangent: bfloat16 [16, 2048, 768], P('rows', 'seq'), may hold values from -6 to 6
- query_weight: float32 [768, 768], P(('rows', 'seq')), may hold values from -0.0546875 to 0.0546875
- key_weight: float32 [768, 768], P(('rows', 'seq')), may hold values from -0.21875 to 0.21875
- value_weight: float32 [768, 768], P(('rows', 'seq')), may hold values from -0.21875 to 0.21875
- out_weight: float32 [768, 768], P(('rows', 'seq')), may hold values from -2.5 to 2.5
- gate_weight: float32 [768, 2048], P(('rows', 'seq')), may hold values from -0.21875 to 0.21875
- up_weight: float32 [768, 2048], P(('rows', 'seq')), may hold values from -0.21875 to 0.21875
- down_weight: float32 [2048, 768], P(('rows', 'seq')), may hold values from -0.125 to 0.125
- first_gain: float32 [768], P(('rows', 'seq')), may hold values from 0.25 to 1.75
- second_gain: float32 [768], P(('rows', 'seq')), may hold values from 0.25 to 1.75
- bias_table: float32 [384], P(('rows', 'seq')), may hold values from -3 to 3
Outputs:
- output: bfloat16 [16, 2048, 768], P('rows', 'seq')
- input_grad: float32 [16, 2048, 768], P('rows', 'seq')
- query_weight_grad: float32 [768, 768], P(('rows', 'seq'))
- key_weight_grad: float32 [768, 768], P(('rows', 'seq'))
- value_weight_grad: float32 [768, 768], P(('rows', 'seq'))
- out_weight_grad: float32 [768, 768], P(('rows', 'seq'))
- gate_weight_grad: float32 [768, 2048], P(('rows', 'seq'))
- up_weight_grad: float32 [768, 2048], P(('rows', 'seq'))
- down_weight_grad: float32 [2048, 768], P(('rows', 'seq'))
- first_gain_grad: float32 [768], P(('rows', 'seq'))
- second_gain_grad: float32 [768], P(('rows', 'seq'))
- bias_table_grad: float32 [384], P(('rows', 'seq'))
Inputs may be any that keep to these rules, and one draw needn't show every extreme that they name: Row b's first lengths[b] tokens are valid, the rest are padding; at least one row has all 2048 tokens valid.
All inputs are finite; a program needn't handle non-finite values.
Results may differ from a plain program's by a relative error of at most 0.039.
Values may be sent and summed in bfloat16 or wider, within the bound.
A program may use at most 192 MiB of HBM per device.

v0:
```python
import math

import jax
import jax.numpy as jnp
from jax import lax
from jax.sharding import PartitionSpec as P

HEADS = 12
HEAD_DIM = 64
BUCKETS = 32


EPSILON = 1e-06
NEGATIVE = -1e30
LIMITS = (1, 2, 3, 4, 5, 6, 7, 8, 12, 16, 23, 32, 46, 64, 91)


def laid_out(parts, dim):
    lengths = list(parts.shape[1:])
    lengths[dim] *= parts.shape[0]
    return jnp.moveaxis(parts, 0, dim).reshape(lengths)


def gather_together(arrays, axis, dims):
    vector = jnp.concatenate([a.reshape(-1) for a in arrays])
    lines, at, done = (lax.all_gather(vector, axis), 0, [])
    for a, dim in zip(arrays, dims):
        parts = lines[:, at : at + a.size].reshape(-1, *a.shape)
        done.append(laid_out(parts, dim))
        at += a.size
    return tuple(done)


def sent_together(arrays, axis, dim, along):
    widths = [a.shape[along] for a in arrays]
    both = jnp.concatenate(arrays, axis=along)
    whole = lax.all_gather(both, axis, axis=dim, tiled=True)
    return tuple(jnp.split(whole, [sum(widths[:k]) for k in range(1, len(widths))], axis=along))


def in_one_piece(arrays, axis, dim, along):
    both = jnp.concatenate(arrays, axis=along)
    whole, at, done = (lax.psum_scatter(both, axis, scatter_dimension=dim, tiled=True), 0, [])
    for a in arrays:
        done.append(lax.slice_in_dim(whole, at, at + a.shape[along], axis=along))
        at += a.shape[along]
    return tuple(done)


def cut_along(shard, dim, size):
    before, after = (shard.shape[:dim], shard.shape[dim + 1 :])
    return jnp.moveaxis(shard.reshape(*before, size, -1, *after), dim, 0)


def sum_packed(arrays, axis, dims):
    size = lax.axis_size(axis)
    parts = [cut_along(a, dim, size) for a, dim in zip(arrays, dims)]
    lines = jnp.concatenate([b.reshape(size, -1) for b in parts], axis=1)
    span = max(16, -(-lines.shape[1] // 1024) * 8)
    lines = jnp.pad(lines, ((0, 0), (0, span * 128 - lines.shape[1]))).reshape(-1, 128)
    vector, at, done = (lax.psum_scatter(lines, axis, tiled=True).reshape(-1), 0, [])
    for b in parts:
        part = b[0]
        done.append(vector[at : at + part.size].reshape(part.shape))
        at += part.size
    return tuple(done)


def bucket_ids(offsets):
    distance = jnp.abs(offsets)
    bucket_sum = (offsets > 0).astype(jnp.int32) * (BUCKETS // 2)
    for threshold in LIMITS:
        bucket_sum = bucket_sum + (distance >= threshold).astype(jnp.int32)
    return bucket_sum


def rms_norm(values, gain_vector):
    mean_square = jnp.mean(values * values, axis=-1, keepdims=True)
    return values * lax.rsqrt(mean_square + EPSILON) * gain_vector


def block_scores(query_part, key_part, query_at, key_at, table_mat, lengths):
    bucket_of = bucket_ids(key_at[None, :] - query_at[:, None])
    onehot = (bucket_of[:, :, None] == jnp.arange(BUCKETS, dtype=jnp.int32)).astype(jnp.bfloat16)
    bias_block = jnp.einsum("qkb,hb->hqk", onehot, table_mat, preferred_element_type=jnp.float32)
    scores = (
        jnp.einsum("rqhd,rkhd->rhqk", query_part, key_part, preferred_element_type=jnp.float32)
        + bias_block[None]
    )
    key_valid = key_at[None, :] < lengths[:, None]
    return (jnp.where(key_valid[:, None, None, :], scores, NEGATIVE), bucket_of)


def table_term(score_grad, bucket_of):
    selector = (bucket_of[:, :, None] == jnp.arange(BUCKETS, dtype=jnp.int32)).astype(jnp.bfloat16)
    upper = score_grad.astype(jnp.bfloat16)
    lower = (score_grad - upper.astype(jnp.float32)).astype(jnp.bfloat16)
    total = jnp.einsum("rhqk,qkb->hb", upper, selector, preferred_element_type=jnp.float32)
    return total + jnp.einsum("rhqk,qkb->hb", lower, selector, preferred_element_type=jnp.float32)


def per_device(
    tokens,
    lengths,
    cotangent,
    query_weight,
    key_weight,
    value_weight,
    out_weight,
    gate_weight,
    up_weight,
    down_weight,
    first_gain,
    second_gain,
    bias_table,
):
    gathered = gather_together(
        (
            query_weight.astype(jnp.bfloat16),
            key_weight.astype(jnp.bfloat16),
            value_weight.astype(jnp.bfloat16),
            out_weight.astype(jnp.bfloat16),
            gate_weight.astype(jnp.bfloat16),
            up_weight.astype(jnp.bfloat16),
            down_weight.astype(jnp.bfloat16),
            first_gain.astype(jnp.bfloat16),
            second_gain.astype(jnp.bfloat16),
            bias_table.astype(jnp.bfloat16),
        ),
        ("rows", "seq"),
        (0, 0, 0, 0, 0, 0, 0, 0, 0, 0),
    )
    (
        query_full,
        key_full,
        value_full,
        out_full,
        gate_full,
        up_full,
        down_full,
        gain_one,
        gain_two,
        table_full,
    ) = gathered
    table_mat = table_full.reshape(HEADS, BUCKETS)
    row_count, local_len, model_width = tokens.shape
    total_len = local_len * lax.axis_size("seq")
    token_count = row_count * local_len
    head_shape = (row_count, local_len, HEADS, HEAD_DIM)
    block_len = math.gcd(total_len, 1024)
    block_count = total_len // block_len
    block_ids = jnp.arange(block_count, dtype=jnp.int32)
    inputs = tokens.reshape(token_count, model_width).astype(jnp.float32)
    normed, first_pull = jax.vjp(rms_norm, inputs, gain_one.astype(jnp.float32))
    normed_low = normed.astype(jnp.bfloat16)
    queries = jnp.dot(normed_low, query_full, preferred_element_type=jnp.float32).astype(
        jnp.bfloat16
    )
    keys_rows = jnp.dot(normed_low, key_full, preferred_element_type=jnp.float32).astype(
        jnp.bfloat16
    )
    values_rows = jnp.dot(normed_low, value_full, preferred_element_type=jnp.float32).astype(
        jnp.bfloat16
    )
    query_heads = queries.reshape(head_shape)
    keys_all, values_all = sent_together(
        (
            keys_rows.reshape(row_count, local_len, model_width),
            values_rows.reshape(row_count, local_len, model_width),
        ),
        "seq",
        1,
        0,
    )
    query_pos = lax.axis_index("seq") * local_len + jnp.arange(local_len, dtype=jnp.int32)

    def key_slice(source, block_start):
        part_rows = lax.dynamic_slice_in_dim(source, block_start, block_len, 1)
        return part_rows.reshape(row_count, block_len, HEADS, HEAD_DIM)

    def stats_step(state_in, block_index):
        running_max, running_sum = state_in
        block_start = block_index * block_len
        key_at = block_start + jnp.arange(block_len, dtype=jnp.int32)
        scores = block_scores(
            query_heads, key_slice(keys_all, block_start), query_pos, key_at, table_mat, lengths
        )[0]
        new_max = jnp.maximum(running_max, jnp.max(scores, axis=-1))
        new_sum = running_sum * jnp.exp(running_max - new_max) + jnp.sum(
            jnp.exp(scores - new_max[..., None]), axis=-1
        )
        return ((new_max, new_sum), None)

    start_max = jnp.full((row_count, HEADS, local_len), NEGATIVE, jnp.float32)
    start_sum = jnp.zeros((row_count, HEADS, local_len), jnp.float32)
    final_max, final_sum = lax.scan(stats_step, (start_max, start_sum), block_ids)[0]
    log_total = final_max + jnp.log(final_sum)

    def mix_step(mixed_sum, block_index):
        block_start = block_index * block_len
        key_at = block_start + jnp.arange(block_len, dtype=jnp.int32)
        scores = block_scores(
            query_heads, key_slice(keys_all, block_start), query_pos, key_at, table_mat, lengths
        )[0]
        probs_low = jnp.exp(scores - log_total[..., None]).astype(jnp.bfloat16)
        return (
            mixed_sum
            + jnp.einsum(
                "rhqk,rkhd->rqhd",
                probs_low,
                key_slice(values_all, block_start),
                preferred_element_type=jnp.float32,
            ),
            None,
        )

    mixed_sum = lax.scan(mix_step, jnp.zeros(head_shape, jnp.float32), block_ids)[0]
    attended_low = mixed_sum.reshape(token_count, model_width).astype(jnp.bfloat16)
    middle = inputs + jnp.dot(attended_low, out_full, preferred_element_type=jnp.float32)
    normed_two, second_pull = jax.vjp(rms_norm, middle, gain_two.astype(jnp.float32))
    normed_two_low = normed_two.astype(jnp.bfloat16)
    gate_act = jnp.dot(normed_two_low, gate_full, preferred_element_type=jnp.float32)
    up_act = jnp.dot(normed_two_low, up_full, preferred_element_type=jnp.float32)
    product, gated_pull = jax.vjp(
        lambda gate_in, up_in: jax.nn.gelu(gate_in, approximate=True) * up_in, gate_act, up_act
    )
    hidden = product.astype(jnp.bfloat16)
    output = middle + jnp.dot(hidden, down_full, preferred_element_type=jnp.float32)
    output_low = output.astype(jnp.bfloat16).reshape(tokens.shape)
    upstream_low = cotangent.reshape(token_count, model_width)
    upstream = upstream_low.astype(jnp.float32)
    down_weight_grad = jnp.einsum(
        "nf,nd->fd", hidden, upstream_low, preferred_element_type=jnp.float32
    )
    hidden_grad = jnp.einsum(
        "nd,fd->nf", upstream_low, down_full, preferred_element_type=jnp.float32
    )
    gate_grad, up_grad = gated_pull(hidden_grad)
    gate_grad_low = gate_grad.astype(jnp.bfloat16)
    up_grad_low = up_grad.astype(jnp.bfloat16)
    gate_weight_grad = jnp.einsum(
        "nd,nf->df", normed_two_low, gate_grad_low, preferred_element_type=jnp.float32
    )
    up_weight_grad = jnp.einsum(
        "nd,nf->df", normed_two_low, up_grad_low, preferred_element_type=jnp.float32
    )
    normed_two_grad = jnp.einsum(
        "nf,df->nd", gate_grad_low, gate_full, preferred_element_type=jnp.float32
    ) + jnp.einsum("nf,df->nd", up_grad_low, up_full, preferred_element_type=jnp.float32)
    middle_norm_grad, second_gain_term = second_pull(normed_two_grad)
    middle_grad = upstream + middle_norm_grad
    middle_low = middle_grad.astype(jnp.bfloat16)
    out_weight_grad = jnp.einsum(
        "nd,ne->de", attended_low, middle_low, preferred_element_type=jnp.float32
    )
    grad_heads = (
        jnp.einsum("ne,de->nd", middle_low, out_full, preferred_element_type=jnp.float32)
        .astype(jnp.bfloat16)
        .reshape(head_shape)
    )
    row_delta = jnp.einsum(
        "rqhd,rqhd->rhq",
        grad_heads,
        attended_low.reshape(head_shape),
        preferred_element_type=jnp.float32,
    )
    full_shape = (row_count, total_len, HEADS, HEAD_DIM)
    table_zero = jnp.zeros((HEADS, BUCKETS), jnp.float32)
    keys_again, values_again = (keys_all, values_all)

    def key_step(state_in, block_index):
        query_acc, table_acc, key_terms, value_terms = state_in
        block_start = block_index * block_len
        key_at = block_start + jnp.arange(block_len, dtype=jnp.int32)
        key_part = key_slice(keys_again, block_start)
        value_part = key_slice(values_again, block_start)
        scores, bucket_of = block_scores(
            query_heads, key_part, query_pos, key_at, table_mat, lengths
        )
        probs = jnp.exp(scores - log_total[..., None])
        probs_low = probs.astype(jnp.bfloat16)
        value_term = jnp.einsum(
            "rhqk,rqhd->rkhd", probs_low, grad_heads, preferred_element_type=jnp.float32
        )
        prob_grad = jnp.einsum(
            "rqhd,rkhd->rhqk", grad_heads, value_part, preferred_element_type=jnp.float32
        )
        score_grad = probs * (prob_grad - row_delta[..., None])
        score_low = score_grad.astype(jnp.bfloat16)
        query_acc = query_acc + jnp.einsum(
            "rhqk,rkhd->rqhd", score_low, key_part, preferred_element_type=jnp.float32
        )
        key_term = jnp.einsum(
            "rhqk,rqhd->rkhd", score_low, query_heads, preferred_element_type=jnp.float32
        )
        table_acc = table_acc + table_term(score_grad, bucket_of)
        key_terms = lax.dynamic_update_slice_in_dim(key_terms, key_term, block_start, 1)
        value_terms = lax.dynamic_update_slice_in_dim(value_terms, value_term, block_start, 1)
        return ((query_acc, table_acc, key_terms, value_terms), None)

    start_state = (
        jnp.zeros(head_shape, jnp.float32),
        table_zero,
        jnp.zeros(full_shape, jnp.float32),
        jnp.zeros(full_shape, jnp.float32),
    )
    query_grad, table_grad, key_terms, value_terms = lax.scan(key_step, start_state, block_ids)[0]
    key_grad, value_grad = in_one_piece(
        (
            key_terms.reshape(row_count, total_len, model_width),
            value_terms.reshape(row_count, total_len, model_width),
        ),
        "seq",
        1,
        0,
    )
    query_low = query_grad.reshape(token_count, model_width).astype(jnp.bfloat16)
    key_low = key_grad.reshape(token_count, model_width).astype(jnp.bfloat16)
    value_low = value_grad.reshape(token_count, model_width).astype(jnp.bfloat16)
    query_weight_grad = jnp.einsum(
        "nd,ne->de", normed_low, query_low, preferred_element_type=jnp.float32
    )
    key_weight_grad = jnp.einsum(
        "nd,ne->de", normed_low, key_low, preferred_element_type=jnp.float32
    )
    value_weight_grad = jnp.einsum(
        "nd,ne->de", normed_low, value_low, preferred_element_type=jnp.float32
    )
    normed_grad = jnp.einsum("ne,de->nd", query_low, query_full, preferred_element_type=jnp.float32)
    normed_grad = normed_grad + jnp.einsum(
        "ne,de->nd", key_low, key_full, preferred_element_type=jnp.float32
    )
    normed_grad = normed_grad + jnp.einsum(
        "ne,de->nd", value_low, value_full, preferred_element_type=jnp.float32
    )
    input_norm_grad, first_gain_term = first_pull(normed_grad)
    input_grad = (middle_grad + input_norm_grad).reshape(tokens.shape)
    summed = sum_packed(
        (
            query_weight_grad,
            key_weight_grad,
            value_weight_grad,
            out_weight_grad,
            gate_weight_grad,
            up_weight_grad,
            down_weight_grad,
            first_gain_term,
            second_gain_term,
            table_grad.reshape(HEADS * BUCKETS),
        ),
        ("rows", "seq"),
        (0, 0, 0, 0, 0, 0, 0, 0, 0, 0),
    )
    return (
        output_low,
        input_grad,
        summed[0],
        summed[1],
        summed[2],
        summed[3],
        summed[4],
        summed[5],
        summed[6],
        summed[7],
        summed[8],
        summed[9],
    )


def solution(mesh):
    in_specs = (
        P("rows", "seq", None),
        P("rows"),
        P("rows", "seq", None),
        P(("rows", "seq"), None),
        P(("rows", "seq"), None),
        P(("rows", "seq"), None),
        P(("rows", "seq"), None),
        P(("rows", "seq"), None),
        P(("rows", "seq"), None),
        P(("rows", "seq"), None),
        P(("rows", "seq")),
        P(("rows", "seq")),
        P(("rows", "seq")),
    )
    out_specs = (
        P("rows", "seq", None),
        P("rows", "seq", None),
        P(("rows", "seq"), None),
        P(("rows", "seq"), None),
        P(("rows", "seq"), None),
        P(("rows", "seq"), None),
        P(("rows", "seq"), None),
        P(("rows", "seq"), None),
        P(("rows", "seq"), None),
        P(("rows", "seq")),
        P(("rows", "seq")),
        P(("rows", "seq")),
    )
    return jax.shard_map(
        per_device, mesh=mesh, in_specs=in_specs, out_specs=out_specs, check_vma=False
    )
```

profile of v0, /device:TPU:1, one launch (start us, length us, event | category | flops | bytes accessed | tf_op | source)
XLA Modules:
  0.0 1406.9 jit_solution(7627139228949856112)
XLA Ops:
  25.1 174.4 %all-reduce.6.cloned.1.call-done = bf16[7079808]{0:T(1024)(128)(2,1)} async-done(((bf16[7079808]{0:T(1024)(128)(2,1)}), bf16[7079808]{0:T(1024)(128)(2,1)}) %all-reduce.6.cloned.1.call-update) | async-done | bytes 14159632
  199.5 34.1 %reshape.632 = bf16[128,55311]{1,0:T(8,128)(2,1)} reshape(bf16[7079808]{0:T(1024)(128)(2,1)} %all-reduce.6.cloned.1.call-done) | data formatting | bytes 28319232 | tf_op jit(solution)/shard_map/all_gather | solution.py:26
  280.7 67.6 %all-gather.3.cloned.1.call-done = bf16[4,2048,768]{1,2,0:T(8,128)(2,1)} async-done(((bf16[4,128,768]{1,2,0:T(8,128)(2,1)}), bf16[4,2048,768]{1,2,0:T(8,128)(2,1)}) %all-gather.3.cloned.1.call-update) | async-done | bytes 12582928 | tf_op jit(solution)/shard_map/all_gather | solution.py:37
  348.2 10.8 fusion.158
  359.0 71.4 %while.41 = (s32[]{:T(128)}, f32[2,12,128]{2,1,0:T(8,128)S(1)}, f32[2,12,128]{2,1,0:T(8,128)S(1)}, s32[2]{0:T(128)S(1)}, s32[2]{0:T(128)}, /*index=5*/bf16[2,204...) while((s32[]{:T(128)}, f32[2,12,128]{2,1,0:T(8,128)S(1)}, ...), condition=%wide.region_4.5_spmd.clone, body=%wide.region_1.4_spmd.clone.sunk | while | flops 535971968 | bytes 92848120 | solution.py:196
  368.1 8.2 copy.140
  386.9 7.9 exponential_reduce_fusion.2
  403.7 8.2 copy.140
  422.5 7.9 exponential_reduce_fusion.2
  431.1 66.7 %while.42 = (s32[]{:T(128)}, f32[2,128,12,64]{1,3,2,0:T(8,128)}, s32[2]{0:T(128)S(1)}, bf16[2,2048,768]{1,2,0:T(8,128)(2,1)}, s32[2]{0:T(128)}, /*index=5*/bf16[...) while((s32[]{:T(128)}, f32[2,128,12,64]{1,3,2,0:T(8,128)}, ...), condition=%wide.region_6.7_spmd.clone, body=%wide.region_5.6_spmd.clone.sunk | while | flops 929565824 | bytes 47085540 | solution.py:217
  445.9 8.2 copy.141
  454.9 9.7 fusion.260
  478.9 8.2 copy.141
  487.9 9.8 fusion.260
  527.8 310.1 %while.43 = (s32[]{:T(128)}, f32[2,128,12,64]{1,3,2,0:T(8,128)}, f32[12,32]{1,0:T(8,128)S(1)}, f32[2,2048,12,64]{1,3,2,0:T(8,128)}, f32[2,2048,12,64]{1,3,2,0:T(...) while((s32[]{:T(128)}, f32[2,128,12,64]{1,3,2,0:T(8,128)}, ...), condition=%wide.region_12.13_spmd.clone, body=%wide.region_9.0_spmd.clone.sunk | while | flops 2384990464 | bytes 244910416 | solution.py:307
  539.7 74.4 %copy.144 = pred[128,1024,32]{1,2,0:T(32,128)(4,1)S(1)} copy(pred[128,1024,32]{0,2,1:T(32,128)(4,1)S(1)} %iota_compare_fusion.28) | data formatting | bytes 8388608 | tf_op jit(solution)/shard_map/while/body/eval_jaxpr/eq | solution.py:84
  620.1 8.2 copy.145
  634.6 16.1 %convert_reduce_fusion.3 = (bf16[12,128,1024]{1,2,0:T(8,128)(2,1)}, bf16[12,128,1024]{1,2,0:T(8,128)(2,1)}, bf16[2,12,128,1024]{2,3,1,0:T(8,128)(2,1)}) fusion(f32[2,12,128]{2,1,0:T(8,128)} %get-tuple-element.891, bf16[2,1024,12,64]{1,3,2,0:T(8,128)(2,1)} %bitcast.284, bf16[2,128,12,64]{1,3,2,0:T(8,128)(2,1)} %get-tuple-element.890, ...), kind=kOutput, calls=%fused_computation.85.clone.1 | convolution fusion | flops 440401920 | bytes 35022848 | tf_op jit(solution)/shard_map/while/body/eval_jaxpr/rqhd,rkhd->rhqk/dot_general | solution.py:285
  663.3 7.8 bitcast_dynamic-update-slice_fusion.4
  688.9 74.4 %copy.144 = pred[128,1024,32]{1,2,0:T(32,128)(4,1)S(1)} copy(pred[128,1024,32]{0,2,1:T(32,128)(4,1)S(1)} %iota_compare_fusion.28) | data formatting | bytes 8388608 | tf_op jit(solution)/shard_map/while/body/eval_jaxpr/eq | solution.py:84
  769.3 8.2 copy.145
  783.8 16.1 %convert_reduce_fusion.3 = (bf16[12,128,1024]{1,2,0:T(8,128)(2,1)}, bf16[12,128,1024]{1,2,0:T(8,128)(2,1)}, bf16[2,12,128,1024]{2,3,1,0:T(8,128)(2,1)}) fusion(f32[2,12,128]{2,1,0:T(8,128)} %get-tuple-element.891, bf16[2,1024,12,64]{1,3,2,0:T(8,128)(2,1)} %bitcast.284, bf16[2,128,12,64]{1,3,2,0:T(8,128)(2,1)} %get-tuple-element.890, ...), kind=kOutput, calls=%fused_computation.85.clone.1 | convolution fusion | flops 440401920 | bytes 35022848 | tf_op jit(solution)/shard_map/while/body/eval_jaxpr/rqhd,rkhd->rhqk/dot_general | solution.py:285
  812.6 7.9 bitcast_dynamic-update-slice_fusion.4
  837.8 12.7 copy.85
  850.5 12.6 copy.84
  863.1 17.5 %pad_maximum_fusion = f32[4,2048,768]{2,1,0:T(8,128)} fusion(f32[2,2048,768]{2,1,0:T(8,128)} %copy.85, f32[2,2048,768]{2,1,0:T(8,128)} %copy.84), kind=kLoop, calls=%fused_computation.136 | loop fusion | flops 6291456 | bytes 50331648 | tf_op jit(solution)/shard_map/concatenate | solution.py:42
  897.7 9.2 reshape_reshape.60
  911.7 8.7 reshape_reshape.61
  937.8 130.9 %reduce-scatter.2.cloned.1.call-done = f32[4,128,768]{2,1,0:T(8,128)} async-done(((f32[4,2048,768]{2,1,0:T(8,128)}), f32[4,128,768]{2,1,0:T(8,128)}) %reduce-scatter.2.cloned.1.call-update) | async-done | bytes 1572880 | tf_op jit(solution)/shard_map/reduce_scatter | solution.py:43
  1109.5 20.7 %pad.4 = f32[128,56320]{1,0:T(8,128)} pad(f32[128,55311]{1,0:T(8,128)} %dynamic-update-slice.10, f32[]{:T(128)} %constant.108.clone.1), padding=0_0x0_1009 | pad | bytes 57155076 | tf_op jit(solution)/shard_map/jit(_pad)/pad | solution.py:60
  1130.3 25.4 %reshape.620 = f32[56320,128]{1,0:T(8,128)} reshape(f32[128,56320]{1,0:T(8,128)} %pad.4) | data formatting | bytes 57671680 | tf_op jit(solution)/shard_map/reshape | solution.py:60
  1161.8 230.1 %all-reduce.8.cloned.1.call-done = f32[56320,128]{1,0:T(8,128)} async-done(((f32[56320,128]{1,0:T(8,128)}), f32[56320,128]{1,0:T(8,128)}) %all-reduce.8.cloned.1.call-update) | async-done | bytes 28835856
  (344 shorter events, 339.7 us)
Async XLA Ops:
  7.2 192.3 %all-reduce.6.cloned.1.call-start = ((), (), s32[]{:S(2)}) async-start(), calls=%async_computation.3 | async-start | bytes 28319744
  23.4 324.9 %all-gather.3.cloned.1.call-start = ((), (), s32[]{:S(2)}) async-start(), calls=%async_computation.1 | async-start | bytes 13369344 | tf_op jit(solution)/shard_map/all_gather | solution.py:37
  241.1 13.2 copy-start.8
  244.1 10.3 copy-start.17
  247.6 821.2 %reduce-scatter.2.cloned.1.call-start = ((), (), s32[]{:S(2)}) async-start(), calls=%async_computation.2 | async-start | bytes 26738688 | tf_op jit(solution)/shard_map/reduce_scatter | solution.py:43
  280.7 78.4 %copy-start.38 = (f32[2,12,128]{2,1,0:T(8,128)S(1)}, f32[2,12,128]{2,1,0:T(8,128)}, u32[]{:S(2)}) copy-start(f32[2,12,128]{2,1,0:T(8,128)} %custom-call.1) | copy-start | bytes 36868
  501.7 9.4 copy-start.22
  650.7 20.3 %slice-start.2 = ((s8[12582912]{0:T(1024)(128)(4,1)}), s8[4194304]{0:T(1024)(128)(4,1)S(1)}, s32[]{:S(2)}) async-start(s8[12582912]{0:T(1024)(128)(4,1)} %bitcast.279), calls=%async_computation.7 | async-start | bytes 8388608 | tf_op jit(solution)/shard_map/while
  655.8 15.2 %slice-start.3 = ((s8[12582912]{0:T(1024)(128)(4,1)}), s8[4194304]{0:T(1024)(128)(4,1)S(1)}, s32[]{:S(2)}) async-start(s8[12582912]{0:T(1024)(128)(4,1)} %bitcast.279), calls=%async_computation.8 | async-start | bytes 8388608 | tf_op jit(solution)/shard_map/while
  659.5 11.6 slice-start.4
  663.2 7.8 slice-start
  663.2 7.8 slice-start.1
  663.2 7.8 copy-start.5
  800.0 20.6 %slice-start.2 = ((s8[12582912]{0:T(1024)(128)(4,1)}), s8[4194304]{0:T(1024)(128)(4,1)S(1)}, s32[]{:S(2)}) async-start(s8[12582912]{0:T(1024)(128)(4,1)} %bitcast.279), calls=%async_computation.7 | async-start | bytes 8388608 | tf_op jit(solution)/shard_map/while
  805.2 15.3 %slice-start.3 = ((s8[12582912]{0:T(1024)(128)(4,1)}), s8[4194304]{0:T(1024)(128)(4,1)S(1)}, s32[]{:S(2)}) async-start(s8[12582912]{0:T(1024)(128)(4,1)} %bitcast.279), calls=%async_computation.8 | async-start | bytes 8388608 | tf_op jit(solution)/shard_map/while
  808.9 11.7 slice-start.4
  812.6 7.9 slice-start
  812.6 7.9 slice-start.1
  812.6 7.9 copy-start.5
  837.8 12.7 copy-start.48
  880.6 511.3 %all-reduce.8.cloned.1.call-start = ((), (), s32[]{:S(2)}) async-start(), calls=%async_computation.4 | async-start | bytes 57671680
  897.7 9.2 copy-start.28
  911.7 8.7 copy-start.31
  911.7 8.7 copy-start.33
  924.1 7.5 copy-start.44
  924.1 8.2 copy-start.49
  924.1 9.0 copy-start.20
  1075.0 6.2 copy-start.18
  1084.8 6.9 copy-start.21
  1084.8 8.5 slice-start.5
  1093.3 7.4 slice-start.9
  1101.6 6.3 copy-start.39
  (44 other events, 155.6 us)
Sparse Core Ops, SparseCore 0:
  23.5 175.9 all-reduce.5
  247.7 100.5 all-gather.2
  880.8 187.9 reduce-scatter.1
  1155.8 236.0 all-reduce.7
where the time goes:
time: 1420 us; the launch traced here: 1410 us
  waiting for transfers between devices  603 us (42%)
  local copies, waits for them, and re-layouts  499 us (35%)
  matrix products  209 us (15%)
  other arithmetic  64.4 us (5%)
  loops' own time  16.5 us (1%)
  between operations  14.7 us (1%)
    unnamed x6, waiting for transfers between devices  405 us
    eq x2, local copies, waits for them, and re-layouts, block_scores(): bucket_of[:, :, None] == jnp.arange(BUCKETS, dtype=jnp.int32)  149 us
    reduce_scatter x1, waiting for transfers between devices, in_one_piece(): lax.psum_scatter(both, axis, scatter_dimension=dim, tiled=True)  131 us
    all_gather x1, waiting for transfers between devices, sent_together(): whole = lax.all_gather(both, axis, axis=dim, tiled=True)  67.6 us
    dot_general x6, local copies, waits for them, and re-layouts, block_scores(): jnp.einsum('qkb,hb->hqk', onehot, table_mat, preferred_element_type=jnp.f...  49.4 us
    unnamed x113, local copies, waits for them, and re-layouts  41 us
    another operation x7, local copies, waits for them, and re-layouts, sum_packed(): lines = jnp.concatenate([b.reshape(size, -1) for b in parts], axis=1)  38.5 us
    dot_general x6, matrix products, block_scores(): jnp.einsum('qkb,hb->hqk', onehot, table_mat, preferred_element_type=jnp.f...  38.2 us
  transfers between devices with their start and end apart: 4, of which 4 were waited for; matrix products, arithmetic and copies ran while one was open for 7% of the time, Pallas kernels for 0%

commit v1 on v0

--- a/solution.py
+++ b/solution.py
@@ -1,9 +1,602 @@
 import math
+import functools
 
 import jax
 import jax.numpy as jnp
 from jax import lax
+from jax.experimental import pallas as pl
+from jax.experimental.pallas import tpu as pltpu
 from jax.sharding import PartitionSpec as P
+
+MESH = pl.DeviceIdType.MESH
+BF = jnp.bfloat16
+F32 = jnp.float32
+D = 768
+SEQ = 2048
+EPSILON = 1e-06
+NEGATIVE = -1e30
+LIMITS = (1, 2, 3, 4, 5, 6, 7, 8, 12, 16, 23, 32, 46, 64, 91)
+NSEM = 192
+BQ = 256
+STEPS = 12
+
+
+def dev(x, y, z, c):
+    return ((z % 2) * 4 + x, (y * 2 + z // 2) * 2 + c)
+
+
+def first_head(t):
+    return (3 * t) // 2
+
+
+def iota(shape, dim):
+    return lax.broadcasted_iota(jnp.int32, shape, dim)
+
+
+def dot(a, b):
+    return jnp.dot(a, b, preferred_element_type=F32)
+
+
+def dot_nt(a, b):
+    return lax.dot_general(a, b, (((1,), (1,)), ((), ())), preferred_element_type=F32)
+
+
+class Comm:
+    def __init__(self, x, y, z, c, send_sem, recv_sem):
+        self.x, self.y, self.z, self.c = x, y, z, c
+        self.ss, self.rs = send_sem, recv_sem
+        self.next = 0
+        self.pending = []
+
+    def take(self, n=1):
+        at = self.next
+        self.next += n
+        assert self.next <= NSEM
+        return at
+
+    def peer(self, axis, offset):
+        x, y, z, c = self.x, self.y, self.z, self.c
+        if axis == "x":
+            return dev((x + offset) % 4, y, z, c)
+        if axis == "y":
+            return dev(x, (y + offset) % 4, z, c)
+        if axis == "z":
+            return dev(x, y, (z + offset) % 4, c)
+        return dev(x, y, z, 1 - c)
+
+    def place(self, axis, offset):
+        at = {"x": self.x, "y": self.y, "z": self.z}[axis]
+        return (at + offset) % 4
+
+    def copy(self, src, dst, i, to, j=None):
+        return pltpu.make_async_remote_copy(
+            src_ref=src,
+            dst_ref=dst,
+            send_sem=self.ss.at[i],
+            recv_sem=self.rs.at[i if j is None else j],
+            device_id=to,
+            device_id_type=MESH,
+        )
+
+    def send(self, src, dst, i, to):
+        cp = self.copy(src, dst, i, to)
+        cp.start()
+        self.pending.append(cp)
+
+    def recv(self, dst, i):
+        self.copy(dst, dst, i, self.peer("c", 0)).wait_recv()
+
+    def send_or_keep(self, src, dst, i, to, j, own):
+        cp = self.copy(src, dst, i, to, j)
+        keep = pltpu.make_async_copy(src, dst, self.rs.at[j])
+
+        @pl.when(own)
+        def _():
+            keep.start()
+
+        @pl.when(jnp.logical_not(own))
+        def _():
+            cp.start()
+
+        self.pending.append((cp, own))
+
+    def drain(self):
+        for cp in self.pending:
+            if isinstance(cp, tuple):
+                cp, own = cp
+
+                @pl.when(jnp.logical_not(own))
+                def _():
+                    cp.wait_send()
+            else:
+                cp.wait_send()
+        self.pending = []
+
+
+class Direct:
+    def __init__(self, comm, axis, views):
+        self.comm, self.axis, self.views = comm, axis, views
+        self.count = len(views(comm.place(axis, 0)))
+        self.base = comm.take(3 * self.count)
+
+    def start(self):
+        for k, off in enumerate((1, 3, 2)):
+            for n, ref in enumerate(self.views(self.comm.place(self.axis, 0))):
+                self.comm.send(ref, ref, self.base + k * self.count + n, self.comm.peer(self.axis, off))
+
+    def wait(self):
+        for k, off in enumerate((1, 3, 2)):
+            for n, ref in enumerate(self.views(self.comm.place(self.axis, -off + 4))):
+                self.comm.recv(ref, self.base + k * self.count + n)
+
+
+class Ring:
+    def __init__(self, comm, axis, views, halves):
+        self.comm, self.axis, self.views, self.halves = comm, axis, views, halves
+        self.count = len(views(comm.place(axis, 0)))
+        self.base = comm.take(4 * self.count)
+
+    def start(self, source=None):
+        own = self.views(self.comm.place(self.axis, 0))
+        for n, ref in enumerate(own):
+            src = ref if source is None else source[n]
+            for k, off in enumerate((1, 3)):
+                self.comm.send(src, ref, self.base + k * self.count + n, self.comm.peer(self.axis, off))
+
+    def forward(self):
+        for k, off in enumerate((1, 3)):
+            came = self.comm.place(self.axis, -off + 4)
+            for n, ref in enumerate(self.views(came)):
+                self.comm.recv(ref, self.base + k * self.count + n)
+            for n, ref in enumerate(self.halves(came, k)):
+                self.comm.send(ref, ref, self.base + (2 + k) * self.count + n, self.comm.peer(self.axis, off))
+
+    def wait(self):
+        far = self.comm.place(self.axis, 2)
+        for k in range(2):
+            for n, ref in enumerate(self.halves(far, k)):
+                self.comm.recv(ref, self.base + (2 + k) * self.count + n)
+
+
+def bucket_ids(offsets):
+    distance = jnp.abs(offsets)
+    bucket_sum = jnp.where(offsets > 0, 16, 0)
+    for threshold in LIMITS:
+        bucket_sum = bucket_sum + jnp.where(distance >= threshold, 1, 0)
+    return bucket_sum
+
+
+def rms_scale(values):
+    return lax.rsqrt(jnp.mean(values * values, axis=-1, keepdims=True) + EPSILON)
+
+
+def greet(comm):
+    x, y, z, c = comm.x, comm.y, comm.z, comm.c
+    zl, zh = z % 2, z // 2
+    barrier = pltpu.get_barrier_semaphore()
+    count = 0
+    peers = []
+    for dy in range(4):
+        for dh in range(2):
+            for dc in range(2):
+                if dy or dh or dc:
+                    peers.append(dev(x, (y + dy) % 4, ((zh + dh) % 2) * 2 + zl, (c + dc) % 2))
+    for off in (1, 2, 3):
+        peers.append(comm.peer("x", off))
+    for off in (1, 3):
+        peers.append(comm.peer("z", off))
+    for peer in peers:
+        pl.semaphore_signal(barrier, inc=1, device_id=peer, device_id_type=MESH)
+        count += 1
+    return barrier, count
+
+
+def cast_up(v):
+    return v.astype(F32)
+
+
+def head_bias(tables, o):
+    return tables[o : o + 1, 0:1], tables[o : o + 1, 1023:1024]
+
+
+def mega(stop, *refs):
+    names = [n for n, _ in INPUTS] + [n for n, _ in outputs_of(stop)] + [n for n, _ in SCRATCH]
+    r = dict(zip(names, refs))
+    rows, seq = lax.axis_index("rows"), lax.axis_index("seq")
+    x, y, zl, zh, c = rows % 4, seq // 4, rows // 4, (seq // 2) % 2, seq % 2
+    z = zh * 2 + zl
+    flat = rows * 16 + seq
+    t = c * 4 + y
+    comm = Comm(x, y, z, c, r["send_sem"], r["recv_sem"])
+    barrier, count = greet(comm)
+
+    lanes = iota((1, 1024), 1)
+    first_row = jnp.zeros((1, 1024), F32)
+    second_row = jnp.zeros((1, 1024), F32)
+    for i in range(6):
+        first_row += jnp.where(lanes == 6 * flat + i, r["g1"][i], 0.0)
+        second_row += jnp.where(lanes == 6 * flat + i, r["g2"][i], 0.0)
+    for i in range(3):
+        at = 768 + 3 * flat + i
+        first_row += jnp.where(lanes == at, r["bt"][i], 0.0)
+        second_row += jnp.where((lanes >= 768) & (lanes == at - 256), r["bt"][i], 0.0)
+    first_row = cast_up(first_row.astype(BF))
+    second_row = cast_up(second_row.astype(BF))
+    wst, w0 = r["wst"], r["w0"]
+    for cc in range(2):
+        for yy in range(4):
+            d, h0 = cc * 4 + yy, first_head(cc * 4 + yy)
+            for i, name in enumerate(("wq", "wk", "wv")):
+                wst[d, 0:6, 128 * i : 128 * (i + 1)] = r[name][:, 64 * h0 : 64 * h0 + 128]
+            for i, name in enumerate(("wg", "wu")):
+                for k in range(2):
+                    tile = 2 * (2 * yy + k) + cc
+                    at = 384 + 256 * i + 128 * k
+                    wst[d, 0:6, at : at + 128] = r[name][:, 128 * tile : 128 * tile + 128]
+            if yy < 3:
+                at = (cc * 3 + yy) * 128
+                wst[d, 0:6, 896:1024] = r["wo"][:, at : at + 128]
+            else:
+                wst[d, 0:6, 896:1024] = jnp.zeros((6, 128), F32)
+            wst[d, 6:7, :] = first_row
+            wst[d, 7:8, :] = second_row
+    r["wdst"][...] = r["wd"][...].astype(BF)
+
+    pl.semaphore_wait(barrier, count)
+
+    W1, WD, WQ, G5 = r["W1"], r["WD"], r["WQ"], r["G5"]
+    T5, TK, CT, tok, cot = r["T5"], r["TK"], r["CT"], r["tok"], r["cot"]
+    slot = (y % 2) * 4 + zh * 2 + c
+    base0 = comm.take(8)
+    baser = comm.take(8)
+    for cc in range(2):
+        for yy in range(4):
+            to = dev(x, yy, (y // 2) * 2 + zl, cc)
+            own = (y == yy) & (c == cc) & (zh == y // 2)
+            cp = comm.copy(wst.at[cc * 4 + yy], w0.at[slot], base0 + cc * 4 + yy, to, baser + slot)
+            keep = pltpu.make_async_copy(wst.at[cc * 4 + yy], w0.at[slot], comm.rs.at[baser + slot])
+            pl.when(own)(keep.start)
+            pl.when(jnp.logical_not(own))(cp.start)
+            comm.pending.append((cp, own))
+    wd_to = (zh * 2 + c, y % 2, y // 2)
+    own_wd = (wd_to[0] == y) & (wd_to[1] == zh) & (wd_to[2] == c)
+    wdi = comm.take()
+    wd_region = WD.at[zl, x, wd_to[1], pl.ds(16 * wd_to[0], 16)]
+    comm.send_or_keep(
+        r["wdst"], wd_region, wdi, dev(x, wd_to[0], wd_to[1] * 2 + zl, wd_to[2]), wdi, own_wd
+    )
+
+    other = comm.peer("z", 2)
+    zi = comm.take()
+    comm.send(tok.at[1 - zh], T5.at[y, zh, c], zi, other)
+    own_tokens = Ring(
+        comm,
+        "y",
+        lambda yy: [T5.at[yy, zh, c]],
+        lambda yy, k: [T5.at[yy, zh, c, pl.ds(64 * k, 64)]],
+    )
+    own_tokens.start(source=[tok.at[zh]])
+    local = comm.take(3)
+    keep_tokens = pltpu.make_async_copy(tok.at[zh], T5.at[y, zh, c], comm.ss.at[local])
+    keep_tokens.start()
+    keep_tk = pltpu.make_async_copy(tok, TK.at[:, c], comm.ss.at[local + 1])
+    keep_tk.start()
+    keep_ct = pltpu.make_async_copy(cot, CT.at[:, c], comm.ss.at[local + 2])
+    keep_ct.start()
+    pair = comm.take(2)
+
+    for j in range(8):
+        comm.recv(w0.at[j], baser + j)
+    asm = r["asm"]
+    gsum = jnp.zeros((2, 1024), F32)
+    for j in range(8):
+        asm[6 * j : 6 * j + 6, :] = w0[j, 0:6, :]
+        gsum += w0[j, 6:8, :]
+    WQ[zl, x, zh] = asm[:, 0:384].astype(BF)
+    G5[zl, x, zh] = jnp.concatenate([gsum, jnp.zeros((6, 1024), F32)], axis=0)
+    W1[zl, x, zh, :, pl.ds(pl.multiple_of(640 * y, 128), 640)] = asm[:, 384:1024].astype(BF)
+    qkv_a1 = Direct(comm, "x", lambda xx: [WQ.at[zl, xx, zh, :, pl.ds(0, 256)], G5.at[zl, xx, zh]])
+    qkv_b1 = Direct(comm, "z", lambda zz: [WQ.at[zz % 2, x, zz // 2, :, pl.ds(256, 128)]])
+    qkv_a1.start()
+    qkv_b1.start()
+    comm.recv(WD.at[zl, x, zh, pl.ds(16 * y, 16)], wdi)
+    ff_y = Direct(
+        comm,
+        "y",
+        lambda yy: [
+            W1.at[zl, x, zh, :, pl.ds(pl.multiple_of(640 * yy, 128), 640)],
+            WD.at[zl, x, zh, pl.ds(16 * yy, 16)],
+        ],
+    )
+    ff_y.start()
+
+    comm.recv(T5.at[y, 1 - zh, c], zi)
+    far_tokens = Ring(
+        comm,
+        "y",
+        lambda yy: [T5.at[yy, 1 - zh, c]],
+        lambda yy, k: [T5.at[yy, 1 - zh, c, pl.ds(64 * k, 64)]],
+    )
+    far_tokens.start()
+    keep_tokens.wait()
+    sib = comm.peer("c", 0)
+    across = comm.take(4)
+
+    def cross(k):
+        yy = (y + (0, 1, 3, 2)[k]) % 4
+        comm.send(T5.at[yy, :, c], T5.at[yy, :, c], across + k, sib)
+
+    def crossed(k):
+        yy = (y + (0, 1, 3, 2)[k]) % 4
+        comm.recv(T5.at[yy, :, 1 - c], across + k)
+
+    cross(0)
+    own_tokens.forward()
+    qkv_a1.wait()
+    qkv_b1.wait()
+    qkv_a2 = Direct(
+        comm,
+        "z",
+        lambda zz: [WQ.at[zz % 2, :, zz // 2, :, pl.ds(0, 256)], G5.at[zz % 2, :, zz // 2]],
+    )
+    qkv_b2 = Direct(comm, "x", lambda xx: [WQ.at[:, xx, :, :, pl.ds(256, 128)]])
+    qkv_a2.start()
+    qkv_b2.start()
+    far_tokens.forward()
+    cross(1)
+    cross(2)
+    ff_y.wait()
+    ff_a1 = Direct(
+        comm,
+        "x",
+        lambda xx: [WO_A(W1.at[zl, xx, zh]), WD.at[zl, xx, zh, :, pl.ds(0, 384)]],
+    )
+    ff_b1 = Direct(
+        comm,
+        "z",
+        lambda zz: [
+            W1.at[zz % 2, x, zz // 2, :, pl.ds(1280, 1280)],
+            WD.at[zz % 2, x, zz // 2, :, pl.ds(384, 384)],
+        ],
+    )
+    ff_a1.start()
+    ff_b1.start()
+    own_tokens.wait()
+    far_tokens.wait()
+    cross(3)
+    keep_tk.wait()
+    keep_ct.wait()
+    comm.send(TK.at[:, c], TK.at[:, c], pair, sib)
+    comm.send(CT.at[:, c], CT.at[:, c], pair + 1, sib)
+
+    qkv_a2.wait()
+    qkv_b2.wait()
+    total = jnp.zeros((8, 1024), F32)
+    for a in range(2):
+        for b in range(4):
+            for e in range(2):
+                total += G5[a, b, e]
+    r["GS"][...] = total
+    h0 = first_head(t)
+    table_row = jnp.concatenate([total[0:1, 768:1024], total[1:2, 768:896]], axis=1)
+    table_row = jnp.broadcast_to(table_row, (8, 384))
+    table_row = pltpu.roll(table_row, 384 - 32 * h0, 1)[:, 0:128]
+    lane = iota((8, 128), 1)
+    sub = iota((8, 128), 0)
+    table_two = jnp.where((lane // 32) == sub, table_row, 0.0).astype(BF)
+    r["OH"][...] = jnp.where(
+        bucket_ids(iota((128, 1024), 1) - 512) == iota((128, 1024), 0) % 32, 1.0, 0.0
+    ).astype(BF)
+    by_offset = dot(table_two, r["OH"][...])
+    r["BO"][...] = by_offset
+    for h in range(2):
+        for k in range(4):
+            rolled = pltpu.roll(
+                jnp.broadcast_to(by_offset[h : h + 1, :], (64, 1024)), 640 + 64 * k, 1, stride=1, stride_axis=0
+            )
+            r["BT"][h, 64 * k : 64 * k + 64, :] = rolled[:, 0:512]
+
+    for k in range(4):
+        crossed(k)
+    N, QA, KT, KN, VN, VT = r["N"], r["QA"], r["KT"], r["KN"], r["VN"], r["VT"]
+    row_len = r["lens"][zh]
+
+    def project(i, carry):
+        raw = cast_up(T5[i // 2, i % 2].reshape(256, D))
+        normed = (raw * rms_scale(raw) * r["GS"][0:1, 0:768]).astype(BF)
+        N[pl.ds(i * 256, 256), :] = normed
+        res = dot(normed, WQ[...].reshape(D, 384))
+        q, k_, v = res[:, 0:128], res[:, 128:256], res[:, 256:384]
+        at = pl.ds(pl.multiple_of(i * 256, 256), 256)
+        KN[at, :] = k_.astype(BF)
+        VN[at, :] = v.astype(BF)
+        VT[:, at] = v.T.astype(BF)
+        kt = k_.T
+        lane = iota((256, 128), 1)
+        sub = iota((128, 256), 0)
+        key_at = i * 256 + iota((128, 256), 1)
+        for h in range(2):
+            base = 64 * (1 - h)
+            hot = jnp.where((lane == base + i) | (lane == base + 8), 1.0, 0.0)
+            QA[h, at, :] = jnp.where(lane // 64 == h, q, hot).astype(BF)
+            left, right = head_bias(r["BO"][...], h)
+            start = 256 * (sub - base)
+            extra = jnp.where(key_at < start - 128, left, 0.0) + jnp.where(
+                key_at >= start + 384, right, 0.0
+            )
+            masked = jnp.where(key_at >= row_len, NEGATIVE, 0.0)
+            extra = jnp.where(sub - base < 8, extra, jnp.where(sub - base == 8, masked, 0.0))
+            KT[h, :, at] = jnp.where(sub // 64 == h, kt, extra).astype(BF)
+        return carry
+
+    lax.fori_loop(0, 8, project, 0)
+    r["ON"][...] = jnp.zeros((SEQ, 128), BF)
+
+    SC, PB, BT, ON, LI = r["SC"], r["PB"], r["BT"], r["ON"], r["LI"]
+
+    def unit_of(step):
+        ui = step // 4
+        u = jnp.where(ui == 0, 1, jnp.where(ui == 1, 0, 2))
+        number = 3 * t + u
+        head = number // 2 - h0
+        start = (number % 2) * 1024 + (step % 4) * 256
+        return head, pl.multiple_of(start, 256)
+
+    def attend(step, carry):
+        head, q0 = unit_of(step)
+        qa = QA[head, pl.ds(q0, BQ), :]
+        for j in range(8):
+            SC[:, 128 + 256 * j : 384 + 256 * j] = dot(qa, KT[head, :, 256 * j : 256 * j + 256])
+        SC[:, pl.ds(q0, 512)] = SC[:, pl.ds(q0, 512)] + BT[head]
+        top = SC[:, 128:256]
+        for j in range(2, 17):
+            top = jnp.maximum(top, SC[:, 128 * j : 128 * j + 128])
+        top = jnp.max(top, axis=1, keepdims=True)
+        sums = jnp.zeros((BQ, 128), F32)
+        for j in range(16):
+            p = jnp.exp(SC[:, 128 + 128 * j : 256 + 128 * j] - top)
+            sums += p
+            PB[step, :, 128 * j : 128 * j + 128] = p.astype(BF)
+        inv = 1.0 / jnp.sum(sums, axis=1, keepdims=True)
+        LI[step] = jnp.broadcast_to(inv, (BQ, 128))
+        mixed = dot(PB[step], VN[...]) * inv
+        lane = iota((BQ, 128), 1)
+        ON[pl.ds(q0, BQ), :] = jnp.where(lane // 64 == head, mixed, cast_up(ON[pl.ds(q0, BQ), :])).astype(BF)
+        return carry
+
+    A = r["A"]
+    base_o = comm.take(8)
+    base_or = comm.take(8)
+
+    def give(half, n):
+        for i in range(4):
+            yy, hh = 2 * half + i // 2, i % 2
+            src = ON.at[pl.ds(pl.multiple_of(256 * (yy * 2 + hh), 256), 256)]
+            dst = A.at[zh, :, pl.ds(pl.multiple_of(128 * y, 128), 128)]
+            own = (yy == y) & (hh == zh)
+            cp = comm.copy(src, dst, base_o + 4 * n + i, dev(x, yy, hh * 2 + zl, c), base_or + y * 2 + zh)
+            keep = pltpu.make_async_copy(src, dst, comm.rs.at[base_or + y * 2 + zh])
+            pl.when(own)(keep.start)
+            pl.when(jnp.logical_not(own))(cp.start)
+            comm.pending.append((cp, own))
+
+    single = (3 * t + 1) % 2
+    lax.fori_loop(0, 2, attend, 0)
+    ff_a1.wait()
+    ff_b1.wait()
+    ff_a2 = Ring(
+        comm,
+        "z",
+        lambda zz: [
+            W1.at[zz % 2, :, zz // 2, :, pl.ds(0, 1280)],
+            WD.at[zz % 2, :, zz // 2, :, pl.ds(0, 384)],
+        ],
+        lambda zz, k: [
+            W1.at[zz % 2, pl.ds(2 * k, 2), zz // 2, :, pl.ds(0, 1280)],
+            WD.at[zz % 2, pl.ds(2 * k, 2), zz // 2, :, pl.ds(0, 384)],
+        ],
+    )
+    ff_b2 = Ring(
+        comm,
+        "x",
+        lambda xx: [
+            W1.at[:, xx, :, :, pl.ds(1280, 1280)],
+            WD.at[:, xx, :, :, pl.ds(384, 384)],
+        ],
+        lambda xx, k: [
+            W1.at[k, xx, :, :, pl.ds(1280, 1280)],
+            WD.at[k, xx, :, :, pl.ds(384, 384)],
+        ],
+    )
+    ff_a2.start()
+    ff_b2.start()
+    lax.fori_loop(2, 4, attend, 0)
+    give(single, 0)
+    lax.fori_loop(4, 9, attend, 0)
+    ff_a2.forward()
+    ff_b2.forward()
+    lax.fori_loop(9, STEPS, attend, 0)
+    give(1 - single, 1)
+    ff_a2.wait()
+    ff_b2.wait()
+    for yy in range(4):
+        for hh in range(2):
+            comm.recv(A.at[hh, :, pl.ds(128 * yy, 128)], base_or + yy * 2 + hh)
+    comm.recv(TK.at[:, 1 - c], pair)
+    comm.recv(CT.at[:, 1 - c], pair + 1)
+    if stop == "fwd":
+        comm.drain()
+        for name, _ in outputs_of(stop):
+            r[name][...] = r[name[2:]][...]
+        return
+
+
+def WO_A(ref):
+    return ref.at[:, pl.ds(0, 1280)]
+
+
+INPUTS = [
+    ("lens", "s"), ("g1", "s"), ("g2", "s"), ("bt", "s"),
+    ("tok", "v"), ("cot", "v"), ("wq", "v"), ("wk", "v"), ("wv", "v"), ("wo", "v"),
+    ("wg", "v"), ("wu", "v"), ("wd", "v"),
+]
+SCRATCH = [
+    ("W1", ((2, 4, 2, 48, 2560), BF)),
+    ("WD", ((2, 4, 2, 64, 768), BF)),
+    ("WQ", ((2, 4, 2, 48, 384), BF)),
+    ("G5", ((2, 4, 2, 8, 1024), F32)),
+    ("T5", ((4, 2, 2, 128, 768), BF)),
+    ("TK", ((2, 2, 128, 768), BF)),
+    ("CT", ((2, 2, 128, 768), BF)),
+    ("wst", ((8, 8, 1024), F32)),
+    ("w0", ((8, 8, 1024), F32)),
+    ("asm", ((48, 1024), F32)),
+    ("wdst", ((16, 768), BF)),
+    ("GS", ((8, 1024), F32)),
+    ("OH", ((128, 1024), BF)),
+    ("BO", ((8, 1024), F32)),
+    ("BT", ((2, 256, 512), F32)),
+    ("N", ((2048, 768), BF)),
+    ("QA", ((2, 2048, 128), BF)),
+    ("KT", ((2, 128, 2048), BF)),
+    ("KN", ((2048, 128), BF)),
+    ("VN", ((2048, 128), BF)),
+    ("VT", ((128, 2048), BF)),
+    ("SC", ((256, 2304), F32)),
+    ("PB", ((12, 256, 2048), BF)),
+    ("ON", ((2048, 128), BF)),
+    ("LI", ((12, 256, 128), F32)),
+    ("A", ((2, 256, 512), BF)),
+    ("send_sem", None),
+    ("recv_sem", None),
+]
+
+
+def outputs_of(stop):
+    if stop == "fwd":
+        shapes = dict((n, s) for n, s in SCRATCH if s is not None)
+        return [("o_" + n, shapes[n]) for n in ("A", "ON", "N", "WQ", "GS", "KN")]
+    return []
+
+
+def call_mega(stop, *args):
+    spec = {"s": pl.BlockSpec(memory_space=pltpu.SMEM), "v": pl.BlockSpec(memory_space=pltpu.VMEM)}
+    outs = outputs_of(stop)
+    scratch = []
+    for _, s in SCRATCH:
+        scratch.append(pltpu.SemaphoreType.DMA((NSEM,)) if s is None else pltpu.VMEM(s[0], s[1]))
+    return pl.pallas_call(
+        functools.partial(mega, stop),
+        out_shape=[jax.ShapeDtypeStruct(s[0], s[1]) for _, s in outs],
+        in_specs=[spec[k] for _, k in INPUTS],
+        out_specs=[pl.BlockSpec(memory_space=pltpu.VMEM) for _ in outs],
+        scratch_shapes=scratch,
+        name="layer",
+        compiler_params=pltpu.CompilerParams(
+            collective_id=0, has_side_effects=True, vmem_limit_bytes=62 * 2**20
+        ),
+    )(*args)
+
 
 HEADS = 12
 HEAD_DIM = 64
@@ -64,14 +657,6 @@
         done.append(vector[at : at + part.size].reshape(part.shape))
         at += part.size
     return tuple(done)
-
-
-def bucket_ids(offsets):
-    distance = jnp.abs(offsets)
-    bucket_sum = (offsets > 0).astype(jnp.int32) * (BUCKETS // 2)
-    for threshold in LIMITS:
-        bucket_sum = bucket_sum + (distance >= threshold).astype(jnp.int32)
-    return bucket_sum
 
 
 def rms_norm(values, gain_vector):
@@ -196,26 +781,20 @@
     final_max, final_sum = lax.scan(stats_step, (start_max, start_sum), block_ids)[0]
     log_total = final_max + jnp.log(final_sum)
 
-    def mix_step(mixed_sum, block_index):
-        block_start = block_index * block_len
-        key_at = block_start + jnp.arange(block_len, dtype=jnp.int32)
-        scores = block_scores(
-            query_heads, key_slice(keys_all, block_start), query_pos, key_at, table_mat, lengths
-        )[0]
-        probs_low = jnp.exp(scores - log_total[..., None]).astype(jnp.bfloat16)
-        return (
-            mixed_sum
-            + jnp.einsum(
-                "rhqk,rkhd->rqhd",
-                probs_low,
-                key_slice(values_all, block_start),
-                preferred_element_type=jnp.float32,
-            ),
-            None,
-        )
-
-    mixed_sum = lax.scan(mix_step, jnp.zeros(head_shape, jnp.float32), block_ids)[0]
-    attended_low = mixed_sum.reshape(token_count, model_width).astype(jnp.bfloat16)
+    pieces = call_mega(
+        "fwd", lengths, first_gain, second_gain, bias_table, tokens, cotangent, query_weight,
+        key_weight, value_weight, out_weight, gate_weight, up_weight, down_weight
+    )[0]
+    core = lax.axis_index("seq") % 2
+    heads_c = jnp.zeros((2, 256, 384), jnp.bfloat16)
+    for k, at in enumerate((0, 64, 192, 256)):
+        heads_c = heads_c.at[:, :, at : at + 128].add(pieces[:, :, 128 * k : 128 * k + 128])
+    mine = lax.dynamic_slice_in_dim(heads_c, core * 128, 128, 1)
+    theirs = lax.dynamic_slice_in_dim(heads_c, (1 - core) * 128, 128, 1)
+    came = lax.ppermute(theirs, "seq", [(i, i ^ 1) for i in range(16)])
+    attended_low = jnp.concatenate(
+        [jnp.where(core == 0, mine, came), jnp.where(core == 0, came, mine)], axis=-1
+    ).reshape(token_count, model_width)
     middle = inputs + jnp.dot(attended_low, out_full, preferred_element_type=jnp.float32)
     normed_two, second_pull = jax.vjp(rms_norm, middle, gain_two.astype(jnp.float32))
     normed_two_low = normed_two.astype(jnp.bfloat16)

time: 1420 us -> 1410 us (level)
  Pallas kernels: 0 us -> 104 us
  waiting for transfers between devices: 603 us -> 552 us
  matrix products: 209 us -> 177 us
  local copies, waits for them, and re-layouts: 499 us -> 475 us
    pallas_call x0 -> x1, Pallas kernels: none -> 104 us  [call_mega(): pl.pallas_call(functools.partial(mega, stop), out_shape=[jax.ShapeDtypeSt...]
    all_gather x1, waiting for transfers between devices: 67.6 us -> 0.01 us  [sent_together(): whole = lax.all_gather(both, axis, axis=dim, tiled=True)]
    dot_general x2 -> x0, matrix products: 19.4 us -> none  [mix_step(): jnp.einsum('rhqk,rkhd->rqhd', probs_low, key_slice(values_all, block_star...]
    dot_general x6 -> x4, local copies, waits for them, and re-layouts: 49.4 us -> 32.9 us  [block_scores(): jnp.einsum('qkb,hb->hqk', onehot, table_mat, preferred_element_type=jnp.f...]
    reduce_scatter x1, waiting for transfers between devices: 131 us -> 146 us  [in_one_piece(): lax.psum_scatter(both, axis, scatter_dimension=dim, tiled=True)]
    dot_general x6 -> x4, matrix products: 38.2 us -> 25.1 us  [block_scores(): jnp.einsum('qkb,hb->hqk', onehot, table_mat, preferred_element_type=jnp.f...]
    unnamed x113 -> x118, local copies, waits for them, and re-layouts: 41 us -> 43.2 us
  transfers between devices with their start and end apart: 4 -> 5, of which waited for: 4 -> 4; matrix products, arithmetic and copies ran while one was open for 7% -> 8% of each run, Pallas kernels for 0% -> 7%
where the time goes in v1:
time: 1410 us; the launch traced here: 1400 us
  waiting for transfers between devices  552 us (39%)
  local copies, waits for them, and re-layouts  475 us (34%)
  matrix products  177 us (13%)
  Pallas kernels  104 us (7%)
  other arithmetic  65.6 us (5%)
  between operations  14.7 us (1%)
    unnamed x6, waiting for transfers between devices  405 us
    eq x2, local copies, waits for them, and re-layouts, block_scores(): bucket_of[:, :, None] == jnp.arange(BUCKETS, dtype=jnp.int32)  149 us
    reduce_scatter x1, waiting for transfers between devices, in_one_piece(): lax.psum_scatter(both, axis, scatter_dimension=dim, tiled=True)  146 us
    pallas_call x1, Pallas kernels, call_mega(): pl.pallas_call(functools.partial(mega, stop), out_shape=[jax.ShapeDtypeSt...  104 us
    unnamed x118, local copies, waits for them, and re-layouts  43.2 us
    another operation x7, local copies, waits for them, and re-layouts, sum_packed(): lines = jnp.concatenate([b.reshape(size, -1) for b in parts], axis=1)  38.4 us
    all_gather x1, local copies, waits for them, and re-layouts, gather_together(): lines, at, done = (lax.all_gather(vector, axis), 0, [])  34.1 us
    dot_general x4, local copies, waits for them, and re-layouts, block_scores(): jnp.einsum('qkb,hb->hqk', onehot, table_mat, preferred_element_type=jnp.f...  32.9 us
  transfers between devices with their start and end apart: 5, of which 4 were waited for; matrix products, arithmetic and copies ran while one was open for 8% of the time, Pallas kernels for 7%

profile of v1, /device:TPU:1, one launch (start us, length us, event | category | flops | bytes accessed | tf_op | source)
XLA Modules:
  0.0 1401.6 jit_solution(18279767842033953864)
XLA Ops:
  25.1 174.5 %all-reduce.6.cloned.1.call-done = bf16[7079808]{0:T(1024)(128)(2,1)} async-done(((bf16[7079808]{0:T(1024)(128)(2,1)}), bf16[7079808]{0:T(1024)(128)(2,1)}) %all-reduce.6.cloned.1.call-update) | async-done | bytes 14159632
  199.6 34.1 %reshape.635 = bf16[128,55311]{1,0:T(8,128)(2,1)} reshape(bf16[7079808]{0:T(1024)(128)(2,1)} %all-reduce.6.cloned.1.call-done) | data formatting | bytes 28319232 | tf_op jit(solution)/shard_map/all_gather | solution.py:619
  249.2 104.3 %layer.1 = (bf16[2,256,512]{2,1,0:T(8,128)(2,1)}, bf16[2048,128]{1,0:T(8,128)(2,1)}, bf16[2048,768]{1,0:T(8,128)(2,1)}, bf16[2,4,2,48,384]{4,3,2,1,0:T(8,128)(2,...) custom-call(s32[2]{0:T(128)} %refs_0_.1, f32[6]{0:T(128)} %refs_1_.1, f32[6]{0:T(128)} %refs_2_.1, f32[3]{0:T(128)} %refs_3_.1, ...), custom_call_target="tpu_custom_call" | custom-call | tf_op jit(solution)/shard_map/layer/pallas_call | solution.py:588
  415.3 10.6 fusion.118
  425.9 71.2 %while.34 = (s32[]{:T(128)}, f32[2,12,128]{2,1,0:T(8,128)S(1)}, f32[2,12,128]{2,1,0:T(8,128)S(1)}, s32[2]{0:T(128)S(1)}, s32[2]{0:T(128)}, /*index=5*/bf16[2,204...) while((s32[]{:T(128)}, f32[2,12,128]{2,1,0:T(8,128)S(1)}, ...), condition=%wide.region_6.7_spmd.clone, body=%wide.region_3.0_spmd.clone.sunk | while | flops 535971968 | bytes 92848120 | solution.py:781
  428.3 6.6 fusion.203
  434.9 8.2 copy.123
  453.7 7.9 exponential_reduce_fusion.2
  463.8 6.6 fusion.203
  470.4 8.2 copy.123
  489.2 7.9 exponential_reduce_fusion.2
  498.3 6.1 broadcast.752
  504.4 6.2 broadcast.752.clone
  510.6 307.4 %while.35 = (s32[]{:T(128)}, f32[2,128,12,64]{1,3,2,0:T(8,128)}, f32[12,32]{1,0:T(8,128)S(1)}, f32[2,2048,12,64]{1,3,2,0:T(8,128)}, f32[2,2048,12,64]{1,3,2,0:T(...) while((s32[]{:T(128)}, f32[2,128,12,64]{1,3,2,0:T(8,128)}, ...), condition=%wide.region_10.11_spmd.clone, body=%wide.region_7.10_spmd.clone.sunk | while | flops 2384990464 | bytes 244955504 | solution.py:886
  522.4 74.4 %copy.126 = pred[128,1024,32]{1,2,0:T(32,128)(4,1)S(1)} copy(pred[128,1024,32]{0,2,1:T(32,128)(4,1)S(1)} %iota_compare_fusion.22) | data formatting | bytes 8388608 | tf_op jit(solution)/shard_map/while/body/eval_jaxpr/eq | solution.py:669
  602.9 8.2 copy.127
  617.5 16.1 %convert_reduce_fusion.3 = (bf16[12,128,1024]{1,2,0:T(8,128)(2,1)}, bf16[12,128,1024]{1,2,0:T(8,128)(2,1)}, bf16[2,12,128,1024]{2,3,1,0:T(8,128)(2,1)}) fusion(f32[2,12,128]{2,1,0:T(8,128)} %get-tuple-element.695, bf16[2,1024,12,64]{1,3,2,0:T(8,128)(2,1)} %bitcast.228, bf16[2,128,12,64]{1,3,2,0:T(8,128)(2,1)} %get-tuple-element.694, ...), kind=kOutput, calls=%fused_computation.45.clone.1 | convolution fusion | flops 440401920 | bytes 35022848 | tf_op jit(solution)/shard_map/while/body/eval_jaxpr/rqhd,rkhd->rhqk/dot_general | solution.py:864
  646.2 7.9 bitcast_dynamic-update-slice_fusion.4
  671.1 74.4 %copy.126 = pred[128,1024,32]{1,2,0:T(32,128)(4,1)S(1)} copy(pred[128,1024,32]{0,2,1:T(32,128)(4,1)S(1)} %iota_compare_fusion.22) | data formatting | bytes 8388608 | tf_op jit(solution)/shard_map/while/body/eval_jaxpr/eq | solution.py:669
  751.5 8.2 copy.127
  766.2 16.1 %convert_reduce_fusion.3 = (bf16[12,128,1024]{1,2,0:T(8,128)(2,1)}, bf16[12,128,1024]{1,2,0:T(8,128)(2,1)}, bf16[2,12,128,1024]{2,3,1,0:T(8,128)(2,1)}) fusion(f32[2,12,128]{2,1,0:T(8,128)} %get-tuple-element.695, bf16[2,1024,12,64]{1,3,2,0:T(8,128)(2,1)} %bitcast.228, bf16[2,128,12,64]{1,3,2,0:T(8,128)(2,1)} %get-tuple-element.694, ...), kind=kOutput, calls=%fused_computation.45.clone.1 | convolution fusion | flops 440401920 | bytes 35022848 | tf_op jit(solution)/shard_map/while/body/eval_jaxpr/rqhd,rkhd->rhqk/dot_general | solution.py:864
  795.0 7.8 bitcast_dynamic-update-slice_fusion.4
  818.0 12.7 copy.80
  830.7 12.6 copy.79
  843.3 17.5 %pad_maximum_fusion = f32[4,2048,768]{2,1,0:T(8,128)} fusion(f32[2,2048,768]{2,1,0:T(8,128)} %copy.80, f32[2,2048,768]{2,1,0:T(8,128)} %copy.79), kind=kLoop, calls=%fused_computation.96 | loop fusion | flops 6291456 | bytes 50331648 | tf_op jit(solution)/shard_map/concatenate | solution.py:635
  870.6 8.4 reshape_reshape.64
  883.2 9.1 reshape_reshape.65
  897.0 8.5 reshape_reshape.66
  917.4 145.8 %reduce-scatter.2.cloned.1.call-done = f32[4,128,768]{2,1,0:T(8,128)} async-done(((f32[4,2048,768]{2,1,0:T(8,128)}), f32[4,128,768]{2,1,0:T(8,128)}) %reduce-scatter.2.cloned.1.call-update) | async-done | bytes 1572880 | tf_op jit(solution)/shard_map/reduce_scatter | solution.py:636
  1104.0 20.7 %pad.13 = f32[128,56320]{1,0:T(8,128)} pad(f32[128,55311]{1,0:T(8,128)} %dynamic-update-slice.22, f32[]{:T(128)} %constant.249.clone.1), padding=0_0x0_1009 | pad | bytes 57155076 | tf_op jit(solution)/shard_map/jit(_pad)/pad | solution.py:653
  1124.7 25.4 %reshape.623 = f32[56320,128]{1,0:T(8,128)} reshape(f32[128,56320]{1,0:T(8,128)} %pad.13) | data formatting | bytes 57671680 | tf_op jit(solution)/shard_map/reshape | solution.py:653
  1156.3 230.3 %all-reduce.8.cloned.1.call-done = f32[56320,128]{1,0:T(8,128)} async-done(((f32[56320,128]{1,0:T(8,128)}), f32[56320,128]{1,0:T(8,128)}) %all-reduce.8.cloned.1.call-update) | async-done | bytes 28835856
  (342 shorter events, 288.5 us)
Async XLA Ops:
  7.2 192.4 %all-reduce.6.cloned.1.call-start = ((), (), s32[]{:S(2)}) async-start(), calls=%async_computation.3 | async-start | bytes 28319744
  23.4 391.9 %all-gather.3.cloned.1.call-start = ((), (), s32[]{:S(2)}) async-start(), calls=%async_computation.1 | async-start | bytes 13369344 | tf_op jit(solution)/shard_map/all_gather | solution.py:630
  241.1 150.8 %copy-start.7 = (bf16[2,128,768]{2,1,0:T(8,128)(2,1)}, bf16[2,128,768]{2,1,0:T(8,128)(2,1)S(1)}, u32[]{:S(2)}) copy-start(bf16[2,128,768]{2,1,0:T(8,128)(2,1)S(1)} %fusion.98) | copy-start | bytes 1179652
  241.8 111.7 %copy-start.52 = (pred[384]{0:T(512)(128)(4,1)S(1)}, pred[384]{0:T(512)(128)(4,1)}, u32[]{:S(2)}) copy-start(pred[384]{0:T(512)(128)(4,1)} %constant.243.clone.1) | copy-start | bytes 1156
  249.1 114.7 %copy-start.26 = (bf16[128,4608]{1,0:T(8,128)(2,1)S(1)}, bf16[128,4608]{1,0:T(8,128)(2,1)}, u32[]{:S(2)}) copy-start(bf16[128,4608]{1,0:T(8,128)(2,1)} %get-tuple-element.421) | copy-start | bytes 3538948
  249.2 814.1 %reduce-scatter.2.cloned.1.call-start = ((), (), s32[]{:S(2)}) async-start(), calls=%async_computation.2 | async-start | bytes 26738688 | tf_op jit(solution)/shard_map/reduce_scatter | solution.py:636
  353.5 12.7 copy-start.40
  359.8 1.5 collective-permute-start
  401.1 10.3 copy-start.14
  415.3 10.6 copy-start.39
  633.6 20.4 %slice-start.2 = ((s8[12582912]{0:T(1024)(128)(4,1)}), s8[4194304]{0:T(1024)(128)(4,1)S(1)}, s32[]{:S(2)}) async-start(s8[12582912]{0:T(1024)(128)(4,1)} %bitcast.223), calls=%async_computation.7 | async-start | bytes 8388608 | tf_op jit(solution)/shard_map/while
  638.7 15.3 %slice-start.3 = ((s8[12582912]{0:T(1024)(128)(4,1)}), s8[4194304]{0:T(1024)(128)(4,1)S(1)}, s32[]{:S(2)}) async-start(s8[12582912]{0:T(1024)(128)(4,1)} %bitcast.223), calls=%async_computation.8 | async-start | bytes 8388608 | tf_op jit(solution)/shard_map/while
  642.4 11.7 slice-start.4
  646.1 7.9 slice-start
  646.1 7.9 slice-start.1
  646.2 7.9 copy-start.5
  646.2 7.9 copy-start.35
  782.3 20.5 %slice-start.2 = ((s8[12582912]{0:T(1024)(128)(4,1)}), s8[4194304]{0:T(1024)(128)(4,1)S(1)}, s32[]{:S(2)}) async-start(s8[12582912]{0:T(1024)(128)(4,1)} %bitcast.223), calls=%async_computation.7 | async-start | bytes 8388608 | tf_op jit(solution)/shard_map/while
  787.5 15.3 %slice-start.3 = ((s8[12582912]{0:T(1024)(128)(4,1)}), s8[4194304]{0:T(1024)(128)(4,1)S(1)}, s32[]{:S(2)}) async-start(s8[12582912]{0:T(1024)(128)(4,1)} %bitcast.223), calls=%async_computation.8 | async-start | bytes 8388608 | tf_op jit(solution)/shard_map/while
  791.2 11.6 slice-start.4
  794.9 7.9 slice-start.1
  795.0 7.9 copy-start.5
  795.0 7.9 copy-start.35
  818.0 12.7 copy-start.50
  860.8 525.8 %all-reduce.8.cloned.1.call-start = ((), (), s32[]{:S(2)}) async-start(), calls=%async_computation.4 | async-start | bytes 57671680
  870.6 8.4 copy-start.28
  883.2 9.1 copy-start.30
  883.2 9.1 copy-start.34
  897.0 8.5 copy-start.46
  897.0 9.3 copy-start.6
  897.0 9.8 copy-start.8
  1079.2 8.5 slice-start.5
  (49 other events, 196.0 us)
Sparse Core Ops, SparseCore 0:
  23.5 176.0 all-reduce.5
  249.3 132.4 all-gather.2
  860.9 202.2 reduce-scatter.1
  1150.3 236.3 all-reduce.7

commit v2 on v1

--- a/solution.py
+++ b/solution.py
@@ -1,4 +1,3 @@
-import math
 import functools
 
 import jax
@@ -16,7 +15,7 @@
 EPSILON = 1e-06
 NEGATIVE = -1e30
 LIMITS = (1, 2, 3, 4, 5, 6, 7, 8, 12, 16, 23, 32, 46, 64, 91)
-NSEM = 192
+NSEM = 400
 BQ = 256
 STEPS = 12
 
@@ -156,6 +155,25 @@
         for k in range(2):
             for n, ref in enumerate(self.halves(far, k)):
                 self.comm.recv(ref, self.base + (2 + k) * self.count + n)
+
+
+class Scatter:
+    def __init__(self, comm, axis, views, bufs):
+        self.comm, self.axis, self.views, self.bufs = comm, axis, views, bufs
+        self.base = comm.take(3 * len(bufs))
+
+    def start(self):
+        for k, off in enumerate((1, 3, 2)):
+            refs = self.views(self.comm.place(self.axis, off))
+            for n, ref in enumerate(refs):
+                self.comm.send(
+                    ref, self.bufs[n].at[k], self.base + k * len(refs) + n, self.comm.peer(self.axis, off)
+                )
+
+    def wait(self):
+        for k in range(3):
+            for n, buf in enumerate(self.bufs):
+                self.comm.recv(buf.at[k], self.base + k * len(self.bufs) + n)
 
 
 def bucket_ids(offsets):
@@ -398,13 +416,12 @@
 
     for k in range(4):
         crossed(k)
-    N, QA, KT, KN, VN, VT = r["N"], r["QA"], r["KT"], r["KN"], r["VN"], r["VT"]
+    QA, KT, KN, VN, VT = r["QA"], r["KT"], r["KN"], r["VN"], r["VT"]
     row_len = r["lens"][zh]
 
     def project(i, carry):
         raw = cast_up(T5[i // 2, i % 2].reshape(256, D))
         normed = (raw * rms_scale(raw) * r["GS"][0:1, 0:768]).astype(BF)
-        N[pl.ds(i * 256, 256), :] = normed
         res = dot(normed, WQ[...].reshape(D, 384))
         q, k_, v = res[:, 0:128], res[:, 128:256], res[:, 256:384]
         at = pl.ds(pl.multiple_of(i * 256, 256), 256)
@@ -431,6 +448,7 @@
 
     lax.fori_loop(0, 8, project, 0)
     r["ON"][...] = jnp.zeros((SEQ, 128), BF)
+    r["LI"][...] = jnp.zeros((BQ, 128), F32)
 
     SC, PB, BT, ON, LI = r["SC"], r["PB"], r["BT"], r["ON"], r["LI"]
 
@@ -458,9 +476,9 @@
             sums += p
             PB[step, :, 128 * j : 128 * j + 128] = p.astype(BF)
         inv = 1.0 / jnp.sum(sums, axis=1, keepdims=True)
-        LI[step] = jnp.broadcast_to(inv, (BQ, 128))
+        lane = iota((BQ, 128), 1)
+        LI[...] = jnp.where(lane == step, inv, LI[...])
         mixed = dot(PB[step], VN[...]) * inv
-        lane = iota((BQ, 128), 1)
         ON[pl.ds(q0, BQ), :] = jnp.where(lane // 64 == head, mixed, cast_up(ON[pl.ds(q0, BQ), :])).astype(BF)
         return carry
 
@@ -524,11 +542,483 @@
             comm.recv(A.at[hh, :, pl.ds(128 * yy, 128)], base_or + yy * 2 + hh)
     comm.recv(TK.at[:, 1 - c], pair)
     comm.recv(CT.at[:, 1 - c], pair + 1)
-    if stop == "fwd":
-        comm.drain()
-        for name, _ in outputs_of(stop):
-            r[name][...] = r[name[2:]][...]
-        return
+    comm.drain()
+
+    WOF = r["WOF"]
+    base_w = comm.take(3)
+    keeps = []
+    for yy in range(3):
+        cols = pl.ds(pl.multiple_of((c * 3 + yy) * 128, 128), 128)
+        piece = pl.ds(640 * yy + 512, 128)
+        comm.send(W1.at[1 - c, :, :, :, piece], WOF.at[:, :, :, cols], base_w + yy, sib)
+        keep = pltpu.make_async_copy(
+            W1.at[c, :, :, :, piece], WOF.at[:, :, :, cols], comm.ss.at[comm.take()]
+        )
+        keep.start()
+        keeps.append(keep)
+    lane = iota((256, 128), 1)
+    for hh in range(2):
+        p0, p1, p2, p3 = [cast_up(A[hh, :, 128 * k : 128 * k + 128]) for k in range(4)]
+        p1, p2 = pltpu.roll(p1, 64, 1), pltpu.roll(p2, 64, 1)
+        A[hh, :, 0:128] = (p0 + jnp.where(lane >= 64, p1, 0.0)).astype(BF)
+        A[hh, :, 128:256] = jnp.where(lane < 64, p1, p2).astype(BF)
+        A[hh, :, 256:384] = (p3 + jnp.where(lane < 64, p2, 0.0)).astype(BF)
+    for keep in keeps:
+        keep.wait()
+    for yy in range(3):
+        cols = pl.ds(pl.multiple_of(((1 - c) * 3 + yy) * 128, 128), 128)
+        comm.recv(WOF.at[:, :, :, cols], base_w + yy)
+
+    POS, POR, MID, N2, N2T = r["POS"], r["POR"], r["MID"], r["N2"], r["N2T"]
+    base_p = comm.take(2)
+    for hh in range(2):
+        term = dot(A[hh, :, 0:384], WOF[...].reshape(384, D))
+        POS[hh] = term.astype(BF).reshape(2, 128, D)
+        comm.send(POS.at[hh], POR.at[hh], base_p + hh, sib)
+    second_gain = r["GS"][1:2, 0:768]
+    for hh in range(2):
+        comm.recv(POR.at[hh], base_p + hh)
+        for k in range(2):
+            middle = cast_up(TK[hh, k]) + (cast_up(POS[hh, k]) + cast_up(POR[hh, k]))
+            MID[2 * hh + k] = middle
+            normed = middle * rms_scale(middle) * second_gain
+            N2[128 * k : 128 * k + 128, 768 * hh : 768 * hh + 768] = normed.astype(BF)
+            at = 256 * hh + 128 * k
+            N2T[:, at : at + 128] = normed.T.astype(BF)
+
+    HX, HIDT, GU = r["HX"], r["HIDT"], r["GU"]
+
+    def gated(k, carry):
+        at = pl.multiple_of(640 * k, 128)
+        gate_w = W1[:, :, :, :, pl.ds(at, 256)].reshape(D, 256)
+        up_w = W1[:, :, :, :, pl.ds(at + 256, 256)].reshape(D, 256)
+        down_w = WD[k // 2, pl.ds((2 * k) % 4, 2)].reshape(256, D)
+        for hh in range(2):
+            gate = dot(N2[:, 768 * hh : 768 * hh + 768], gate_w)
+            up = dot(N2[:, 768 * hh : 768 * hh + 768], up_w)
+            back = dot_nt(CT[hh].reshape(256, D), down_w)
+            square = gate * gate
+            th = jnp.tanh(0.7978845608028654 * (gate + 0.044715 * (square * gate)))
+            half = 0.5 * (1.0 + th)
+            gelu = gate * half
+            slope = half + (0.5 * gate) * (1.0 - th * th) * (
+                0.7978845608028654 * (1.0 + 3 * 0.044715 * square)
+            )
+            hidden = gelu * up
+            cols = pl.ds(pl.multiple_of(256 * k, 256), 256)
+            HX[:, pl.ds(pl.multiple_of(1024 * hh + 256 * k, 256), 256)] = hidden.astype(BF)
+            HIDT[cols, 256 * hh : 256 * hh + 256] = hidden.T.astype(BF)
+            both = pl.multiple_of(512 * k, 512)
+            GU[hh, :, :, pl.ds(both, 256)] = (back * up * slope).astype(BF).reshape(2, 128, 256)
+            GU[hh, :, :, pl.ds(both + 256, 256)] = (back * gelu).astype(BF).reshape(2, 128, 256)
+        return carry
+
+    lax.fori_loop(0, 4, gated, 0)
+    PNR, SC = r["PNR"], r["SC"]
+    base_n = comm.take(2)
+    comm.drain()
+    for hh in range(2):
+        term = dot_nt(GU[hh, :, :, 0:512].reshape(256, 512), W1[:, :, :, :, 0:512].reshape(D, 512))
+        for k in range(1, 4):
+            term += dot_nt(
+                GU[hh, :, :, 512 * k : 512 * k + 512].reshape(256, 512),
+                W1[:, :, :, :, 640 * k : 640 * k + 512].reshape(D, 512),
+            )
+        POS[hh] = term.astype(BF).reshape(2, 128, D)
+        comm.send(POS.at[hh], PNR.at[hh], base_n + hh, sib)
+    PYS, PYR = r["PYS"], r["PYR"]
+    yi = comm.take()
+    down_all = WD[...].reshape(1024, D)
+    for hh in range(2):
+        PYS[hh] = dot(HX[pl.ds(pl.multiple_of(128 * (1 - c), 128), 128), 1024 * hh : 1024 * hh + 1024], down_all).astype(BF)
+    comm.send(PYS, PYR, yi, sib)
+    for hh in range(2):
+        SC[128 * hh : 128 * hh + 128, 0:768] = dot(HX[pl.ds(pl.multiple_of(128 * c, 128), 128), 1024 * hh : 1024 * hh + 1024], down_all)
+
+    ML, DOS, DO, VEC = r["ML"], r["DOS"], r["DO"], r["VEC"]
+    VEC[...] = jnp.zeros((8, 1024), F32)
+    base_d = comm.take(8)
+    base_dr = comm.take(8)
+    m = y * 2 + zh
+    for hh in range(2):
+        comm.recv(PNR.at[hh], base_n + hh)
+        for k in range(2):
+            grad = cast_up(POS[hh, k]) + cast_up(PNR[hh, k])
+            middle = MID[2 * hh + k]
+            scale = rms_scale(middle)
+            gained = grad * second_gain
+            mean = jnp.mean(middle * gained, axis=-1, keepdims=True)
+            full = cast_up(CT[hh, k]) + scale * gained - middle * (scale * scale * scale * mean)
+            ML[hh, k] = full.astype(BF)
+
+            @pl.when(c == k)
+            def _():
+                r["din"][hh] = full
+                VEC[1:2, 0:768] += jnp.sum(grad * middle * scale, axis=0, keepdims=True)
+
+        given = dot_nt(ML[hh].reshape(256, D), WOF[...].reshape(384, D))
+        g0, g1, g2 = given[:, 0:128], given[:, 128:256], given[:, 256:384]
+        r0, r1, r2 = pltpu.roll(g0, 64, 1), pltpu.roll(g1, 64, 1), pltpu.roll(g2, 64, 1)
+        DOS[0, hh] = g0.astype(BF)
+        DOS[1, hh] = jnp.where(lane < 64, r0, r1).astype(BF)
+        DOS[2, hh] = jnp.where(lane < 64, r1, r2).astype(BF)
+        DOS[3, hh] = g2.astype(BF)
+        for yy in range(4):
+            dst = DO.at[pl.ds(pl.multiple_of(256 * m, 256), 256)]
+            own = (yy == y) & (hh == zh)
+            cp = comm.copy(DOS.at[yy, hh], dst, base_d + 4 * hh + yy, dev(x, yy, hh * 2 + zl, c), base_dr + m)
+            keep = pltpu.make_async_copy(DOS.at[yy, hh], dst, comm.rs.at[base_dr + m])
+            pl.when(own)(keep.start)
+            pl.when(jnp.logical_not(own))(cp.start)
+            comm.pending.append((cp, own))
+
+    def down_term(k, carry):
+        res = dot(HIDT[pl.ds(pl.multiple_of(256 * k, 256), 256), :], CT[...].reshape(512, D))
+        WD[k // 2, pl.ds((2 * k) % 4, 2)] = res.astype(BF).reshape(2, 2, 64, D)
+        return carry
+
+    lax.fori_loop(0, 4, down_term, 0)
+
+    def gated_term(k, carry):
+        res = dot(N2T[...], GU[:, :, :, pl.ds(pl.multiple_of(512 * k, 512), 512)].reshape(512, 512))
+        at = pl.multiple_of(640 * k, 128)
+        W1[:, :, :, :, pl.ds(at, 512)] = res.astype(BF).reshape(2, 4, 2, 48, 512)
+        return carry
+
+    lax.fori_loop(0, 4, gated_term, 0)
+    attended_t = jnp.concatenate(
+        [cast_up(A[hh, :, 0:384]).T.astype(BF) for hh in range(2)], axis=1
+    )
+    WOF[...] = dot(attended_t, ML[...].reshape(512, D)).astype(BF).reshape(4, 2, 48, D)
+    base_g = comm.take(3)
+    keeps = []
+    for yy in range(3):
+        piece = pl.ds(640 * yy + 512, 128)
+        own_cols = pl.ds(pl.multiple_of((c * 3 + yy) * 128, 128), 128)
+        sib_cols = pl.ds(pl.multiple_of(((1 - c) * 3 + yy) * 128, 128), 128)
+        comm.send(WOF.at[:, :, :, sib_cols], W1.at[c, :, :, :, piece], base_g + yy, sib)
+        keep = pltpu.make_async_copy(
+            WOF.at[:, :, :, own_cols], W1.at[c, :, :, :, piece], comm.ss.at[comm.take()]
+        )
+        keep.start()
+        keeps.append(keep)
+    for keep in keeps:
+        keep.wait()
+    for yy in range(3):
+        comm.recv(W1.at[1 - c, :, :, :, pl.ds(640 * yy + 512, 128)], base_g + yy)
+    low, high = pl.ds(0, 1280), pl.ds(1280, 1280)
+    low_d, high_d = pl.ds(0, 384), pl.ds(384, 384)
+    ff_ra = Scatter(
+        comm,
+        "z",
+        lambda zz: [W1.at[zz % 2, :, zz // 2, :, low], WD.at[zz % 2, :, zz // 2, :, low_d]],
+        [r["RA1"], r["RA2"]],
+    )
+    ff_rb = Scatter(
+        comm,
+        "x",
+        lambda xx: [W1.at[:, xx, :, :, high], WD.at[:, xx, :, :, high_d]],
+        [r["RB1"], r["RB2"]],
+    )
+    ff_ra.start()
+    ff_rb.start()
+    comm.recv(PYR, yi)
+    for hh in range(2):
+        middle = MID[pl.ds(2 * hh + c, 1)].reshape(128, D)
+        r["out"][hh] = (middle + SC[128 * hh : 128 * hh + 128, 0:768] + cast_up(PYR[hh])).astype(BF)
+
+    DS, DVT = r["HX"], r["DVT"]
+    DS[...] = jnp.zeros((BQ, 2304), BF)
+    SC[:, 0:2048] = jnp.zeros((256, SEQ), F32)
+    DVT[...] = jnp.zeros((128, SEQ), F32)
+    N2[:, 0:1024] = jnp.zeros((BQ, 1024), BF)
+    BT[...] = jnp.zeros((2, 256, 512), F32)
+    for yy in range(4):
+        for hh in range(2):
+            comm.recv(DO.at[pl.ds(256 * (yy * 2 + hh), 256)], base_dr + yy * 2 + hh)
+
+    def retreat(step, carry):
+        head, q0 = unit_of(step)
+        lane = iota((BQ, 128), 1)
+        inv = jnp.sum(jnp.where(lane == step, LI[...], 0.0), axis=1, keepdims=True)
+        given = jnp.where(lane // 64 == head, cast_up(DO[pl.ds(q0, BQ), :]) * inv, 0.0)
+        given_low = given.astype(BF)
+        delta = jnp.sum(cast_up(given_low) * cast_up(ON[pl.ds(q0, BQ), :]), axis=1, keepdims=True)
+        given_t = given.T.astype(BF)
+        query_t = cast_up(QA[head, pl.ds(q0, BQ), :]).T.astype(BF)
+        for j in range(8):
+            cols = slice(256 * j, 256 * j + 256)
+            probs = PB[step, :, cols]
+            grad = dot(given_low, VT[:, cols])
+            DS[:, 128 + 256 * j : 384 + 256 * j] = (cast_up(probs) * (grad - delta)).astype(BF)
+            DVT[:, cols] += dot(given_t, probs)
+        key_rows = pl.ds(pl.multiple_of(128 * head, 128), 128)
+        for j in range(8):
+            cols = slice(256 * j, 256 * j + 256)
+            SC[key_rows, cols] += dot(query_t, DS[:, 128 + 256 * j : 384 + 256 * j])
+        moved = dot(DS[:, 128:2176], KN[...])
+        block = pl.ds(pl.multiple_of(q0 // 2, 128), 128)
+        N2[:, block] = jnp.where(lane // 64 == head, moved, cast_up(N2[:, block])).astype(BF)
+        BT[head] += cast_up(DS[:, pl.ds(q0, 512)])
+        return carry
+
+    def add_low(refs, bufs):
+        for ref, buf in zip(refs, bufs):
+            total = cast_up(ref[...])
+            for k in range(3):
+                total += cast_up(buf[k])
+            ref[...] = total.astype(BF)
+
+    lax.fori_loop(0, 9, retreat, 0)
+    ff_ra.wait()
+    ff_rb.wait()
+
+    def add_a(i, carry):
+        add_low(
+            [W1.at[zl, i, zh, :, low], WD.at[zl, i, zh, :, low_d]],
+            [r["RA1"].at[:, i], r["RA2"].at[:, i]],
+        )
+        return carry
+
+    def add_b(i, carry):
+        add_low(
+            [W1.at[i // 2, x, i % 2, :, high], WD.at[i // 2, x, i % 2, :, high_d]],
+            [r["RB1"].at[:, i // 2, i % 2], r["RB2"].at[:, i // 2, i % 2]],
+        )
+        return carry
+
+    lax.fori_loop(0, 4, add_a, 0)
+    lax.fori_loop(0, 4, add_b, 0)
+    ff_ra2 = Scatter(
+        comm,
+        "x",
+        lambda xx: [W1.at[zl, xx, zh, :, low], WD.at[zl, xx, zh, :, low_d]],
+        [r["SA1"], r["SA2"]],
+    )
+    ff_rb2 = Scatter(
+        comm,
+        "z",
+        lambda zz: [W1.at[zz % 2, x, zz // 2, :, high], WD.at[zz % 2, x, zz // 2, :, high_d]],
+        [r["SB1"], r["SB2"]],
+    )
+    ff_ra2.start()
+    ff_rb2.start()
+    lax.fori_loop(9, STEPS, retreat, 0)
+
+    lane = iota((8, 128), 1)
+    sub = iota((8, 128), 0)
+    diagonals = []
+    flip = jnp.where(iota((256, 256), 0) + iota((256, 256), 1) == 255, 1.0, 0.0).astype(BF)
+    table_grad = jnp.zeros((1, 128), F32)
+    one = iota((1, 128), 1)
+    for h in range(2):
+        near = jnp.zeros((1, 1024), F32)
+        whole = BT[h]
+        upper = whole.astype(BF)
+        lower = (whole - cast_up(upper)).astype(BF)
+        flipped = dot(flip, upper) + dot(flip, lower)
+        for k in range(4):
+            part = jnp.concatenate([flipped[64 * k : 64 * k + 64], jnp.zeros((64, 512), F32)], axis=1)
+            part = pltpu.roll(part, 129 + 64 * k, 1, stride=1, stride_axis=0)
+            near += jnp.sum(part, axis=0, keepdims=True)
+        diagonals.append(near)
+        base = 64 * (1 - h)
+        rows_far = SC[128 * h + base : 128 * h + base + 8, 0:2048]
+        key_at = iota((8, SEQ), 1)
+        start = 256 * iota((8, SEQ), 0)
+        left = jnp.sum(jnp.where(key_at < start - 128, rows_far, 0.0), axis=(0, 1), keepdims=True)
+        right = jnp.sum(jnp.where(key_at >= start + 384, rows_far, 0.0), axis=(0, 1), keepdims=True)
+        table_grad += jnp.where(one == 32 * h + 15, left, 0.0) + jnp.where(one == 32 * h + 31, right, 0.0)
+    near = jnp.concatenate(diagonals + [jnp.zeros((6, 1024), F32)], axis=0)
+    upper = near.astype(BF)
+    lower = (near - cast_up(upper)).astype(BF)
+    sums = dot_nt(upper, r["OH"][...]) + dot_nt(lower, r["OH"][...])
+    table_grad += jnp.sum(jnp.where(lane // 32 == sub, sums, 0.0), axis=0, keepdims=True)
+    spread = jnp.concatenate([table_grad, jnp.zeros((1, 256), F32)], axis=1)
+    spread = pltpu.roll(jnp.broadcast_to(spread, (8, 384)), 32 * h0, 1)
+    VEC[0:1, 768:1024] = spread[0:1, 0:256]
+    VEC[1:2, 768:896] = spread[0:1, 256:384]
+
+    YR, DWQ = r["YR"], r["DWQ"]
+    first_gain = r["GS"][0:1, 0:768]
+    base_s = comm.take(4)
+    MID[...] = jnp.zeros((4, 128, D), F32)
+
+    def sib_at(yy):
+        return GU.at[yy // 2, :, :, pl.ds(pl.multiple_of((yy % 2) * 1024, 128), 768)]
+
+    def place_of(k):
+        return (y + jnp.where(k == 0, 2, jnp.where(k == 1, 1, jnp.where(k == 2, 3, 0)))) % 4
+
+    def spread_back(k, carry):
+        yy = place_of(k)
+
+        def half(hh, inner):
+            at = pl.ds(pl.multiple_of(512 * yy + 256 * hh, 256), 256)
+            raw = cast_up(T5[yy, hh].reshape(256, D))
+            scale = rms_scale(raw)
+            normed = (raw * scale * first_gain).astype(BF)
+            dq = N2[:, pl.ds(pl.multiple_of(256 * yy + 128 * hh, 128), 128)]
+            sub = iota((128, 256), 0)
+            dkt = jnp.where(sub < 64, SC[0:128, at], SC[128:256, at])
+            dvt = DVT[:, at]
+            dk, dv = dkt.T.astype(BF), dvt.T.astype(BF)
+            dqt = cast_up(dq).T.astype(BF)
+            grad = dot_nt(jnp.concatenate([dq, dk, dv], axis=1), WQ[...].reshape(D, 384))
+            VEC[0:1, 0:768] += jnp.sum(grad * raw * scale, axis=0, keepdims=True)
+            MID[0] += dot(dqt, normed)
+            MID[1] += dot(dkt.astype(BF), normed)
+            MID[2] += dot(dvt.astype(BF), normed)
+            T5[yy, hh] = grad.astype(BF).reshape(2, 128, D)
+            return inner
+
+        lax.fori_loop(0, 2, half, 0)
+        comm.copy(T5.at[yy, :, 1 - c], sib_at(yy), base_s + k, sib).start()
+        return carry
+
+    lax.fori_loop(0, 4, spread_back, 0)
+    for i in range(3):
+        DWQ[:, :, :, :, 128 * i : 128 * i + 128] = MID[i].T.astype(BF).reshape(2, 4, 2, 48, 128)
+    qa, qb = pl.ds(0, 256), pl.ds(256, 128)
+    q_ra = Scatter(comm, "z", lambda zz: [DWQ.at[zz % 2, :, zz // 2, :, qa]], [r["QA1"]])
+    q_rb = Scatter(comm, "x", lambda xx: [DWQ.at[:, xx, :, :, qb]], [r["QB1"]])
+    v_z = Scatter(comm, "z", lambda zz: [VEC], [r["V1"]])
+    base_y = comm.take(3)
+    for k in range(4):
+        yy = (y + (2, 1, 3, 0)[k]) % 4
+        comm.recv(sib_at(yy), base_s + k)
+        for hh in range(2):
+            T5[yy, hh, c] = (cast_up(T5[yy, hh, c]) + cast_up(sib_at(yy)[hh])).astype(BF)
+        if k < 3:
+            comm.send(T5.at[yy, :, c], YR.at[k], base_y + k, comm.peer("y", (2, 1, 3)[k]))
+        if k == 0:
+            q_ra.start()
+            q_rb.start()
+            v_z.start()
+
+    ff_ra2.wait()
+    ff_rb2.wait()
+    add_low([W1.at[zl, x, zh, :, low], WD.at[zl, x, zh, :, low_d]], [r["SA1"], r["SA2"]])
+    add_low([W1.at[zl, x, zh, :, high], WD.at[zl, x, zh, :, high_d]], [r["SB1"], r["SB2"]])
+    ff_ry = Scatter(
+        comm,
+        "y",
+        lambda yy: [
+            W1.at[zl, x, zh, :, pl.ds(pl.multiple_of(640 * yy, 128), 640)],
+            WD.at[zl, x, zh, pl.ds(16 * yy, 16)],
+        ],
+        [r["SY1"], r["SY2"]],
+    )
+    ff_ry.start()
+    q_ra.wait()
+    q_rb.wait()
+    v_z.wait()
+    for i in range(4):
+        add_low([DWQ.at[zl, i, zh, :, qa]], [r["QA1"].at[:, i]])
+        add_low([DWQ.at[i // 2, x, i % 2, :, qb]], [r["QB1"].at[:, i // 2, i % 2]])
+    VE2 = r["VE2"]
+    VE2[...] = VEC[...] + r["V1"][0] + r["V1"][1] + r["V1"][2]
+    q_ra2 = Scatter(comm, "x", lambda xx: [DWQ.at[zl, xx, zh, :, qa]], [r["QA2"]])
+    q_rb2 = Scatter(comm, "z", lambda zz: [DWQ.at[zz % 2, x, zz // 2, :, qb]], [r["QB2"]])
+    v_x = Scatter(comm, "x", lambda xx: [VE2], [r["V2"]])
+    q_ra2.start()
+    q_rb2.start()
+    v_x.start()
+
+    for k in range(3):
+        comm.recv(YR.at[k], base_y + k)
+    zri = comm.take()
+    ZS, ZR = r["ZS"], r["ZR"]
+
+    def summed(hh):
+        total = cast_up(T5[y, hh, c])
+        for k in range(3):
+            total += cast_up(YR[k, hh])
+        return total
+
+    ZS[...] = summed(1 - zh).astype(BF)
+    comm.send(ZS, ZR, zri, other)
+
+    def finish(hh, grad):
+        raw = cast_up(tok[hh])
+        scale = rms_scale(raw)
+        gained = grad * first_gain
+        mean = jnp.mean(raw * gained, axis=-1, keepdims=True)
+        r["din"][hh] = r["din"][hh] + scale * gained - raw * (scale * scale * scale * mean)
+
+    finish(zh, summed(zh))
+
+    ff_ry.wait()
+    here = pl.ds(pl.multiple_of(640 * y, 128), 640)
+    total = cast_up(W1[zl, x, zh, :, here])
+    for k in range(3):
+        total += cast_up(r["SY1"][k])
+    asm[:, 384:1024] = total
+    total = cast_up(WD[zl, x, zh, pl.ds(16 * y, 16)])
+    for k in range(3):
+        total += cast_up(r["SY2"][k])
+    r["WDG"][...] = total
+    home = (2 * c + zh, y // 2, y % 2)
+    own_home = (home[0] == y) & (home[1] == zh) & (home[2] == c)
+    dwi = comm.take()
+    comm.send_or_keep(
+        r["WDG"], r["dwd_in"], dwi, dev(x, home[0], home[1] * 2 + zl, home[2]), dwi, own_home
+    )
+    q_ra2.wait()
+    q_rb2.wait()
+    v_x.wait()
+    for cols, ref, buf in ((slice(0, 256), qa, r["QA2"]), (slice(256, 384), qb, r["QB2"])):
+        total = cast_up(DWQ[zl, x, zh, :, ref])
+        for k in range(3):
+            total += cast_up(buf[k])
+        asm[:, cols] = total
+    sums = VE2[...] + r["V2"][0] + r["V2"][1] + r["V2"][2]
+    W2R = r["W2R"]
+    base_h = comm.take(8)
+    base_hr = comm.take(8)
+    mine = c * 4 + y
+    for j in range(8):
+        wst[j, 0:6, :] = asm[6 * j : 6 * j + 6, :]
+        wst[j, 6:8, :] = sums[0:2]
+        ys, hs, cs = 2 * zh + j // 4, (j // 2) % 2, j % 2
+        own = (ys == y) & (hs == zh) & (cs == c)
+        cp = comm.copy(wst.at[j], W2R.at[mine], base_h + j, dev(x, ys, hs * 2 + zl, cs), base_hr + mine)
+        keep = pltpu.make_async_copy(wst.at[j], W2R.at[mine], comm.rs.at[base_hr + mine])
+        pl.when(own)(keep.start)
+        pl.when(jnp.logical_not(own))(cp.start)
+        comm.pending.append((cp, own))
+    comm.recv(ZR, zri)
+    finish(1 - zh, cast_up(ZR[...]))
+    for d in range(8):
+        comm.recv(W2R.at[d], base_hr + d)
+    for name in ("dwq", "dwk", "dwv"):
+        r[name][...] = jnp.zeros((6, D), F32)
+    rows_sum = jnp.zeros((2, 1024), F32)
+    for cc in range(2):
+        for yy in range(4):
+            d, first = cc * 4 + yy, 64 * first_head(cc * 4 + yy)
+            for i, name in enumerate(("dwq", "dwk", "dwv")):
+                r[name][:, first : first + 128] += W2R[d, 0:6, 128 * i : 128 * i + 128]
+            for i, name in enumerate(("dwg", "dwu")):
+                for k in range(2):
+                    tile = 2 * (2 * yy + k) + cc
+                    at = 384 + 256 * i + 128 * k
+                    r[name][:, 128 * tile : 128 * tile + 128] = W2R[d, 0:6, at : at + 128]
+            if yy < 3:
+                at = (cc * 3 + yy) * 128
+                r["dwo"][:, at : at + 128] = W2R[d, 0:6, 896:1024]
+            rows_sum += W2R[d, 6:8, :]
+    r["dvec"][0:2, :] = rows_sum
+    r["dvec"][2:8, :] = jnp.zeros((6, 1024), F32)
+    comm.recv(r["dwd_in"], dwi)
+    r["dwd"][...] = r["dwd_in"][...]
+    for k in range(4):
+        yy = (y + (2, 1, 3, 0)[k]) % 4
+        comm.copy(T5.at[yy, :, 1 - c], sib_at(yy), base_s + k, sib).wait_send()
+    comm.drain()
+    if stop != "all":
+        for n in DEBUG:
+            r["o_" + n][...] = r[n][...]
 
 
 def WO_A(ref):
@@ -556,7 +1046,6 @@
     ("OH", ((128, 1024), BF)),
     ("BO", ((8, 1024), F32)),
     ("BT", ((2, 256, 512), F32)),
-    ("N", ((2048, 768), BF)),
     ("QA", ((2, 2048, 128), BF)),
     ("KT", ((2, 128, 2048), BF)),
     ("KN", ((2048, 128), BF)),
@@ -565,18 +1054,74 @@
     ("SC", ((256, 2304), F32)),
     ("PB", ((12, 256, 2048), BF)),
     ("ON", ((2048, 128), BF)),
-    ("LI", ((12, 256, 128), F32)),
+    ("LI", ((256, 128), F32)),
     ("A", ((2, 256, 512), BF)),
+    ("WOF", ((4, 2, 48, 768), BF)),
+    ("POS", ((2, 2, 128, 768), BF)),
+    ("POR", ((2, 2, 128, 768), BF)),
+    ("MID", ((4, 128, 768), F32)),
+    ("N2", ((256, 1536), BF)),
+    ("N2T", ((768, 512), BF)),
+    ("HIDT", ((1024, 512), BF)),
+    ("GU", ((2, 2, 128, 2048), BF)),
+    ("PNR", ((2, 2, 128, 768), BF)),
+    ("PYS", ((2, 128, 768), BF)),
+    ("PYR", ((2, 128, 768), BF)),
+    ("ML", ((2, 2, 128, 768), BF)),
+    ("DOS", ((4, 2, 256, 128), BF)),
+    ("DO", ((2048, 128), BF)),
+    ("RA1", ((3, 4, 48, 1280), BF)),
+    ("RA2", ((3, 4, 64, 384), BF)),
+    ("RB1", ((3, 2, 2, 48, 1280), BF)),
+    ("RB2", ((3, 2, 2, 64, 384), BF)),
+    ("SA1", ((3, 48, 1280), BF)),
+    ("SA2", ((3, 64, 384), BF)),
+    ("SB1", ((3, 48, 1280), BF)),
+    ("SB2", ((3, 64, 384), BF)),
+    ("SY1", ((3, 48, 640), BF)),
+    ("SY2", ((3, 16, 768), BF)),
+    ("HX", ((256, 2304), BF)),
+    ("DVT", ((128, 2048), F32)),
+    ("YR", ((3, 2, 128, 768), BF)),
+    ("ZS", ((128, 768), BF)),
+    ("ZR", ((128, 768), BF)),
+    ("DWQ", ((2, 4, 2, 48, 384), BF)),
+    ("QA1", ((3, 4, 48, 256), BF)),
+    ("QA2", ((3, 48, 256), BF)),
+    ("QB1", ((3, 2, 2, 48, 128), BF)),
+    ("QB2", ((3, 48, 128), BF)),
+    ("VEC", ((8, 1024), F32)),
+    ("V1", ((3, 8, 1024), F32)),
+    ("V2", ((3, 8, 1024), F32)),
+    ("VE2", ((8, 1024), F32)),
+    ("W2R", ((8, 8, 1024), F32)),
+    ("WDG", ((16, 768), F32)),
+    ("dwd_in", ((16, 768), F32)),
     ("send_sem", None),
     ("recv_sem", None),
 ]
 
 
+OUTPUTS = [
+    ("out", ((2, 128, 768), BF)),
+    ("din", ((2, 128, 768), F32)),
+    ("dwq", ((6, 768), F32)),
+    ("dwk", ((6, 768), F32)),
+    ("dwv", ((6, 768), F32)),
+    ("dwo", ((6, 768), F32)),
+    ("dwg", ((6, 2048), F32)),
+    ("dwu", ((6, 2048), F32)),
+    ("dwd", ((16, 768), F32)),
+    ("dvec", ((8, 1024), F32)),
+]
+DEBUG = []
+
+
 def outputs_of(stop):
-    if stop == "fwd":
-        shapes = dict((n, s) for n, s in SCRATCH if s is not None)
-        return [("o_" + n, shapes[n]) for n in ("A", "ON", "N", "WQ", "GS", "KN")]
-    return []
+    if stop == "all":
+        return OUTPUTS
+    shapes = dict((n, s) for n, s in SCRATCH if s is not None)
+    return OUTPUTS + [("o_" + n, shapes[n]) for n in DEBUG]
 
 
 def call_mega(stop, *args):
@@ -598,92 +1143,6 @@
     )(*args)
 
 
-HEADS = 12
-HEAD_DIM = 64
-BUCKETS = 32
-
-
-EPSILON = 1e-06
-NEGATIVE = -1e30
-LIMITS = (1, 2, 3, 4, 5, 6, 7, 8, 12, 16, 23, 32, 46, 64, 91)
-
-
-def laid_out(parts, dim):
-    lengths = list(parts.shape[1:])
-    lengths[dim] *= parts.shape[0]
-    return jnp.moveaxis(parts, 0, dim).reshape(lengths)
-
-
-def gather_together(arrays, axis, dims):
-    vector = jnp.concatenate([a.reshape(-1) for a in arrays])
-    lines, at, done = (lax.all_gather(vector, axis), 0, [])
-    for a, dim in zip(arrays, dims):
-        parts = lines[:, at : at + a.size].reshape(-1, *a.shape)
-        done.append(laid_out(parts, dim))
-        at += a.size
-    return tuple(done)
-
-
-def sent_together(arrays, axis, dim, along):
-    widths = [a.shape[along] for a in arrays]
-    both = jnp.concatenate(arrays, axis=along)
-    whole = lax.all_gather(both, axis, axis=dim, tiled=True)
-    return tuple(jnp.split(whole, [sum(widths[:k]) for k in range(1, len(widths))], axis=along))
-
-
-def in_one_piece(arrays, axis, dim, along):
-    both = jnp.concatenate(arrays, axis=along)
-    whole, at, done = (lax.psum_scatter(both, axis, scatter_dimension=dim, tiled=True), 0, [])
-    for a in arrays:
-        done.append(lax.slice_in_dim(whole, at, at + a.shape[along], axis=along))
-        at += a.shape[along]
-    return tuple(done)
-
-
-def cut_along(shard, dim, size):
-    before, after = (shard.shape[:dim], shard.shape[dim + 1 :])
-    return jnp.moveaxis(shard.reshape(*before, size, -1, *after), dim, 0)
-
-
-def sum_packed(arrays, axis, dims):
-    size = lax.axis_size(axis)
-    parts = [cut_along(a, dim, size) for a, dim in zip(arrays, dims)]
-    lines = jnp.concatenate([b.reshape(size, -1) for b in parts], axis=1)
-    span = max(16, -(-lines.shape[1] // 1024) * 8)
-    lines = jnp.pad(lines, ((0, 0), (0, span * 128 - lines.shape[1]))).reshape(-1, 128)
-    vector, at, done = (lax.psum_scatter(lines, axis, tiled=True).reshape(-1), 0, [])
-    for b in parts:
-        part = b[0]
-        done.append(vector[at : at + part.size].reshape(part.shape))
-        at += part.size
-    return tuple(done)
-
-
-def rms_norm(values, gain_vector):
-    mean_square = jnp.mean(values * values, axis=-1, keepdims=True)
-    return values * lax.rsqrt(mean_square + EPSILON) * gain_vector
-
-
-def block_scores(query_part, key_part, query_at, key_at, table_mat, lengths):
-    bucket_of = bucket_ids(key_at[None, :] - query_at[:, None])
-    onehot = (bucket_of[:, :, None] == jnp.arange(BUCKETS, dtype=jnp.int32)).astype(jnp.bfloat16)
-    bias_block = jnp.einsum("qkb,hb->hqk", onehot, table_mat, preferred_element_type=jnp.float32)
-    scores = (
-        jnp.einsum("rqhd,rkhd->rhqk", query_part, key_part, preferred_element_type=jnp.float32)
-        + bias_block[None]
-    )
-    key_valid = key_at[None, :] < lengths[:, None]
-    return (jnp.where(key_valid[:, None, None, :], scores, NEGATIVE), bucket_of)
-
-
-def table_term(score_grad, bucket_of):
-    selector = (bucket_of[:, :, None] == jnp.arange(BUCKETS, dtype=jnp.int32)).astype(jnp.bfloat16)
-    upper = score_grad.astype(jnp.bfloat16)
-    lower = (score_grad - upper.astype(jnp.float32)).astype(jnp.bfloat16)
-    total = jnp.einsum("rhqk,qkb->hb", upper, selector, preferred_element_type=jnp.float32)
-    return total + jnp.einsum("rhqk,qkb->hb", lower, selector, preferred_element_type=jnp.float32)
-
-
 def per_device(
     tokens,
     lengths,
@@ -699,283 +1158,41 @@
     second_gain,
     bias_table,
 ):
-    gathered = gather_together(
-        (
-            query_weight.astype(jnp.bfloat16),
-            key_weight.astype(jnp.bfloat16),
-            value_weight.astype(jnp.bfloat16),
-            out_weight.astype(jnp.bfloat16),
-            gate_weight.astype(jnp.bfloat16),
-            up_weight.astype(jnp.bfloat16),
-            down_weight.astype(jnp.bfloat16),
-            first_gain.astype(jnp.bfloat16),
-            second_gain.astype(jnp.bfloat16),
-            bias_table.astype(jnp.bfloat16),
-        ),
-        ("rows", "seq"),
-        (0, 0, 0, 0, 0, 0, 0, 0, 0, 0),
-    )
-    (
-        query_full,
-        key_full,
-        value_full,
-        out_full,
-        gate_full,
-        up_full,
-        down_full,
-        gain_one,
-        gain_two,
-        table_full,
-    ) = gathered
-    table_mat = table_full.reshape(HEADS, BUCKETS)
-    row_count, local_len, model_width = tokens.shape
-    total_len = local_len * lax.axis_size("seq")
-    token_count = row_count * local_len
-    head_shape = (row_count, local_len, HEADS, HEAD_DIM)
-    block_len = math.gcd(total_len, 1024)
-    block_count = total_len // block_len
-    block_ids = jnp.arange(block_count, dtype=jnp.int32)
-    inputs = tokens.reshape(token_count, model_width).astype(jnp.float32)
-    normed, first_pull = jax.vjp(rms_norm, inputs, gain_one.astype(jnp.float32))
-    normed_low = normed.astype(jnp.bfloat16)
-    queries = jnp.dot(normed_low, query_full, preferred_element_type=jnp.float32).astype(
-        jnp.bfloat16
-    )
-    keys_rows = jnp.dot(normed_low, key_full, preferred_element_type=jnp.float32).astype(
-        jnp.bfloat16
-    )
-    values_rows = jnp.dot(normed_low, value_full, preferred_element_type=jnp.float32).astype(
-        jnp.bfloat16
-    )
-    query_heads = queries.reshape(head_shape)
-    keys_all, values_all = sent_together(
-        (
-            keys_rows.reshape(row_count, local_len, model_width),
-            values_rows.reshape(row_count, local_len, model_width),
-        ),
-        "seq",
-        1,
-        0,
-    )
-    query_pos = lax.axis_index("seq") * local_len + jnp.arange(local_len, dtype=jnp.int32)
-
-    def key_slice(source, block_start):
-        part_rows = lax.dynamic_slice_in_dim(source, block_start, block_len, 1)
-        return part_rows.reshape(row_count, block_len, HEADS, HEAD_DIM)
-
-    def stats_step(state_in, block_index):
-        running_max, running_sum = state_in
-        block_start = block_index * block_len
-        key_at = block_start + jnp.arange(block_len, dtype=jnp.int32)
-        scores = block_scores(
-            query_heads, key_slice(keys_all, block_start), query_pos, key_at, table_mat, lengths
-        )[0]
-        new_max = jnp.maximum(running_max, jnp.max(scores, axis=-1))
-        new_sum = running_sum * jnp.exp(running_max - new_max) + jnp.sum(
-            jnp.exp(scores - new_max[..., None]), axis=-1
-        )
-        return ((new_max, new_sum), None)
-
-    start_max = jnp.full((row_count, HEADS, local_len), NEGATIVE, jnp.float32)
-    start_sum = jnp.zeros((row_count, HEADS, local_len), jnp.float32)
-    final_max, final_sum = lax.scan(stats_step, (start_max, start_sum), block_ids)[0]
-    log_total = final_max + jnp.log(final_sum)
-
-    pieces = call_mega(
-        "fwd", lengths, first_gain, second_gain, bias_table, tokens, cotangent, query_weight,
-        key_weight, value_weight, out_weight, gate_weight, up_weight, down_weight
-    )[0]
-    core = lax.axis_index("seq") % 2
-    heads_c = jnp.zeros((2, 256, 384), jnp.bfloat16)
-    for k, at in enumerate((0, 64, 192, 256)):
-        heads_c = heads_c.at[:, :, at : at + 128].add(pieces[:, :, 128 * k : 128 * k + 128])
-    mine = lax.dynamic_slice_in_dim(heads_c, core * 128, 128, 1)
-    theirs = lax.dynamic_slice_in_dim(heads_c, (1 - core) * 128, 128, 1)
-    came = lax.ppermute(theirs, "seq", [(i, i ^ 1) for i in range(16)])
-    attended_low = jnp.concatenate(
-        [jnp.where(core == 0, mine, came), jnp.where(core == 0, came, mine)], axis=-1
-    ).reshape(token_count, model_width)
-    middle = inputs + jnp.dot(attended_low, out_full, preferred_element_type=jnp.float32)
-    normed_two, second_pull = jax.vjp(rms_norm, middle, gain_two.astype(jnp.float32))
-    normed_two_low = normed_two.astype(jnp.bfloat16)
-    gate_act = jnp.dot(normed_two_low, gate_full, preferred_element_type=jnp.float32)
-    up_act = jnp.dot(normed_two_low, up_full, preferred_element_type=jnp.float32)
-    product, gated_pull = jax.vjp(
-        lambda gate_in, up_in: jax.nn.gelu(gate_in, approximate=True) * up_in, gate_act, up_act
-    )
-    hidden = product.astype(jnp.bfloat16)
-    output = middle + jnp.dot(hidden, down_full, preferred_element_type=jnp.float32)
-    output_low = output.astype(jnp.bfloat16).reshape(tokens.shape)
-    upstream_low = cotangent.reshape(token_count, model_width)
-    upstream = upstream_low.astype(jnp.float32)
-    down_weight_grad = jnp.einsum(
-        "nf,nd->fd", hidden, upstream_low, preferred_element_type=jnp.float32
-    )
-    hidden_grad = jnp.einsum(
-        "nd,fd->nf", upstream_low, down_full, preferred_element_type=jnp.float32
-    )
-    gate_grad, up_grad = gated_pull(hidden_grad)
-    gate_grad_low = gate_grad.astype(jnp.bfloat16)
-    up_grad_low = up_grad.astype(jnp.bfloat16)
-    gate_weight_grad = jnp.einsum(
-        "nd,nf->df", normed_two_low, gate_grad_low, preferred_element_type=jnp.float32
-    )
-    up_weight_grad = jnp.einsum(
-        "nd,nf->df", normed_two_low, up_grad_low, preferred_element_type=jnp.float32
-    )
-    normed_two_grad = jnp.einsum(
-        "nf,df->nd", gate_grad_low, gate_full, preferred_element_type=jnp.float32
-    ) + jnp.einsum("nf,df->nd", up_grad_low, up_full, preferred_element_type=jnp.float32)
-    middle_norm_grad, second_gain_term = second_pull(normed_two_grad)
-    middle_grad = upstream + middle_norm_grad
-    middle_low = middle_grad.astype(jnp.bfloat16)
-    out_weight_grad = jnp.einsum(
-        "nd,ne->de", attended_low, middle_low, preferred_element_type=jnp.float32
-    )
-    grad_heads = (
-        jnp.einsum("ne,de->nd", middle_low, out_full, preferred_element_type=jnp.float32)
-        .astype(jnp.bfloat16)
-        .reshape(head_shape)
-    )
-    row_delta = jnp.einsum(
-        "rqhd,rqhd->rhq",
-        grad_heads,
-        attended_low.reshape(head_shape),
-        preferred_element_type=jnp.float32,
-    )
-    full_shape = (row_count, total_len, HEADS, HEAD_DIM)
-    table_zero = jnp.zeros((HEADS, BUCKETS), jnp.float32)
-    keys_again, values_again = (keys_all, values_all)
-
-    def key_step(state_in, block_index):
-        query_acc, table_acc, key_terms, value_terms = state_in
-        block_start = block_index * block_len
-        key_at = block_start + jnp.arange(block_len, dtype=jnp.int32)
-        key_part = key_slice(keys_again, block_start)
-        value_part = key_slice(values_again, block_start)
-        scores, bucket_of = block_scores(
-            query_heads, key_part, query_pos, key_at, table_mat, lengths
-        )
-        probs = jnp.exp(scores - log_total[..., None])
-        probs_low = probs.astype(jnp.bfloat16)
-        value_term = jnp.einsum(
-            "rhqk,rqhd->rkhd", probs_low, grad_heads, preferred_element_type=jnp.float32
-        )
-        prob_grad = jnp.einsum(
-            "rqhd,rkhd->rhqk", grad_heads, value_part, preferred_element_type=jnp.float32
-        )
-        score_grad = probs * (prob_grad - row_delta[..., None])
-        score_low = score_grad.astype(jnp.bfloat16)
-        query_acc = query_acc + jnp.einsum(
-            "rhqk,rkhd->rqhd", score_low, key_part, preferred_element_type=jnp.float32
-        )
-        key_term = jnp.einsum(
-            "rhqk,rqhd->rkhd", score_low, query_heads, preferred_element_type=jnp.float32
-        )
-        table_acc = table_acc + table_term(score_grad, bucket_of)
-        key_terms = lax.dynamic_update_slice_in_dim(key_terms, key_term, block_start, 1)
-        value_terms = lax.dynamic_update_slice_in_dim(value_terms, value_term, block_start, 1)
-        return ((query_acc, table_acc, key_terms, value_terms), None)
-
-    start_state = (
-        jnp.zeros(head_shape, jnp.float32),
-        table_zero,
-        jnp.zeros(full_shape, jnp.float32),
-        jnp.zeros(full_shape, jnp.float32),
-    )
-    query_grad, table_grad, key_terms, value_terms = lax.scan(key_step, start_state, block_ids)[0]
-    key_grad, value_grad = in_one_piece(
-        (
-            key_terms.reshape(row_count, total_len, model_width),
-            value_terms.reshape(row_count, total_len, model_width),
-        ),
-        "seq",
-        1,
-        0,
-    )
-    query_low = query_grad.reshape(token_count, model_width).astype(jnp.bfloat16)
-    key_low = key_grad.reshape(token_count, model_width).astype(jnp.bfloat16)
-    value_low = value_grad.reshape(token_count, model_width).astype(jnp.bfloat16)
-    query_weight_grad = jnp.einsum(
-        "nd,ne->de", normed_low, query_low, preferred_element_type=jnp.float32
-    )
-    key_weight_grad = jnp.einsum(
-        "nd,ne->de", normed_low, key_low, preferred_element_type=jnp.float32
-    )
-    value_weight_grad = jnp.einsum(
-        "nd,ne->de", normed_low, value_low, preferred_element_type=jnp.float32
-    )
-    normed_grad = jnp.einsum("ne,de->nd", query_low, query_full, preferred_element_type=jnp.float32)
-    normed_grad = normed_grad + jnp.einsum(
-        "ne,de->nd", key_low, key_full, preferred_element_type=jnp.float32
-    )
-    normed_grad = normed_grad + jnp.einsum(
-        "ne,de->nd", value_low, value_full, preferred_element_type=jnp.float32
-    )
-    input_norm_grad, first_gain_term = first_pull(normed_grad)
-    input_grad = (middle_grad + input_norm_grad).reshape(tokens.shape)
-    summed = sum_packed(
-        (
-            query_weight_grad,
-            key_weight_grad,
-            value_weight_grad,
-            out_weight_grad,
-            gate_weight_grad,
-            up_weight_grad,
-            down_weight_grad,
-            first_gain_term,
-            second_gain_term,
-            table_grad.reshape(HEADS * BUCKETS),
-        ),
-        ("rows", "seq"),
-        (0, 0, 0, 0, 0, 0, 0, 0, 0, 0),
-    )
+    done = call_mega(
+        "all",
+        lengths,
+        first_gain,
+        second_gain,
+        bias_table,
+        tokens,
+        cotangent,
+        query_weight,
+        key_weight,
+        value_weight,
+        out_weight,
+        gate_weight,
+        up_weight,
+        down_weight,
+    )
+    flat = lax.axis_index("rows") * 16 + lax.axis_index("seq")
+    vectors = done[9]
+    table = jnp.concatenate([vectors[0, 768:1024], vectors[1, 768:896]])
     return (
-        output_low,
-        input_grad,
-        summed[0],
-        summed[1],
-        summed[2],
-        summed[3],
-        summed[4],
-        summed[5],
-        summed[6],
-        summed[7],
-        summed[8],
-        summed[9],
+        *done[:9],
+        lax.dynamic_slice(vectors, (0, 6 * flat), (1, 6))[0],
+        lax.dynamic_slice(vectors, (1, 6 * flat), (1, 6))[0],
+        lax.dynamic_slice(table, (3 * flat,), (3,)),
     )
 
 
 def solution(mesh):
-    in_specs = (
-        P("rows", "seq", None),
-        P("rows"),
-        P("rows", "seq", None),
-        P(("rows", "seq"), None),
-        P(("rows", "seq"), None),
-        P(("rows", "seq"), None),
-        P(("rows", "seq"), None),
-        P(("rows", "seq"), None),
-        P(("rows", "seq"), None),
-        P(("rows", "seq"), None),
-        P(("rows", "seq")),
-        P(("rows", "seq")),
-        P(("rows", "seq")),
-    )
-    out_specs = (
-        P("rows", "seq", None),
-        P("rows", "seq", None),
-        P(("rows", "seq"), None),
-        P(("rows", "seq"), None),
-        P(("rows", "seq"), None),
-        P(("rows", "seq"), None),
-        P(("rows", "seq"), None),
-        P(("rows", "seq"), None),
-        P(("rows", "seq"), None),
-        P(("rows", "seq")),
-        P(("rows", "seq")),
-        P(("rows", "seq")),
-    )
+    tokens = P("rows", "seq", None)
+    matrix = P(("rows", "seq"), None)
+    vector = P(("rows", "seq"))
     return jax.shard_map(
-        per_device, mesh=mesh, in_specs=in_specs, out_specs=out_specs, check_vma=False
-    )
+        per_device,
+        mesh=mesh,
+        in_specs=(tokens, P("rows"), tokens, *([matrix] * 7), *([vector] * 3)),
+        out_specs=(tokens, tokens, *([matrix] * 7), *([vector] * 3)),
+        check_vma=False,
+    )

time: 1410 us -> 187 us (0.13)
  waiting for transfers between devices: 552 us -> 0 us
  local copies, waits for them, and re-layouts: 475 us -> 11 us
  matrix products: 177 us -> 0 us
  Pallas kernels: 104 us -> 175 us
  other arithmetic: 65.6 us -> 0.01 us
    unnamed x6 -> x0, waiting for transfers between devices: 405 us -> none
    dot_general x41 -> x0, matrix products: 177 us -> none  [the longest x2 32.3 us: key_step(): jnp.einsum('rqhd,rkhd->rhqk', grad_heads, value_part, preferred_element_t...]
    eq x2 -> x0, local copies, waits for them, and re-layouts: 149 us -> none  [block_scores(): bucket_of[:, :, None] == jnp.arange(BUCKETS, dtype=jnp.int32)]
    reduce_scatter x1 -> x0, waiting for transfers between devices: 146 us -> none  [in_one_piece(): lax.psum_scatter(both, axis, scatter_dimension=dim, tiled=True)]
    another operation x18 -> x0, local copies, waits for them, and re-layouts: 78 us -> none  [the longest x7 38.4 us: sum_packed(): lines = jnp.concatenate([b.reshape(size, -1) for b in parts], axis=1)]
    pallas_call x1, Pallas kernels: 104 us -> 175 us  [call_mega(): pl.pallas_call(functools.partial(mega, stop), out_shape=[jax.ShapeDtypeSt...]
    reshape x24 -> x0, local copies, waits for them, and re-layouts: 60.2 us -> none  [the longest x1 25.4 us: sum_packed(): jnp.pad(lines, ((0, 0), (0, span * 128 - lines.shape[1]))).reshape(-1, 128)]
    unnamed x118 -> x25, local copies, waits for them, and re-layouts: 43.2 us -> 7.65 us
  transfers between devices with their start and end apart: 5 -> 0, of which waited for: 4 -> 0; matrix products, arithmetic and copies ran while one was open for 8% -> 0% of each run, Pallas kernels for 7% -> 0%
where the time goes in v2:
time: 187 us
  Pallas kernels  175 us (94%)
  local copies, waits for them, and re-layouts  11 us (6%)
    pallas_call x1, Pallas kernels, call_mega(): pl.pallas_call(functools.partial(mega, stop), out_shape=[jax.ShapeDtypeSt...  175 us
    unnamed x25, local copies, waits for them, and re-layouts  7.65 us

profile of v2, /device:TPU:1, one launch (start us, length us, event | category | flops | bytes accessed | tf_op | source)
XLA Modules:
  0.0 186.7 jit_solution(13803944937519906817)
XLA Ops:
  0.7 175.0 %layer.1 = (bf16[2,128,768]{2,1,0:T(8,128)(2,1)}, f32[2,128,768]{2,1,0:T(8,128)}, f32[6,768]{1,0:T(8,128)}, f32[6,768]{1,0:T(8,128)}, f32[6,768]{1,0:T(8,128)}, ...) custom-call(s32[2]{0:T(128)} %refs_0_.1, f32[6]{0:T(128)} %refs_1_.1, ...), custom_call_target="tpu_custom_call" | custom-call | tf_op jit(solution)/shard_map/layer/pallas_call | solution.py:1133
  175.7 0.0 copy-start
  175.7 0.8 slice_bitcast_fusion
  176.4 1.4 dynamic-slice_bitcast_fusion
  177.8 0.7 slice.6
  178.5 0.6 dynamic_slice.11
  179.1 1.8 copy.34
  180.8 0.0 copy-done
  180.8 0.0 copy-start.7
  180.8 0.9 copy.35
  181.7 0.0 copy-done.7
  181.7 0.0 copy-start.6
  181.7 0.0 copy-start.5
  181.7 0.6 copy.36
  182.3 0.1 copy-done.6
  182.5 0.0 copy-start.2
  182.5 0.6 copy.37
  183.1 0.0 copy-done.5
  183.1 0.0 copy-start.4
  183.1 0.6 copy.38
  183.7 0.1 copy-done.4
  183.8 0.6 copy.39
  184.4 0.0 copy-done.2
  184.4 0.0 copy-start.1
  184.4 0.6 copy.40
  185.1 0.2 copy-done.1
  185.3 0.0 copy-start.3
  185.3 0.6 copy.41
  185.9 0.2 copy-done.3
  186.1 0.6 copy.42
  (1 shorter events, 0.0 us)
Async XLA Ops:
  175.7 5.2 %copy-start = (f32[2,128,768]{2,1,0:T(8,128)S(1)}, f32[2,128,768]{2,1,0:T(8,128)}, u32[]{:S(2)}) copy-start(f32[2,128,768]{2,1,0:T(8,128)} %get-tuple-element.47) | copy-start | bytes 2359300
  180.8 0.9 copy-start.7
  181.7 0.7 copy-start.6
  181.7 1.4 copy-start.5
  182.5 2.0 %copy-start.2 = (f32[6,2048]{1,0:T(8,128)S(1)}, f32[6,2048]{1,0:T(8,128)}, u32[]{:S(2)}) copy-start(f32[6,2048]{1,0:T(8,128)} %get-tuple-element.52) | copy-start | bytes 147460
  183.1 0.7 copy-start.4
  184.4 0.9 copy-start.1
  185.3 0.8 copy-start.3

commit v3 on v2

--- a/solution.py
+++ b/solution.py
@@ -1,5 +1,3 @@
-import functools
-
 import jax
 import jax.numpy as jnp
 from jax import lax
@@ -15,7 +13,7 @@
 EPSILON = 1e-06
 NEGATIVE = -1e30
 LIMITS = (1, 2, 3, 4, 5, 6, 7, 8, 12, 16, 23, 32, 46, 64, 91)
-NSEM = 400
+NSEM = 240
 BQ = 256
 STEPS = 12
 
@@ -217,8 +215,8 @@
     return tables[o : o + 1, 0:1], tables[o : o + 1, 1023:1024]
 
 
-def mega(stop, *refs):
-    names = [n for n, _ in INPUTS] + [n for n, _ in outputs_of(stop)] + [n for n, _ in SCRATCH]
+def mega(*refs):
+    names = [n for n, _ in INPUTS] + [n for n, _ in OUTPUTS] + [n for n, _ in SCRATCH]
     r = dict(zip(names, refs))
     rows, seq = lax.axis_index("rows"), lax.axis_index("seq")
     x, y, zl, zh, c = rows % 4, seq // 4, rows // 4, (seq // 2) % 2, seq % 2
@@ -226,6 +224,18 @@
     flat = rows * 16 + seq
     t = c * 4 + y
     comm = Comm(x, y, z, c, r["send_sem"], r["recv_sem"])
+    local_sem = r["local_sem"]
+    TK, CT, T5, tok, cot = r["TK"], r["CT"], r["T5"], r["tok"], r["cot"]
+    loads = []
+    for i, name in enumerate(("wq", "wk", "wv", "wo", "wg", "wu", "wd")):
+        loads.append(pltpu.make_async_copy(r["h_" + name], r[name], local_sem.at[i]))
+        loads[-1].start()
+    keep_tokens = pltpu.make_async_copy(tok.at[zh], T5.at[y, zh, c], local_sem.at[7])
+    keep_tk = pltpu.make_async_copy(tok, TK.at[:, c], local_sem.at[8])
+    keep_ct = pltpu.make_async_copy(cot, CT.at[:, c], local_sem.at[9])
+    keep_tokens.start()
+    keep_tk.start()
+    keep_ct.start()
     barrier, count = greet(comm)
 
     lanes = iota((1, 1024), 1)
@@ -241,6 +251,8 @@
     first_row = cast_up(first_row.astype(BF))
     second_row = cast_up(second_row.astype(BF))
     wst, w0 = r["wst"], r["w0"]
+    for load in loads:
+        load.wait()
     for cc in range(2):
         for yy in range(4):
             d, h0 = cc * 4 + yy, first_head(cc * 4 + yy)
@@ -249,13 +261,13 @@
             for i, name in enumerate(("wg", "wu")):
                 for k in range(2):
                     tile = 2 * (2 * yy + k) + cc
-                    at = 384 + 256 * i + 128 * k
+                    at = 512 + 256 * i + 128 * k
                     wst[d, 0:6, at : at + 128] = r[name][:, 128 * tile : 128 * tile + 128]
             if yy < 3:
                 at = (cc * 3 + yy) * 128
-                wst[d, 0:6, 896:1024] = r["wo"][:, at : at + 128]
+                wst[d, 0:6, 384:512] = r["wo"][:, at : at + 128]
             else:
-                wst[d, 0:6, 896:1024] = jnp.zeros((6, 128), F32)
+                wst[d, 0:6, 384:512] = jnp.zeros((6, 128), F32)
             wst[d, 6:7, :] = first_row
             wst[d, 7:8, :] = second_row
     r["wdst"][...] = r["wd"][...].astype(BF)
@@ -263,7 +275,16 @@
     pl.semaphore_wait(barrier, count)
 
     W1, WD, WQ, G5 = r["W1"], r["WD"], r["WQ"], r["G5"]
-    T5, TK, CT, tok, cot = r["T5"], r["TK"], r["CT"], r["tok"], r["cot"]
+    other = comm.peer("z", 2)
+    zi = comm.take()
+    comm.send(tok.at[1 - zh], T5.at[y, zh, c], zi, other)
+    own_tokens = Ring(
+        comm,
+        "y",
+        lambda yy: [T5.at[yy, zh, c]],
+        lambda yy, k: [T5.at[yy, zh, c, pl.ds(64 * k, 64)]],
+    )
+    own_tokens.start(source=[tok.at[zh]])
     slot = (y % 2) * 4 + zh * 2 + c
     base0 = comm.take(8)
     baser = comm.take(8)
@@ -279,28 +300,11 @@
     wd_to = (zh * 2 + c, y % 2, y // 2)
     own_wd = (wd_to[0] == y) & (wd_to[1] == zh) & (wd_to[2] == c)
     wdi = comm.take()
-    wd_region = WD.at[zl, x, wd_to[1], pl.ds(16 * wd_to[0], 16)]
+    wd_region = WD.at[zl, x, wd_to[1], wd_to[0]]
     comm.send_or_keep(
         r["wdst"], wd_region, wdi, dev(x, wd_to[0], wd_to[1] * 2 + zl, wd_to[2]), wdi, own_wd
     )
 
-    other = comm.peer("z", 2)
-    zi = comm.take()
-    comm.send(tok.at[1 - zh], T5.at[y, zh, c], zi, other)
-    own_tokens = Ring(
-        comm,
-        "y",
-        lambda yy: [T5.at[yy, zh, c]],
-        lambda yy, k: [T5.at[yy, zh, c, pl.ds(64 * k, 64)]],
-    )
-    own_tokens.start(source=[tok.at[zh]])
-    local = comm.take(3)
-    keep_tokens = pltpu.make_async_copy(tok.at[zh], T5.at[y, zh, c], comm.ss.at[local])
-    keep_tokens.start()
-    keep_tk = pltpu.make_async_copy(tok, TK.at[:, c], comm.ss.at[local + 1])
-    keep_tk.start()
-    keep_ct = pltpu.make_async_copy(cot, CT.at[:, c], comm.ss.at[local + 2])
-    keep_ct.start()
     pair = comm.take(2)
 
     for j in range(8):
@@ -310,22 +314,15 @@
     for j in range(8):
         asm[6 * j : 6 * j + 6, :] = w0[j, 0:6, :]
         gsum += w0[j, 6:8, :]
-    WQ[zl, x, zh] = asm[:, 0:384].astype(BF)
+    WQ[zl, x, zh] = asm[:, 0:512].astype(BF)
     G5[zl, x, zh] = jnp.concatenate([gsum, jnp.zeros((6, 1024), F32)], axis=0)
-    W1[zl, x, zh, :, pl.ds(pl.multiple_of(640 * y, 128), 640)] = asm[:, 384:1024].astype(BF)
+    W1[zl, x, zh, y] = asm[:, 512:1024].astype(BF)
     qkv_a1 = Direct(comm, "x", lambda xx: [WQ.at[zl, xx, zh, :, pl.ds(0, 256)], G5.at[zl, xx, zh]])
-    qkv_b1 = Direct(comm, "z", lambda zz: [WQ.at[zz % 2, x, zz // 2, :, pl.ds(256, 128)]])
+    qkv_b1 = Direct(comm, "z", lambda zz: [WQ.at[zz % 2, x, zz // 2, :, pl.ds(256, 256)]])
     qkv_a1.start()
     qkv_b1.start()
-    comm.recv(WD.at[zl, x, zh, pl.ds(16 * y, 16)], wdi)
-    ff_y = Direct(
-        comm,
-        "y",
-        lambda yy: [
-            W1.at[zl, x, zh, :, pl.ds(pl.multiple_of(640 * yy, 128), 640)],
-            WD.at[zl, x, zh, pl.ds(16 * yy, 16)],
-        ],
-    )
+    comm.recv(WD.at[zl, x, zh, y], wdi)
+    ff_y = Direct(comm, "y", lambda yy: [W1.at[zl, x, zh, yy], WD.at[zl, x, zh, yy]])
     ff_y.start()
 
     comm.recv(T5.at[y, 1 - zh, c], zi)
@@ -357,31 +354,28 @@
         "z",
         lambda zz: [WQ.at[zz % 2, :, zz // 2, :, pl.ds(0, 256)], G5.at[zz % 2, :, zz // 2]],
     )
-    qkv_b2 = Direct(comm, "x", lambda xx: [WQ.at[:, xx, :, :, pl.ds(256, 128)]])
+    qkv_b2 = Direct(comm, "x", lambda xx: [WQ.at[:, xx, :, :, pl.ds(256, 256)]])
     qkv_a2.start()
     qkv_b2.start()
-    far_tokens.forward()
-    cross(1)
-    cross(2)
     ff_y.wait()
+    low, high = pl.ds(0, 256), pl.ds(256, 256)
+    low_d, high_d = pl.ds(0, 384), pl.ds(384, 384)
     ff_a1 = Direct(
-        comm,
-        "x",
-        lambda xx: [WO_A(W1.at[zl, xx, zh]), WD.at[zl, xx, zh, :, pl.ds(0, 384)]],
+        comm, "x", lambda xx: [W1.at[zl, xx, zh, :, :, low], WD.at[zl, xx, zh, :, :, low_d]]
     )
     ff_b1 = Direct(
         comm,
         "z",
         lambda zz: [
-            W1.at[zz % 2, x, zz // 2, :, pl.ds(1280, 1280)],
-            WD.at[zz % 2, x, zz // 2, :, pl.ds(384, 384)],
+            W1.at[zz % 2, x, zz // 2, :, :, high],
+            WD.at[zz % 2, x, zz // 2, :, :, high_d],
         ],
     )
     ff_a1.start()
     ff_b1.start()
-    own_tokens.wait()
-    far_tokens.wait()
-    cross(3)
+    far_tokens.forward()
+    cross(1)
+    cross(2)
     keep_tk.wait()
     keep_ct.wait()
     comm.send(TK.at[:, c], TK.at[:, c], pair, sib)
@@ -389,6 +383,19 @@
 
     qkv_a2.wait()
     qkv_b2.wait()
+    WOF = r["WOF"]
+    base_w = comm.take(8)
+    base_wr = comm.take(8)
+    for cc in range(2):
+        for yy in range(4):
+            src = WQ.at[cc, :, :, :, pl.ds(384, 128)]
+            dst = WOF.at[:, :, :, pl.ds(pl.multiple_of((c * 3 + y % 3) * 128, 128), 128)]
+            cp = comm.copy(src, dst, base_w + cc * 4 + yy, dev(x, yy, z, cc), base_wr + c * 4 + y)
+            keep = pltpu.make_async_copy(src, dst, comm.rs.at[base_wr + c * 4 + y])
+            here = (yy == y) & (cc == c)
+            pl.when(here & (y < 3))(keep.start)
+            pl.when(jnp.logical_not(here) & (y < 3))(cp.start)
+            comm.pending.append((cp, here | (y == 3)))
     total = jnp.zeros((8, 1024), F32)
     for a in range(2):
         for b in range(4):
@@ -414,19 +421,40 @@
             )
             r["BT"][h, 64 * k : 64 * k + 64, :] = rolled[:, 0:512]
 
-    for k in range(4):
-        crossed(k)
+    ff_a1.wait()
+    ff_b1.wait()
+    ff_a2 = Ring(
+        comm,
+        "z",
+        lambda zz: [
+            W1.at[zz % 2, :, zz // 2, :, :, low],
+            WD.at[zz % 2, :, zz // 2, :, :, low_d],
+        ],
+        lambda zz, k: [
+            W1.at[zz % 2, pl.ds(2 * k, 2), zz // 2, :, :, low],
+            WD.at[zz % 2, pl.ds(2 * k, 2), zz // 2, :, :, low_d],
+        ],
+    )
+    ff_b2 = Ring(
+        comm,
+        "x",
+        lambda xx: [W1.at[:, xx, :, :, :, high], WD.at[:, xx, :, :, :, high_d]],
+        lambda xx, k: [W1.at[k, xx, :, :, :, high], WD.at[k, xx, :, :, :, high_d]],
+    )
+    ff_a2.start()
+    ff_b2.start()
+
     QA, KT, KN, VN, VT = r["QA"], r["KT"], r["KN"], r["VN"], r["VT"]
     row_len = r["lens"][zh]
 
     def project(i, carry):
         raw = cast_up(T5[i // 2, i % 2].reshape(256, D))
         normed = (raw * rms_scale(raw) * r["GS"][0:1, 0:768]).astype(BF)
-        res = dot(normed, WQ[...].reshape(D, 384))
+        res = dot(normed, WQ[:, :, :, :, 0:384].reshape(D, 384))
         q, k_, v = res[:, 0:128], res[:, 128:256], res[:, 256:384]
         at = pl.ds(pl.multiple_of(i * 256, 256), 256)
         KN[at, :] = k_.astype(BF)
-        VN[at, :] = v.astype(BF)
+        VN[at, :] = jnp.concatenate([v, jnp.ones((256, 128), F32)], axis=1).astype(BF)
         VT[:, at] = v.T.astype(BF)
         kt = k_.T
         lane = iota((256, 128), 1)
@@ -446,9 +474,18 @@
             KT[h, :, at] = jnp.where(sub // 64 == h, kt, extra).astype(BF)
         return carry
 
-    lax.fori_loop(0, 8, project, 0)
+    for k in range(4):
+        if k == 3:
+            own_tokens.wait()
+            far_tokens.wait()
+            cross(3)
+        crossed(k)
+        first = 2 * ((y + (0, 1, 3, 2)[k]) % 4)
+        lax.fori_loop(first, first + 2, project, 0)
     r["ON"][...] = jnp.zeros((SEQ, 128), BF)
-    r["LI"][...] = jnp.zeros((BQ, 128), F32)
+    r["LI"][...] = jnp.zeros((1024, 128), F32)
+    r["PB"][:, :, 0:128] = jnp.zeros((3, 1024, 128), BF)
+    r["PB"][:, :, 2176:2304] = jnp.zeros((3, 1024, 128), BF)
 
     SC, PB, BT, ON, LI = r["SC"], r["PB"], r["BT"], r["ON"], r["LI"]
 
@@ -460,27 +497,59 @@
         start = (number % 2) * 1024 + (step % 4) * 256
         return head, pl.multiple_of(start, 256)
 
-    def attend(step, carry):
+    S2 = r["S2"]
+
+    def score_part(step, buf, j, top):
         head, q0 = unit_of(step)
-        qa = QA[head, pl.ds(q0, BQ), :]
+        s = dot(QA[head, pl.ds(q0, BQ), :], KT[head, :, 256 * j : 256 * j + 256])
+        buf[:, 128 + 256 * j : 384 + 256 * j] = s
+        most = jnp.maximum(s[:, 0:128], s[:, 128:256])
+        return most if top is None else jnp.maximum(top, most)
+
+    def score_end(step, buf, top):
+        head, q0 = unit_of(step)
+        buf[:, pl.ds(q0, 512)] = buf[:, pl.ds(q0, 512)] + BT[head]
+        return jnp.max(top, axis=1, keepdims=True)
+
+    def block_of(step):
+        return pl.ds(pl.multiple_of((step % 4) * 256, 256), BQ)
+
+    def prob_part(step, buf, j, top):
+        for k in (2 * j + 1, 2 * j + 2):
+            p = jnp.exp(buf[:, 128 * k : 128 * k + 128] - top)
+            PB[step // 4, block_of(step), 128 * k : 128 * k + 128] = p.astype(BF)
+
+    def mix(step):
+        head, q0 = unit_of(step)
+        mixed = dot(PB[step // 4, block_of(step), 128:2176], VN[...])
+        inv = 1.0 / mixed[:, 128:129]
+        lane = iota((BQ, 128), 1)
+        LI[block_of(step), :] = jnp.where(lane == step // 4, inv, LI[block_of(step), :])
+        mixed = mixed[:, 0:128] * inv
+        ON[pl.ds(q0, BQ), :] = jnp.where(lane // 64 == head, mixed, cast_up(ON[pl.ds(q0, BQ), :])).astype(BF)
+
+    def first_scores(step):
+        top = None
         for j in range(8):
-            SC[:, 128 + 256 * j : 384 + 256 * j] = dot(qa, KT[head, :, 256 * j : 256 * j + 256])
-        SC[:, pl.ds(q0, 512)] = SC[:, pl.ds(q0, 512)] + BT[head]
-        top = SC[:, 128:256]
-        for j in range(2, 17):
-            top = jnp.maximum(top, SC[:, 128 * j : 128 * j + 128])
-        top = jnp.max(top, axis=1, keepdims=True)
-        sums = jnp.zeros((BQ, 128), F32)
-        for j in range(16):
-            p = jnp.exp(SC[:, 128 + 128 * j : 256 + 128 * j] - top)
-            sums += p
-            PB[step, :, 128 * j : 128 * j + 128] = p.astype(BF)
-        inv = 1.0 / jnp.sum(sums, axis=1, keepdims=True)
-        lane = iota((BQ, 128), 1)
-        LI[...] = jnp.where(lane == step, inv, LI[...])
-        mixed = dot(PB[step], VN[...]) * inv
-        ON[pl.ds(q0, BQ), :] = jnp.where(lane // 64 == head, mixed, cast_up(ON[pl.ds(q0, BQ), :])).astype(BF)
-        return carry
+            top = score_part(step, SC, j, top)
+        return score_end(step, SC, top)
+
+    def attend(pair, top_a):
+        one, two = 2 * pair, 2 * pair + 1
+        top_b = None
+        for j in range(8):
+            top_b = score_part(two, S2, j, top_b)
+            prob_part(one, SC, j, top_a)
+        top_b = score_end(two, S2, top_b)
+        mix(one)
+        then = jnp.minimum(two + 1, STEPS - 1)
+        top_a = None
+        for j in range(8):
+            prob_part(two, S2, j, top_b)
+            top_a = score_part(then, SC, j, top_a)
+        top_a = score_end(then, SC, top_a)
+        mix(two)
+        return top_a
 
     A = r["A"]
     base_o = comm.take(8)
@@ -499,41 +568,12 @@
             comm.pending.append((cp, own))
 
     single = (3 * t + 1) % 2
-    lax.fori_loop(0, 2, attend, 0)
-    ff_a1.wait()
-    ff_b1.wait()
-    ff_a2 = Ring(
-        comm,
-        "z",
-        lambda zz: [
-            W1.at[zz % 2, :, zz // 2, :, pl.ds(0, 1280)],
-            WD.at[zz % 2, :, zz // 2, :, pl.ds(0, 384)],
-        ],
-        lambda zz, k: [
-            W1.at[zz % 2, pl.ds(2 * k, 2), zz // 2, :, pl.ds(0, 1280)],
-            WD.at[zz % 2, pl.ds(2 * k, 2), zz // 2, :, pl.ds(0, 384)],
-        ],
-    )
-    ff_b2 = Ring(
-        comm,
-        "x",
-        lambda xx: [
-            W1.at[:, xx, :, :, pl.ds(1280, 1280)],
-            WD.at[:, xx, :, :, pl.ds(384, 384)],
-        ],
-        lambda xx, k: [
-            W1.at[k, xx, :, :, pl.ds(1280, 1280)],
-            WD.at[k, xx, :, :, pl.ds(384, 384)],
-        ],
-    )
-    ff_a2.start()
-    ff_b2.start()
-    lax.fori_loop(2, 4, attend, 0)
+    top_now = lax.fori_loop(0, 2, attend, first_scores(0))
     give(single, 0)
-    lax.fori_loop(4, 9, attend, 0)
+    top_now = lax.fori_loop(2, 3, attend, top_now)
     ff_a2.forward()
     ff_b2.forward()
-    lax.fori_loop(9, STEPS, attend, 0)
+    lax.fori_loop(3, STEPS // 2, attend, top_now)
     give(1 - single, 1)
     ff_a2.wait()
     ff_b2.wait()
@@ -544,18 +584,6 @@
     comm.recv(CT.at[:, 1 - c], pair + 1)
     comm.drain()
 
-    WOF = r["WOF"]
-    base_w = comm.take(3)
-    keeps = []
-    for yy in range(3):
-        cols = pl.ds(pl.multiple_of((c * 3 + yy) * 128, 128), 128)
-        piece = pl.ds(640 * yy + 512, 128)
-        comm.send(W1.at[1 - c, :, :, :, piece], WOF.at[:, :, :, cols], base_w + yy, sib)
-        keep = pltpu.make_async_copy(
-            W1.at[c, :, :, :, piece], WOF.at[:, :, :, cols], comm.ss.at[comm.take()]
-        )
-        keep.start()
-        keeps.append(keep)
     lane = iota((256, 128), 1)
     for hh in range(2):
         p0, p1, p2, p3 = [cast_up(A[hh, :, 128 * k : 128 * k + 128]) for k in range(4)]
@@ -563,13 +591,11 @@
         A[hh, :, 0:128] = (p0 + jnp.where(lane >= 64, p1, 0.0)).astype(BF)
         A[hh, :, 128:256] = jnp.where(lane < 64, p1, p2).astype(BF)
         A[hh, :, 256:384] = (p3 + jnp.where(lane < 64, p2, 0.0)).astype(BF)
-    for keep in keeps:
-        keep.wait()
-    for yy in range(3):
-        cols = pl.ds(pl.multiple_of(((1 - c) * 3 + yy) * 128, 128), 128)
-        comm.recv(WOF.at[:, :, :, cols], base_w + yy)
-
-    POS, POR, MID, N2, N2T = r["POS"], r["POR"], r["MID"], r["N2"], r["N2T"]
+    for cc in range(2):
+        for yy in range(3):
+            comm.recv(WOF.at[:, :, :, pl.ds(128 * (cc * 3 + yy), 128)], base_wr + cc * 4 + yy)
+
+    POS, POR, N2, N2T = r["POS"], r["POR"], r["N2"], r["N2T"]
     base_p = comm.take(2)
     for hh in range(2):
         term = dot(A[hh, :, 0:384], WOF[...].reshape(384, D))
@@ -580,7 +606,7 @@
         comm.recv(POR.at[hh], base_p + hh)
         for k in range(2):
             middle = cast_up(TK[hh, k]) + (cast_up(POS[hh, k]) + cast_up(POR[hh, k]))
-            MID[2 * hh + k] = middle
+            S2[128 * hh : 128 * hh + 128, 768 * k : 768 * k + 768] = middle
             normed = middle * rms_scale(middle) * second_gain
             N2[128 * k : 128 * k + 128, 768 * hh : 768 * hh + 768] = normed.astype(BF)
             at = 256 * hh + 128 * k
@@ -589,9 +615,8 @@
     HX, HIDT, GU = r["HX"], r["HIDT"], r["GU"]
 
     def gated(k, carry):
-        at = pl.multiple_of(640 * k, 128)
-        gate_w = W1[:, :, :, :, pl.ds(at, 256)].reshape(D, 256)
-        up_w = W1[:, :, :, :, pl.ds(at + 256, 256)].reshape(D, 256)
+        gate_w = W1[:, :, :, k, :, 0:256].reshape(D, 256)
+        up_w = W1[:, :, :, k, :, 256:512].reshape(D, 256)
         down_w = WD[k // 2, pl.ds((2 * k) % 4, 2)].reshape(256, D)
         for hh in range(2):
             gate = dot(N2[:, 768 * hh : 768 * hh + 768], gate_w)
@@ -618,11 +643,10 @@
     base_n = comm.take(2)
     comm.drain()
     for hh in range(2):
-        term = dot_nt(GU[hh, :, :, 0:512].reshape(256, 512), W1[:, :, :, :, 0:512].reshape(D, 512))
+        term = dot_nt(GU[hh, :, :, 0:512].reshape(256, 512), W1[:, :, :, 0].reshape(D, 512))
         for k in range(1, 4):
             term += dot_nt(
-                GU[hh, :, :, 512 * k : 512 * k + 512].reshape(256, 512),
-                W1[:, :, :, :, 640 * k : 640 * k + 512].reshape(D, 512),
+                GU[hh, :, :, 512 * k : 512 * k + 512].reshape(256, 512), W1[:, :, :, k].reshape(D, 512)
             )
         POS[hh] = term.astype(BF).reshape(2, 128, D)
         comm.send(POS.at[hh], PNR.at[hh], base_n + hh, sib)
@@ -635,6 +659,18 @@
     for hh in range(2):
         SC[128 * hh : 128 * hh + 128, 0:768] = dot(HX[pl.ds(pl.multiple_of(128 * c, 128), 128), 1024 * hh : 1024 * hh + 1024], down_all)
 
+    def down_term(k, carry):
+        res = dot(HIDT[pl.ds(pl.multiple_of(256 * k, 256), 256), :], CT[...].reshape(512, D))
+        WD[k // 2, pl.ds((2 * k) % 4, 2)] = res.astype(BF).reshape(2, 2, 4, 16, D)
+        return carry
+
+    lax.fori_loop(0, 4, down_term, 0)
+    wd_ra = Scatter(
+        comm, "z", lambda zz: [WD.at[zz % 2, :, zz // 2, :, :, low_d]], [r["RA2"]]
+    )
+    wd_rb = Scatter(comm, "x", lambda xx: [WD.at[:, xx, :, :, :, high_d]], [r["RB2"]])
+    wd_rb.start()
+
     ML, DOS, DO, VEC = r["ML"], r["DOS"], r["DO"], r["VEC"]
     VEC[...] = jnp.zeros((8, 1024), F32)
     base_d = comm.take(8)
@@ -644,7 +680,7 @@
         comm.recv(PNR.at[hh], base_n + hh)
         for k in range(2):
             grad = cast_up(POS[hh, k]) + cast_up(PNR[hh, k])
-            middle = MID[2 * hh + k]
+            middle = S2[128 * hh : 128 * hh + 128, 768 * k : 768 * k + 768]
             scale = rms_scale(middle)
             gained = grad * second_gain
             mean = jnp.mean(middle * gained, axis=-1, keepdims=True)
@@ -672,94 +708,86 @@
             pl.when(jnp.logical_not(own))(cp.start)
             comm.pending.append((cp, own))
 
-    def down_term(k, carry):
-        res = dot(HIDT[pl.ds(pl.multiple_of(256 * k, 256), 256), :], CT[...].reshape(512, D))
-        WD[k // 2, pl.ds((2 * k) % 4, 2)] = res.astype(BF).reshape(2, 2, 64, D)
-        return carry
-
-    lax.fori_loop(0, 4, down_term, 0)
 
     def gated_term(k, carry):
         res = dot(N2T[...], GU[:, :, :, pl.ds(pl.multiple_of(512 * k, 512), 512)].reshape(512, 512))
-        at = pl.multiple_of(640 * k, 128)
-        W1[:, :, :, :, pl.ds(at, 512)] = res.astype(BF).reshape(2, 4, 2, 48, 512)
+        W1[:, :, :, k] = res.astype(BF).reshape(2, 4, 2, 48, 512)
         return carry
 
     lax.fori_loop(0, 4, gated_term, 0)
+    pl.semaphore_signal(r["free_sem"], inc=1, device_id=sib, device_id_type=MESH)
+    ff_ra = Scatter(comm, "z", lambda zz: [W1.at[zz % 2, :, zz // 2, :, :, low]], [r["RA1"]])
+    ff_rb = Scatter(comm, "x", lambda xx: [W1.at[:, xx, :, :, :, high]], [r["RB1"]])
+    ff_rb.start()
     attended_t = jnp.concatenate(
         [cast_up(A[hh, :, 0:384]).T.astype(BF) for hh in range(2)], axis=1
     )
     WOF[...] = dot(attended_t, ML[...].reshape(512, D)).astype(BF).reshape(4, 2, 48, D)
-    base_g = comm.take(3)
-    keeps = []
-    for yy in range(3):
-        piece = pl.ds(640 * yy + 512, 128)
-        own_cols = pl.ds(pl.multiple_of((c * 3 + yy) * 128, 128), 128)
-        sib_cols = pl.ds(pl.multiple_of(((1 - c) * 3 + yy) * 128, 128), 128)
-        comm.send(WOF.at[:, :, :, sib_cols], W1.at[c, :, :, :, piece], base_g + yy, sib)
-        keep = pltpu.make_async_copy(
-            WOF.at[:, :, :, own_cols], W1.at[c, :, :, :, piece], comm.ss.at[comm.take()]
-        )
-        keep.start()
-        keeps.append(keep)
-    for keep in keeps:
-        keep.wait()
-    for yy in range(3):
-        comm.recv(W1.at[1 - c, :, :, :, pl.ds(640 * yy + 512, 128)], base_g + yy)
-    low, high = pl.ds(0, 1280), pl.ds(1280, 1280)
-    low_d, high_d = pl.ds(0, 384), pl.ds(384, 384)
-    ff_ra = Scatter(
-        comm,
-        "z",
-        lambda zz: [W1.at[zz % 2, :, zz // 2, :, low], WD.at[zz % 2, :, zz // 2, :, low_d]],
-        [r["RA1"], r["RA2"]],
-    )
-    ff_rb = Scatter(
-        comm,
-        "x",
-        lambda xx: [W1.at[:, xx, :, :, high], WD.at[:, xx, :, :, high_d]],
-        [r["RB1"], r["RB2"]],
-    )
-    ff_ra.start()
-    ff_rb.start()
+    base_g = comm.take(6)
+    base_gr = comm.take(8)
+    WOR = r["WOR"]
+    for cc in range(2):
+        for yy in range(3):
+            src = WOF.at[:, :, :, pl.ds(128 * (cc * 3 + yy), 128)]
+            cp = comm.copy(src, WOR.at[y, c], base_g + cc * 3 + yy, dev(x, yy, z, cc), base_gr + c * 4 + y)
+            keep = pltpu.make_async_copy(src, WOR.at[y, c], comm.rs.at[base_gr + c * 4 + y])
+            here = (yy == y) & (cc == c)
+            pl.when(here)(keep.start)
+            pl.when(jnp.logical_not(here))(cp.start)
+            comm.pending.append((cp, here))
     comm.recv(PYR, yi)
     for hh in range(2):
-        middle = MID[pl.ds(2 * hh + c, 1)].reshape(128, D)
+        middle = S2[128 * hh : 128 * hh + 128, pl.ds(pl.multiple_of(768 * c, 128), 768)]
         r["out"][hh] = (middle + SC[128 * hh : 128 * hh + 128, 0:768] + cast_up(PYR[hh])).astype(BF)
-
-    DS, DVT = r["HX"], r["DVT"]
-    DS[...] = jnp.zeros((BQ, 2304), BF)
+    stores = [pltpu.make_async_copy(r["out"], r["h_out"], local_sem.at[10])]
+    stores[0].start()
+
     SC[:, 0:2048] = jnp.zeros((256, SEQ), F32)
-    DVT[...] = jnp.zeros((128, SEQ), F32)
+    S2[0:128, 0:2048] = jnp.zeros((128, SEQ), F32)
     N2[:, 0:1024] = jnp.zeros((BQ, 1024), BF)
     BT[...] = jnp.zeros((2, 256, 512), F32)
     for yy in range(4):
         for hh in range(2):
             comm.recv(DO.at[pl.ds(256 * (yy * 2 + hh), 256)], base_dr + yy * 2 + hh)
-
-    def retreat(step, carry):
-        head, q0 = unit_of(step)
-        lane = iota((BQ, 128), 1)
-        inv = jnp.sum(jnp.where(lane == step, LI[...], 0.0), axis=1, keepdims=True)
-        given = jnp.where(lane // 64 == head, cast_up(DO[pl.ds(q0, BQ), :]) * inv, 0.0)
-        given_low = given.astype(BF)
-        delta = jnp.sum(cast_up(given_low) * cast_up(ON[pl.ds(q0, BQ), :]), axis=1, keepdims=True)
+    wd_ra.start()
+    ff_ra.start()
+
+    GL, DL = r["GL"], r["DL"]
+
+    def retreat(ui, carry):
+        head, q0 = unit_of(4 * ui)
+        rows = pl.ds(pl.multiple_of(q0, 1024), 1024)
+        lane = iota((1024, 128), 1)
+        inv = jnp.sum(jnp.where(lane == ui, LI[...], 0.0), axis=1, keepdims=True)
+        given = jnp.where(lane // 64 == head, cast_up(DO[rows, :]) * inv, 0.0)
+        GL[...] = given.astype(BF)
+        delta = jnp.sum(cast_up(GL[...]) * cast_up(ON[rows, :]), axis=1, keepdims=True)
+        DL[...] = jnp.broadcast_to(delta, (1024, 128))
         given_t = given.T.astype(BF)
-        query_t = cast_up(QA[head, pl.ds(q0, BQ), :]).T.astype(BF)
         for j in range(8):
-            cols = slice(256 * j, 256 * j + 256)
-            probs = PB[step, :, cols]
-            grad = dot(given_low, VT[:, cols])
-            DS[:, 128 + 256 * j : 384 + 256 * j] = (cast_up(probs) * (grad - delta)).astype(BF)
-            DVT[:, cols] += dot(given_t, probs)
+            S2[0:128, 256 * j : 256 * j + 256] += dot(given_t, PB[ui, :, 128 + 256 * j : 384 + 256 * j])
+
+        def inner(b, more):
+            block = pl.ds(pl.multiple_of(256 * b, 256), 256)
+            low_rows = GL[block, :]
+            shift = DL[block, 0:1]
+            for j in range(8):
+                cols = slice(128 + 256 * j, 384 + 256 * j)
+                grad = dot(low_rows, VT[:, 256 * j : 256 * j + 256])
+                PB[ui, block, cols] = (cast_up(PB[ui, block, cols]) * (grad - shift)).astype(BF)
+            moved = dot(PB[ui, block, 128:2176], KN[...])
+            at = q0 + 256 * b
+            lane = iota((BQ, 128), 1)
+            spot = pl.ds(pl.multiple_of(at // 2, 128), 128)
+            N2[:, spot] = jnp.where(lane // 64 == head, moved, cast_up(N2[:, spot])).astype(BF)
+            BT[head] += cast_up(PB[ui, block, pl.ds(pl.multiple_of(at, 256), 512)])
+            return more
+
+        lax.fori_loop(0, 4, inner, 0)
+        query_t = cast_up(QA[head, rows, :]).T.astype(BF)
         key_rows = pl.ds(pl.multiple_of(128 * head, 128), 128)
         for j in range(8):
-            cols = slice(256 * j, 256 * j + 256)
-            SC[key_rows, cols] += dot(query_t, DS[:, 128 + 256 * j : 384 + 256 * j])
-        moved = dot(DS[:, 128:2176], KN[...])
-        block = pl.ds(pl.multiple_of(q0 // 2, 128), 128)
-        N2[:, block] = jnp.where(lane // 64 == head, moved, cast_up(N2[:, block])).astype(BF)
-        BT[head] += cast_up(DS[:, pl.ds(q0, 512)])
+            SC[key_rows, 256 * j : 256 * j + 256] += dot(query_t, PB[ui, :, 128 + 256 * j : 384 + 256 * j])
         return carry
 
     def add_low(refs, bufs):
@@ -769,42 +797,90 @@
                 total += cast_up(buf[k])
             ref[...] = total.astype(BF)
 
-    lax.fori_loop(0, 9, retreat, 0)
-    ff_ra.wait()
-    ff_rb.wait()
-
-    def add_a(i, carry):
-        add_low(
-            [W1.at[zl, i, zh, :, low], WD.at[zl, i, zh, :, low_d]],
-            [r["RA1"].at[:, i], r["RA2"].at[:, i]],
-        )
+    lax.fori_loop(0, 3, retreat, 0)
+
+    YR, DWQ = r["YR"], r["DWQ"]
+    first_gain = r["GS"][0:1, 0:768]
+    base_s = comm.take(4)
+    S2[128:256, :] = jnp.zeros((128, 2304), F32)
+
+    def sib_at(yy):
+        return GU.at[yy // 2, :, :, pl.ds(pl.multiple_of((yy % 2) * 1024, 128), 768)]
+
+    def place_of(k):
+        return (y + jnp.where(k == 0, 2, jnp.where(k == 1, 1, jnp.where(k == 2, 3, 0)))) % 4
+
+    def spread_back(k, carry):
+        yy = place_of(k)
+
+        def half(hh, inner):
+            at = pl.ds(pl.multiple_of(512 * yy + 256 * hh, 256), 256)
+            raw = cast_up(T5[yy, hh].reshape(256, D))
+            scale = rms_scale(raw)
+            normed = (raw * scale * first_gain).astype(BF)
+            dq = N2[:, pl.ds(pl.multiple_of(256 * yy + 128 * hh, 128), 128)]
+            sub = iota((128, 256), 0)
+            dkt = jnp.where(sub < 64, SC[0:128, at], SC[128:256, at])
+            dvt = S2[0:128, at]
+            dk, dv = dkt.T.astype(BF), dvt.T.astype(BF)
+            dqt = cast_up(dq).T.astype(BF)
+            grad = dot_nt(jnp.concatenate([dq, dk, dv], axis=1), WQ[:, :, :, :, 0:384].reshape(D, 384))
+            VEC[0:1, 0:768] += jnp.sum(grad * raw * scale, axis=0, keepdims=True)
+            S2[128:256, 0:768] += dot(dqt, normed)
+            S2[128:256, 768:1536] += dot(dkt.astype(BF), normed)
+            S2[128:256, 1536:2304] += dot(dvt.astype(BF), normed)
+            T5[yy, hh] = grad.astype(BF).reshape(2, 128, D)
+            return inner
+
+        lax.fori_loop(0, 2, half, 0)
+        comm.copy(T5.at[yy, :, 1 - c], sib_at(yy), base_s + k, sib).start()
         return carry
 
-    def add_b(i, carry):
-        add_low(
-            [W1.at[i // 2, x, i % 2, :, high], WD.at[i // 2, x, i % 2, :, high_d]],
-            [r["RB1"].at[:, i // 2, i % 2], r["RB2"].at[:, i // 2, i % 2]],
-        )
-        return carry
-
-    lax.fori_loop(0, 4, add_a, 0)
-    lax.fori_loop(0, 4, add_b, 0)
-    ff_ra2 = Scatter(
+    base_y = comm.take(3)
+
+    def pass_on(k):
+        yy = (y + (2, 1, 3, 0)[k]) % 4
+        comm.recv(sib_at(yy), base_s + k)
+        for hh in range(2):
+            T5[yy, hh, c] = (cast_up(T5[yy, hh, c]) + cast_up(sib_at(yy)[hh])).astype(BF)
+        if k < 3:
+            comm.send(T5.at[yy, :, c], YR.at[k], base_y + k, comm.peer("y", (2, 1, 3)[k]))
+
+    pl.semaphore_wait(r["free_sem"], 1)
+    for k in range(4):
+        spread_back(k, 0)
+        if k:
+            pass_on(k - 1)
+    for i in range(3):
+        DWQ[:, :, :, :, 128 * i : 128 * i + 128] = S2[128:256, 768 * i : 768 * i + 768].T.astype(BF).reshape(2, 4, 2, 48, 128)
+
+    @pl.when(y == 3)
+    def _():
+        DWQ[:, :, :, :, 384:512] = jnp.zeros((2, 4, 2, 48, 128), BF)
+
+    @pl.when(y < 3)
+    def _():
+        for k in range(4):
+            for cc in range(2):
+                comm.recv(WOR.at[k, cc], base_gr + cc * 4 + k)
+        for cc in range(2):
+            total = cast_up(WOR[0, cc])
+            for k in range(1, 4):
+                total += cast_up(WOR[k, cc])
+            DWQ[cc, :, :, :, 384:512] = total.astype(BF)
+
+    q_ra = Scatter(
+        comm,
+        "z",
+        lambda zz: [DWQ.at[zz % 2, :, zz // 2, :, low]],
+        [r["QA1"]],
+    )
+    q_rb = Scatter(
         comm,
         "x",
-        lambda xx: [W1.at[zl, xx, zh, :, low], WD.at[zl, xx, zh, :, low_d]],
-        [r["SA1"], r["SA2"]],
-    )
-    ff_rb2 = Scatter(
-        comm,
-        "z",
-        lambda zz: [W1.at[zz % 2, x, zz // 2, :, high], WD.at[zz % 2, x, zz // 2, :, high_d]],
-        [r["SB1"], r["SB2"]],
-    )
-    ff_ra2.start()
-    ff_rb2.start()
-    lax.fori_loop(9, STEPS, retreat, 0)
-
+        lambda xx: [DWQ.at[:, xx, :, :, high]],
+        [r["QB1"]],
+    )
     lane = iota((8, 128), 1)
     sub = iota((8, 128), 0)
     diagonals = []
@@ -839,91 +915,67 @@
     VEC[0:1, 768:1024] = spread[0:1, 0:256]
     VEC[1:2, 768:896] = spread[0:1, 256:384]
 
-    YR, DWQ = r["YR"], r["DWQ"]
-    first_gain = r["GS"][0:1, 0:768]
-    base_s = comm.take(4)
-    MID[...] = jnp.zeros((4, 128, D), F32)
-
-    def sib_at(yy):
-        return GU.at[yy // 2, :, :, pl.ds(pl.multiple_of((yy % 2) * 1024, 128), 768)]
-
-    def place_of(k):
-        return (y + jnp.where(k == 0, 2, jnp.where(k == 1, 1, jnp.where(k == 2, 3, 0)))) % 4
-
-    def spread_back(k, carry):
-        yy = place_of(k)
-
-        def half(hh, inner):
-            at = pl.ds(pl.multiple_of(512 * yy + 256 * hh, 256), 256)
-            raw = cast_up(T5[yy, hh].reshape(256, D))
-            scale = rms_scale(raw)
-            normed = (raw * scale * first_gain).astype(BF)
-            dq = N2[:, pl.ds(pl.multiple_of(256 * yy + 128 * hh, 128), 128)]
-            sub = iota((128, 256), 0)
-            dkt = jnp.where(sub < 64, SC[0:128, at], SC[128:256, at])
-            dvt = DVT[:, at]
-            dk, dv = dkt.T.astype(BF), dvt.T.astype(BF)
-            dqt = cast_up(dq).T.astype(BF)
-            grad = dot_nt(jnp.concatenate([dq, dk, dv], axis=1), WQ[...].reshape(D, 384))
-            VEC[0:1, 0:768] += jnp.sum(grad * raw * scale, axis=0, keepdims=True)
-            MID[0] += dot(dqt, normed)
-            MID[1] += dot(dkt.astype(BF), normed)
-            MID[2] += dot(dvt.astype(BF), normed)
-            T5[yy, hh] = grad.astype(BF).reshape(2, 128, D)
-            return inner
-
-        lax.fori_loop(0, 2, half, 0)
-        comm.copy(T5.at[yy, :, 1 - c], sib_at(yy), base_s + k, sib).start()
+    v_z = Scatter(comm, "z", lambda zz: [VEC], [r["V1"]])
+    q_ra.start()
+    q_rb.start()
+    v_z.start()
+    pass_on(3)
+    wd_ra.wait()
+    wd_rb.wait()
+    ff_ra.wait()
+    ff_rb.wait()
+
+    def add_a(i, carry):
+        add_low(
+            [W1.at[zl, i, zh, :, :, low], WD.at[zl, i, zh, :, :, low_d]],
+            [r["RA1"].at[:, i], r["RA2"].at[:, i]],
+        )
+        add_low(
+            [W1.at[i // 2, x, i % 2, :, :, high], WD.at[i // 2, x, i % 2, :, :, high_d]],
+            [r["RB1"].at[:, i // 2, i % 2], r["RB2"].at[:, i // 2, i % 2]],
+        )
         return carry
 
-    lax.fori_loop(0, 4, spread_back, 0)
-    for i in range(3):
-        DWQ[:, :, :, :, 128 * i : 128 * i + 128] = MID[i].T.astype(BF).reshape(2, 4, 2, 48, 128)
-    qa, qb = pl.ds(0, 256), pl.ds(256, 128)
-    q_ra = Scatter(comm, "z", lambda zz: [DWQ.at[zz % 2, :, zz // 2, :, qa]], [r["QA1"]])
-    q_rb = Scatter(comm, "x", lambda xx: [DWQ.at[:, xx, :, :, qb]], [r["QB1"]])
-    v_z = Scatter(comm, "z", lambda zz: [VEC], [r["V1"]])
-    base_y = comm.take(3)
-    for k in range(4):
-        yy = (y + (2, 1, 3, 0)[k]) % 4
-        comm.recv(sib_at(yy), base_s + k)
-        for hh in range(2):
-            T5[yy, hh, c] = (cast_up(T5[yy, hh, c]) + cast_up(sib_at(yy)[hh])).astype(BF)
-        if k < 3:
-            comm.send(T5.at[yy, :, c], YR.at[k], base_y + k, comm.peer("y", (2, 1, 3)[k]))
-        if k == 0:
-            q_ra.start()
-            q_rb.start()
-            v_z.start()
-
-    ff_ra2.wait()
-    ff_rb2.wait()
-    add_low([W1.at[zl, x, zh, :, low], WD.at[zl, x, zh, :, low_d]], [r["SA1"], r["SA2"]])
-    add_low([W1.at[zl, x, zh, :, high], WD.at[zl, x, zh, :, high_d]], [r["SB1"], r["SB2"]])
-    ff_ry = Scatter(
+    lax.fori_loop(0, 4, add_a, 0)
+    ff_ra2 = Scatter(
         comm,
-        "y",
-        lambda yy: [
-            W1.at[zl, x, zh, :, pl.ds(pl.multiple_of(640 * yy, 128), 640)],
-            WD.at[zl, x, zh, pl.ds(16 * yy, 16)],
+        "x",
+        lambda xx: [W1.at[zl, xx, zh, :, :, low], WD.at[zl, xx, zh, :, :, low_d]],
+        [r["SA1"], r["SA2"]],
+    )
+    ff_rb2 = Scatter(
+        comm,
+        "z",
+        lambda zz: [
+            W1.at[zz % 2, x, zz // 2, :, :, high],
+            WD.at[zz % 2, x, zz // 2, :, :, high_d],
         ],
-        [r["SY1"], r["SY2"]],
-    )
-    ff_ry.start()
+        [r["SB1"], r["SB2"]],
+    )
+    ff_ra2.start()
+    ff_rb2.start()
     q_ra.wait()
     q_rb.wait()
     v_z.wait()
     for i in range(4):
-        add_low([DWQ.at[zl, i, zh, :, qa]], [r["QA1"].at[:, i]])
-        add_low([DWQ.at[i // 2, x, i % 2, :, qb]], [r["QB1"].at[:, i // 2, i % 2]])
+        add_low([DWQ.at[zl, i, zh, :, low]], [r["QA1"].at[:, i]])
+        add_low([DWQ.at[i // 2, x, i % 2, :, high]], [r["QB1"].at[:, i // 2, i % 2]])
     VE2 = r["VE2"]
     VE2[...] = VEC[...] + r["V1"][0] + r["V1"][1] + r["V1"][2]
-    q_ra2 = Scatter(comm, "x", lambda xx: [DWQ.at[zl, xx, zh, :, qa]], [r["QA2"]])
-    q_rb2 = Scatter(comm, "z", lambda zz: [DWQ.at[zz % 2, x, zz // 2, :, qb]], [r["QB2"]])
+    q_ra2 = Scatter(comm, "x", lambda xx: [DWQ.at[zl, xx, zh, :, low]], [r["QA2"]])
+    q_rb2 = Scatter(comm, "z", lambda zz: [DWQ.at[zz % 2, x, zz // 2, :, high]], [r["QB2"]])
     v_x = Scatter(comm, "x", lambda xx: [VE2], [r["V2"]])
     q_ra2.start()
     q_rb2.start()
     v_x.start()
+    ff_ra2.wait()
+    ff_rb2.wait()
+    add_low([W1.at[zl, x, zh, :, :, low], WD.at[zl, x, zh, :, :, low_d]], [r["SA1"], r["SA2"]])
+    add_low([W1.at[zl, x, zh, :, :, high], WD.at[zl, x, zh, :, :, high_d]], [r["SB1"], r["SB2"]])
+    ff_ry = Scatter(
+        comm, "y", lambda yy: [W1.at[zl, x, zh, yy], WD.at[zl, x, zh, yy]], [r["SY1"], r["SY2"]]
+    )
+    ff_ry.start()
 
     for k in range(3):
         comm.recv(YR.at[k], base_y + k)
@@ -940,7 +992,7 @@
     comm.send(ZS, ZR, zri, other)
 
     def finish(hh, grad):
-        raw = cast_up(tok[hh])
+        raw = cast_up(TK[hh, c])
         scale = rms_scale(raw)
         gained = grad * first_gain
         mean = jnp.mean(raw * gained, axis=-1, keepdims=True)
@@ -949,12 +1001,14 @@
     finish(zh, summed(zh))
 
     ff_ry.wait()
-    here = pl.ds(pl.multiple_of(640 * y, 128), 640)
-    total = cast_up(W1[zl, x, zh, :, here])
+    total = cast_up(W1[zl, x, zh, y])
     for k in range(3):
         total += cast_up(r["SY1"][k])
-    asm[:, 384:1024] = total
-    total = cast_up(WD[zl, x, zh, pl.ds(16 * y, 16)])
+    asm[:, 512:1024] = total
+    q_ra2.wait()
+    q_rb2.wait()
+    v_x.wait()
+    total = cast_up(WD[zl, x, zh, y])
     for k in range(3):
         total += cast_up(r["SY2"][k])
     r["WDG"][...] = total
@@ -964,11 +1018,8 @@
     comm.send_or_keep(
         r["WDG"], r["dwd_in"], dwi, dev(x, home[0], home[1] * 2 + zl, home[2]), dwi, own_home
     )
-    q_ra2.wait()
-    q_rb2.wait()
-    v_x.wait()
-    for cols, ref, buf in ((slice(0, 256), qa, r["QA2"]), (slice(256, 384), qb, r["QB2"])):
-        total = cast_up(DWQ[zl, x, zh, :, ref])
+    for cols, buf in ((low, r["QA2"]), (high, r["QB2"])):
+        total = cast_up(DWQ[zl, x, zh, :, cols])
         for k in range(3):
             total += cast_up(buf[k])
         asm[:, cols] = total
@@ -1002,38 +1053,40 @@
             for i, name in enumerate(("dwg", "dwu")):
                 for k in range(2):
                     tile = 2 * (2 * yy + k) + cc
-                    at = 384 + 256 * i + 128 * k
+                    at = 512 + 256 * i + 128 * k
                     r[name][:, 128 * tile : 128 * tile + 128] = W2R[d, 0:6, at : at + 128]
             if yy < 3:
                 at = (cc * 3 + yy) * 128
-                r["dwo"][:, at : at + 128] = W2R[d, 0:6, 896:1024]
+                r["dwo"][:, at : at + 128] = W2R[d, 0:6, 384:512]
             rows_sum += W2R[d, 6:8, :]
-    r["dvec"][0:2, :] = rows_sum
-    r["dvec"][2:8, :] = jnp.zeros((6, 1024), F32)
+    table = jnp.concatenate([rows_sum[0:1, 768:1024], rows_sum[1:2, 768:1024], rows_sum[0:1, 0:512]], axis=1)
+    gains = jnp.broadcast_to(jnp.concatenate([rows_sum, jnp.zeros((6, 1024), F32)], axis=0), (8, 1024))
+    gains = pltpu.roll(gains, 1024 - 6 * flat, 1)[0:2, 0:128]
+    table = pltpu.roll(jnp.broadcast_to(table, (8, 1024)), 1024 - 3 * flat, 1)[0:1, 0:128]
+    r["dvec"][...] = jnp.concatenate([gains, table, jnp.zeros((5, 128), F32)], axis=0)
     comm.recv(r["dwd_in"], dwi)
-    r["dwd"][...] = r["dwd_in"][...]
+    names = ("din", "dwq", "dwk", "dwv", "dwo", "dwg", "dwu", "dwd", "dvec")
+    for i, name in enumerate(names):
+        src = r["dwd_in"] if name == "dwd" else r[name]
+        stores.append(pltpu.make_async_copy(src, r["h_" + name], local_sem.at[11 + i]))
+        stores[-1].start()
     for k in range(4):
         yy = (y + (2, 1, 3, 0)[k]) % 4
         comm.copy(T5.at[yy, :, 1 - c], sib_at(yy), base_s + k, sib).wait_send()
     comm.drain()
-    if stop != "all":
-        for n in DEBUG:
-            r["o_" + n][...] = r[n][...]
-
-
-def WO_A(ref):
-    return ref.at[:, pl.ds(0, 1280)]
+    for store in stores:
+        store.wait()
 
 
 INPUTS = [
     ("lens", "s"), ("g1", "s"), ("g2", "s"), ("bt", "s"),
-    ("tok", "v"), ("cot", "v"), ("wq", "v"), ("wk", "v"), ("wv", "v"), ("wo", "v"),
-    ("wg", "v"), ("wu", "v"), ("wd", "v"),
+    ("tok", "a"), ("cot", "a"), ("h_wq", "a"), ("h_wk", "a"), ("h_wv", "a"), ("h_wo", "a"),
+    ("h_wg", "a"), ("h_wu", "a"), ("h_wd", "a"),
 ]
 SCRATCH = [
-    ("W1", ((2, 4, 2, 48, 2560), BF)),
-    ("WD", ((2, 4, 2, 64, 768), BF)),
-    ("WQ", ((2, 4, 2, 48, 384), BF)),
+    ("W1", ((2, 4, 2, 4, 48, 512), BF)),
+    ("WD", ((2, 4, 2, 4, 16, 768), BF)),
+    ("WQ", ((2, 4, 2, 48, 512), BF)),
     ("G5", ((2, 4, 2, 8, 1024), F32)),
     ("T5", ((4, 2, 2, 128, 768), BF)),
     ("TK", ((2, 2, 128, 768), BF)),
@@ -1049,17 +1102,19 @@
     ("QA", ((2, 2048, 128), BF)),
     ("KT", ((2, 128, 2048), BF)),
     ("KN", ((2048, 128), BF)),
-    ("VN", ((2048, 128), BF)),
+    ("VN", ((2048, 256), BF)),
     ("VT", ((128, 2048), BF)),
     ("SC", ((256, 2304), F32)),
-    ("PB", ((12, 256, 2048), BF)),
+    ("S2", ((256, 2304), F32)),
+    ("PB", ((3, 1024, 2304), BF)),
     ("ON", ((2048, 128), BF)),
-    ("LI", ((256, 128), F32)),
+    ("LI", ((1024, 128), F32)),
+    ("GL", ((1024, 128), BF)),
+    ("DL", ((1024, 128), F32)),
     ("A", ((2, 256, 512), BF)),
     ("WOF", ((4, 2, 48, 768), BF)),
     ("POS", ((2, 2, 128, 768), BF)),
     ("POR", ((2, 2, 128, 768), BF)),
-    ("MID", ((4, 128, 768), F32)),
     ("N2", ((256, 1536), BF)),
     ("N2T", ((768, 512), BF)),
     ("HIDT", ((1024, 512), BF)),
@@ -1070,26 +1125,26 @@
     ("ML", ((2, 2, 128, 768), BF)),
     ("DOS", ((4, 2, 256, 128), BF)),
     ("DO", ((2048, 128), BF)),
-    ("RA1", ((3, 4, 48, 1280), BF)),
-    ("RA2", ((3, 4, 64, 384), BF)),
-    ("RB1", ((3, 2, 2, 48, 1280), BF)),
-    ("RB2", ((3, 2, 2, 64, 384), BF)),
-    ("SA1", ((3, 48, 1280), BF)),
-    ("SA2", ((3, 64, 384), BF)),
-    ("SB1", ((3, 48, 1280), BF)),
-    ("SB2", ((3, 64, 384), BF)),
-    ("SY1", ((3, 48, 640), BF)),
+    ("RA1", ((3, 4, 4, 48, 256), BF)),
+    ("RA2", ((3, 4, 4, 16, 384), BF)),
+    ("RB1", ((3, 2, 2, 4, 48, 256), BF)),
+    ("RB2", ((3, 2, 2, 4, 16, 384), BF)),
+    ("SA1", ((3, 4, 48, 256), BF)),
+    ("SA2", ((3, 4, 16, 384), BF)),
+    ("SB1", ((3, 4, 48, 256), BF)),
+    ("SB2", ((3, 4, 16, 384), BF)),
+    ("SY1", ((3, 48, 512), BF)),
     ("SY2", ((3, 16, 768), BF)),
+    ("WOR", ((4, 2, 4, 2, 48, 128), BF)),
     ("HX", ((256, 2304), BF)),
-    ("DVT", ((128, 2048), F32)),
     ("YR", ((3, 2, 128, 768), BF)),
     ("ZS", ((128, 768), BF)),
     ("ZR", ((128, 768), BF)),
-    ("DWQ", ((2, 4, 2, 48, 384), BF)),
+    ("DWQ", ((2, 4, 2, 48, 512), BF)),
     ("QA1", ((3, 4, 48, 256), BF)),
     ("QA2", ((3, 48, 256), BF)),
-    ("QB1", ((3, 2, 2, 48, 128), BF)),
-    ("QB2", ((3, 48, 128), BF)),
+    ("QB1", ((3, 2, 2, 48, 256), BF)),
+    ("QB2", ((3, 48, 256), BF)),
     ("VEC", ((8, 1024), F32)),
     ("V1", ((3, 8, 1024), F32)),
     ("V2", ((3, 8, 1024), F32)),
@@ -1097,12 +1152,6 @@
     ("W2R", ((8, 8, 1024), F32)),
     ("WDG", ((16, 768), F32)),
     ("dwd_in", ((16, 768), F32)),
-    ("send_sem", None),
-    ("recv_sem", None),
-]
-
-
-OUTPUTS = [
     ("out", ((2, 128, 768), BF)),
     ("din", ((2, 128, 768), F32)),
     ("dwq", ((6, 768), F32)),
@@ -1111,30 +1160,51 @@
     ("dwo", ((6, 768), F32)),
     ("dwg", ((6, 2048), F32)),
     ("dwu", ((6, 2048), F32)),
-    ("dwd", ((16, 768), F32)),
-    ("dvec", ((8, 1024), F32)),
+    ("dvec", ((8, 128), F32)),
+    ("wq", ((6, 768), F32)),
+    ("wk", ((6, 768), F32)),
+    ("wv", ((6, 768), F32)),
+    ("wo", ((6, 768), F32)),
+    ("wg", ((6, 2048), F32)),
+    ("wu", ((6, 2048), F32)),
+    ("wd", ((16, 768), F32)),
+    ("free_sem", 0),
+    ("local_sem", 32),
+    ("send_sem", None),
+    ("recv_sem", None),
 ]
-DEBUG = []
-
-
-def outputs_of(stop):
-    if stop == "all":
-        return OUTPUTS
-    shapes = dict((n, s) for n, s in SCRATCH if s is not None)
-    return OUTPUTS + [("o_" + n, shapes[n]) for n in DEBUG]
-
-
-def call_mega(stop, *args):
-    spec = {"s": pl.BlockSpec(memory_space=pltpu.SMEM), "v": pl.BlockSpec(memory_space=pltpu.VMEM)}
-    outs = outputs_of(stop)
+
+
+OUTPUTS = [
+    ("h_out", ((2, 128, 768), BF)),
+    ("h_din", ((2, 128, 768), F32)),
+    ("h_dwq", ((6, 768), F32)),
+    ("h_dwk", ((6, 768), F32)),
+    ("h_dwv", ((6, 768), F32)),
+    ("h_dwo", ((6, 768), F32)),
+    ("h_dwg", ((6, 2048), F32)),
+    ("h_dwu", ((6, 2048), F32)),
+    ("h_dwd", ((16, 768), F32)),
+    ("h_dvec", ((8, 128), F32)),
+]
+
+
+def call_mega(*args):
+    spec = {"s": pl.BlockSpec(memory_space=pltpu.SMEM), "a": pl.BlockSpec(memory_space=pl.ANY)}
+    outs = OUTPUTS
     scratch = []
     for _, s in SCRATCH:
-        scratch.append(pltpu.SemaphoreType.DMA((NSEM,)) if s is None else pltpu.VMEM(s[0], s[1]))
+        if s == 0:
+            scratch.append(pltpu.SemaphoreType.REGULAR)
+        elif s is None or isinstance(s, int):
+            scratch.append(pltpu.SemaphoreType.DMA((s or NSEM,)))
+        else:
+            scratch.append(pltpu.VMEM(s[0], s[1]))
     return pl.pallas_call(
-        functools.partial(mega, stop),
+        mega,
         out_shape=[jax.ShapeDtypeStruct(s[0], s[1]) for _, s in outs],
         in_specs=[spec[k] for _, k in INPUTS],
-        out_specs=[pl.BlockSpec(memory_space=pltpu.VMEM) for _ in outs],
+        out_specs=[pl.BlockSpec(memory_space=pl.ANY) for _ in outs],
         scratch_shapes=scratch,
         name="layer",
         compiler_params=pltpu.CompilerParams(
@@ -1159,7 +1229,6 @@
     bias_table,
 ):
     done = call_mega(
-        "all",
         lengths,
         first_gain,
         second_gain,
@@ -1174,14 +1243,41 @@
         up_weight,
         down_weight,
     )
-    flat = lax.axis_index("rows") * 16 + lax.axis_index("seq")
-    vectors = done[9]
-    table = jnp.concatenate([vectors[0, 768:1024], vectors[1, 768:896]])
-    return (
-        *done[:9],
-        lax.dynamic_slice(vectors, (0, 6 * flat), (1, 6))[0],
-        lax.dynamic_slice(vectors, (1, 6 * flat), (1, 6))[0],
-        lax.dynamic_slice(table, (3 * flat,), (3,)),
+    return hand_out(*done)
+
+
+def hand_out_kernel(*refs):
+    n = len(OUTPUTS)
+    vectors, ins, outs, held, sem = refs[0], refs[1:n], refs[n : 2 * n + 2], refs[2 * n + 2 : -1], refs[-1]
+    loads = [pltpu.make_async_copy(a, b, sem.at[i]) for i, (a, b) in enumerate(zip(ins, held))]
+    copies = [pltpu.make_async_copy(a, b, sem.at[i]) for i, (a, b) in enumerate(zip(held, outs))]
+    for load in loads:
+        load.start()
+    for load, copy in zip(loads, copies):
+        load.wait()
+        copy.start()
+    for row, (ref, width) in enumerate(zip(outs[n - 1 :], (6, 6, 3))):
+        for i in range(width):
+            ref[i] = vectors[row, i]
+    for copy in copies:
+        copy.wait()
+
+
+def hand_out(*done):
+    shapes = [jax.ShapeDtypeStruct(s[0], s[1]) for _, s in OUTPUTS[:-1]]
+    shapes += [jax.ShapeDtypeStruct((n,), F32) for n in (6, 6, 3)]
+    smem, hbm = pl.BlockSpec(memory_space=pltpu.SMEM), pl.BlockSpec(memory_space=pl.ANY)
+    n = len(done) - 1
+    return tuple(
+        pl.pallas_call(
+            hand_out_kernel,
+            out_shape=shapes,
+            in_specs=[smem] + [hbm] * n,
+            out_specs=[hbm] * n + [smem] * 3,
+            scratch_shapes=[pltpu.VMEM(s[0], s[1]) for _, s in OUTPUTS[:-1]]
+            + [pltpu.SemaphoreType.DMA((n,))],
+            name="hand_out",
+        )(done[-1], *done[:-1])
     )
 
 

time: 187 us -> 160 us (0.86)
  Pallas kernels: 175 us -> 159 us
  local copies, waits for them, and re-layouts: 11 us -> 0 us
    pallas_call x1 -> x2, Pallas kernels: 175 us -> 159 us  [the longest x1 155 us: call_mega(): pl.pallas_call(mega, out_shape=[jax.ShapeDtypeStruct(s[0], s[1]) for _, s...]
    unnamed x25 -> x0, local copies, waits for them, and re-layouts: 7.65 us -> none
    squeeze x2 -> x0, local copies, waits for them, and re-layouts: 2.11 us -> none  [the longest x1 1.36 us: per_device(): lax.dynamic_slice(vectors, (1, 6 * flat), (1, 6))[0]]
where the time goes in v3:
time: 160 us; the launch traced here: 159 us
  Pallas kernels  159 us (99%)
    pallas_call x1, Pallas kernels, call_mega(): pl.pallas_call(mega, out_shape=[jax.ShapeDtypeStruct(s[0], s[1]) for _, s...  155 us
    pallas_call x1, Pallas kernels, hand_out(): pl.pallas_call(hand_out_kernel, out_shape=shapes, in_specs=[smem] + [hbm]...  3.56 us

profile of v3, /device:TPU:1, one launch (start us, length us, event | category | flops | bytes accessed | tf_op | source)
XLA Modules:
  0.0 159.5 jit_solution(18203011824114016942)
XLA Ops:
  0.6 155.1 %layer.1 = (bf16[2,128,768]{2,1,0:T(8,128)(2,1)}, f32[2,128,768]{2,1,0:T(8,128)}, f32[6,768]{1,0:T(8,128)}, f32[6,768]{1,0:T(8,128)}, f32[6,768]{1,0:T(8,128)}, ...) custom-call(s32[2]{0:T(128)} %refs_0_.1, f32[6]{0:T(128)} %refs_1_.1, ...), custom_call_target="tpu_custom_call" | custom-call | tf_op jit(solution)/shard_map/layer/pallas_call | solution.py:1203
  155.8 3.6 %hand_out.1 = (bf16[2,128,768]{2,1,0:T(8,128)(2,1)}, f32[2,128,768]{2,1,0:T(8,128)}, f32[6,768]{1,0:T(8,128)}, f32[6,768]{1,0:T(8,128)}, f32[6,768]{1,0:T(8,128)...) custom-call(f32[8,128]{1,0:T(8,128)} %get-tuple-element.22.refs_0_, ...), custom_call_target="tpu_custom_call" | custom-call | tf_op jit(solution)/shard_map/hand_out/pallas_call | solution.py:1272

commit v4 on v3

--- a/solution.py
+++ b/solution.py
@@ -275,16 +275,6 @@
     pl.semaphore_wait(barrier, count)
 
     W1, WD, WQ, G5 = r["W1"], r["WD"], r["WQ"], r["G5"]
-    other = comm.peer("z", 2)
-    zi = comm.take()
-    comm.send(tok.at[1 - zh], T5.at[y, zh, c], zi, other)
-    own_tokens = Ring(
-        comm,
-        "y",
-        lambda yy: [T5.at[yy, zh, c]],
-        lambda yy, k: [T5.at[yy, zh, c, pl.ds(64 * k, 64)]],
-    )
-    own_tokens.start(source=[tok.at[zh]])
     slot = (y % 2) * 4 + zh * 2 + c
     base0 = comm.take(8)
     baser = comm.take(8)
@@ -305,6 +295,16 @@
         r["wdst"], wd_region, wdi, dev(x, wd_to[0], wd_to[1] * 2 + zl, wd_to[2]), wdi, own_wd
     )
 
+    other = comm.peer("z", 2)
+    zi = comm.take()
+    comm.send(tok.at[1 - zh], T5.at[y, zh, c], zi, other)
+    own_tokens = Ring(
+        comm,
+        "y",
+        lambda yy: [T5.at[yy, zh, c]],
+        lambda yy, k: [T5.at[yy, zh, c, pl.ds(64 * k, 64)]],
+    )
+    own_tokens.start(source=[tok.at[zh]])
     pair = comm.take(2)
 
     for j in range(8):
@@ -346,7 +346,6 @@
         comm.recv(T5.at[yy, :, 1 - c], across + k)
 
     cross(0)
-    own_tokens.forward()
     qkv_a1.wait()
     qkv_b1.wait()
     qkv_a2 = Direct(
@@ -357,6 +356,7 @@
     qkv_b2 = Direct(comm, "x", lambda xx: [WQ.at[:, xx, :, :, pl.ds(256, 256)]])
     qkv_a2.start()
     qkv_b2.start()
+    own_tokens.forward()
     ff_y.wait()
     low, high = pl.ds(0, 256), pl.ds(256, 256)
     low_d, high_d = pl.ds(0, 384), pl.ds(384, 384)
@@ -575,14 +575,11 @@
     ff_b2.forward()
     lax.fori_loop(3, STEPS // 2, attend, top_now)
     give(1 - single, 1)
-    ff_a2.wait()
-    ff_b2.wait()
     for yy in range(4):
         for hh in range(2):
             comm.recv(A.at[hh, :, pl.ds(128 * yy, 128)], base_or + yy * 2 + hh)
     comm.recv(TK.at[:, 1 - c], pair)
     comm.recv(CT.at[:, 1 - c], pair + 1)
-    comm.drain()
 
     lane = iota((256, 128), 1)
     for hh in range(2):
@@ -638,6 +635,8 @@
             GU[hh, :, :, pl.ds(both + 256, 256)] = (back * gelu).astype(BF).reshape(2, 128, 256)
         return carry
 
+    ff_a2.wait()
+    ff_b2.wait()
     lax.fori_loop(0, 4, gated, 0)
     PNR, SC = r["PNR"], r["SC"]
     base_n = comm.take(2)
@@ -659,6 +658,7 @@
     for hh in range(2):
         SC[128 * hh : 128 * hh + 128, 0:768] = dot(HX[pl.ds(pl.multiple_of(128 * c, 128), 128), 1024 * hh : 1024 * hh + 1024], down_all)
 
+    low_r, high_r = pl.ds(0, 256), pl.ds(256, 512)
     def down_term(k, carry):
         res = dot(HIDT[pl.ds(pl.multiple_of(256 * k, 256), 256), :], CT[...].reshape(512, D))
         WD[k // 2, pl.ds((2 * k) % 4, 2)] = res.astype(BF).reshape(2, 2, 4, 16, D)
@@ -666,9 +666,9 @@
 
     lax.fori_loop(0, 4, down_term, 0)
     wd_ra = Scatter(
-        comm, "z", lambda zz: [WD.at[zz % 2, :, zz // 2, :, :, low_d]], [r["RA2"]]
-    )
-    wd_rb = Scatter(comm, "x", lambda xx: [WD.at[:, xx, :, :, :, high_d]], [r["RB2"]])
+        comm, "z", lambda zz: [WD.at[zz % 2, :, zz // 2, :, :, low_r]], [r["RA2"]]
+    )
+    wd_rb = Scatter(comm, "x", lambda xx: [WD.at[:, xx, :, :, :, high_r]], [r["RB2"]])
     wd_rb.start()
 
     ML, DOS, DO, VEC = r["ML"], r["DOS"], r["DO"], r["VEC"]
@@ -854,6 +854,13 @@
     for i in range(3):
         DWQ[:, :, :, :, 128 * i : 128 * i + 128] = S2[128:256, 768 * i : 768 * i + 768].T.astype(BF).reshape(2, 4, 2, 48, 128)
 
+    q_ra = Scatter(
+        comm,
+        "z",
+        lambda zz: [DWQ.at[zz % 2, :, zz // 2, :, low]],
+        [r["QA1"]],
+    )
+    q_ra.start()
     @pl.when(y == 3)
     def _():
         DWQ[:, :, :, :, 384:512] = jnp.zeros((2, 4, 2, 48, 128), BF)
@@ -869,12 +876,6 @@
                 total += cast_up(WOR[k, cc])
             DWQ[cc, :, :, :, 384:512] = total.astype(BF)
 
-    q_ra = Scatter(
-        comm,
-        "z",
-        lambda zz: [DWQ.at[zz % 2, :, zz // 2, :, low]],
-        [r["QA1"]],
-    )
     q_rb = Scatter(
         comm,
         "x",
@@ -916,7 +917,6 @@
     VEC[1:2, 768:896] = spread[0:1, 256:384]
 
     v_z = Scatter(comm, "z", lambda zz: [VEC], [r["V1"]])
-    q_ra.start()
     q_rb.start()
     v_z.start()
     pass_on(3)
@@ -927,11 +927,11 @@
 
     def add_a(i, carry):
         add_low(
-            [W1.at[zl, i, zh, :, :, low], WD.at[zl, i, zh, :, :, low_d]],
+            [W1.at[zl, i, zh, :, :, low], WD.at[zl, i, zh, :, :, low_r]],
             [r["RA1"].at[:, i], r["RA2"].at[:, i]],
         )
         add_low(
-            [W1.at[i // 2, x, i % 2, :, :, high], WD.at[i // 2, x, i % 2, :, :, high_d]],
+            [W1.at[i // 2, x, i % 2, :, :, high], WD.at[i // 2, x, i % 2, :, :, high_r]],
             [r["RB1"].at[:, i // 2, i % 2], r["RB2"].at[:, i // 2, i % 2]],
         )
         return carry
@@ -940,7 +940,7 @@
     ff_ra2 = Scatter(
         comm,
         "x",
-        lambda xx: [W1.at[zl, xx, zh, :, :, low], WD.at[zl, xx, zh, :, :, low_d]],
+        lambda xx: [W1.at[zl, xx, zh, :, :, low], WD.at[zl, xx, zh, :, :, low_r]],
         [r["SA1"], r["SA2"]],
     )
     ff_rb2 = Scatter(
@@ -948,7 +948,7 @@
         "z",
         lambda zz: [
             W1.at[zz % 2, x, zz // 2, :, :, high],
-            WD.at[zz % 2, x, zz // 2, :, :, high_d],
+            WD.at[zz % 2, x, zz // 2, :, :, high_r],
         ],
         [r["SB1"], r["SB2"]],
     )
@@ -970,8 +970,8 @@
     v_x.start()
     ff_ra2.wait()
     ff_rb2.wait()
-    add_low([W1.at[zl, x, zh, :, :, low], WD.at[zl, x, zh, :, :, low_d]], [r["SA1"], r["SA2"]])
-    add_low([W1.at[zl, x, zh, :, :, high], WD.at[zl, x, zh, :, :, high_d]], [r["SB1"], r["SB2"]])
+    add_low([W1.at[zl, x, zh, :, :, low], WD.at[zl, x, zh, :, :, low_r]], [r["SA1"], r["SA2"]])
+    add_low([W1.at[zl, x, zh, :, :, high], WD.at[zl, x, zh, :, :, high_r]], [r["SB1"], r["SB2"]])
     ff_ry = Scatter(
         comm, "y", lambda yy: [W1.at[zl, x, zh, yy], WD.at[zl, x, zh, yy]], [r["SY1"], r["SY2"]]
     )
@@ -1126,13 +1126,13 @@
     ("DOS", ((4, 2, 256, 128), BF)),
     ("DO", ((2048, 128), BF)),
     ("RA1", ((3, 4, 4, 48, 256), BF)),
-    ("RA2", ((3, 4, 4, 16, 384), BF)),
+    ("RA2", ((3, 4, 4, 16, 256), BF)),
     ("RB1", ((3, 2, 2, 4, 48, 256), BF)),
-    ("RB2", ((3, 2, 2, 4, 16, 384), BF)),
+    ("RB2", ((3, 2, 2, 4, 16, 512), BF)),
     ("SA1", ((3, 4, 48, 256), BF)),
-    ("SA2", ((3, 4, 16, 384), BF)),
+    ("SA2", ((3, 4, 16, 256), BF)),
     ("SB1", ((3, 4, 48, 256), BF)),
-    ("SB2", ((3, 4, 16, 384), BF)),
+    ("SB2", ((3, 4, 16, 512), BF)),
     ("SY1", ((3, 48, 512), BF)),
     ("SY2", ((3, 16, 768), BF)),
     ("WOR", ((4, 2, 4, 2, 48, 128), BF)),

time: 160 us -> 155 us (0.969)
  Pallas kernels: 159 us -> 153 us
    pallas_call x1, Pallas kernels: 155 us -> 150 us  [call_mega(): pl.pallas_call(mega, out_shape=[jax.ShapeDtypeStruct(s[0], s[1]) for _, s...]
where the time goes in v4:
time: 155 us; the launch traced here: 154 us
  Pallas kernels  153 us (99%)
    pallas_call x1, Pallas kernels, call_mega(): pl.pallas_call(mega, out_shape=[jax.ShapeDtypeStruct(s[0], s[1]) for _, s...  150 us
    pallas_call x1, Pallas kernels, hand_out(): pl.pallas_call(hand_out_kernel, out_shape=shapes, in_specs=[smem] + [hbm]...  3.56 us

profile of v4, /device:TPU:1, one launch (start us, length us, event | category | flops | bytes accessed | tf_op | source)
XLA Modules:
  0.0 154.3 jit_solution(15266249706528909580)
XLA Ops:
  0.6 149.9 %layer.1 = (bf16[2,128,768]{2,1,0:T(8,128)(2,1)}, f32[2,128,768]{2,1,0:T(8,128)}, f32[6,768]{1,0:T(8,128)}, f32[6,768]{1,0:T(8,128)}, f32[6,768]{1,0:T(8,128)}, ...) custom-call(s32[2]{0:T(128)} %refs_0_.1, f32[6]{0:T(128)} %refs_1_.1, ...), custom_call_target="tpu_custom_call" | custom-call | tf_op jit(solution)/shard_map/layer/pallas_call | solution.py:1203
  150.6 3.6 %hand_out.1 = (bf16[2,128,768]{2,1,0:T(8,128)(2,1)}, f32[2,128,768]{2,1,0:T(8,128)}, f32[6,768]{1,0:T(8,128)}, f32[6,768]{1,0:T(8,128)}, f32[6,768]{1,0:T(8,128)...) custom-call(f32[8,128]{1,0:T(8,128)} %get-tuple-element.22.refs_0_, ...), custom_call_target="tpu_custom_call" | custom-call | tf_op jit(solution)/shard_map/hand_out/pallas_call | solution.py:1272

commit v5 on v4

--- a/solution.py
+++ b/solution.py
@@ -180,6 +180,15 @@
     for threshold in LIMITS:
         bucket_sum = bucket_sum + jnp.where(distance >= threshold, 1, 0)
     return bucket_sum
+
+
+def fold_rows(two):
+    return jnp.concatenate([two[k : k + 1, 256 * i : 256 * i + 256] for k in range(2) for i in range(4)], axis=0)
+
+
+def unfold_rows(eight):
+    rows = [jnp.concatenate([eight[4 * k + i : 4 * k + i + 1] for i in range(4)], axis=1) for k in range(2)]
+    return jnp.concatenate(rows, axis=0)
 
 
 def rms_scale(values):
@@ -315,7 +324,7 @@
         asm[6 * j : 6 * j + 6, :] = w0[j, 0:6, :]
         gsum += w0[j, 6:8, :]
     WQ[zl, x, zh] = asm[:, 0:512].astype(BF)
-    G5[zl, x, zh] = jnp.concatenate([gsum, jnp.zeros((6, 1024), F32)], axis=0)
+    G5[zl, x, zh] = fold_rows(gsum)
     W1[zl, x, zh, y] = asm[:, 512:1024].astype(BF)
     qkv_a1 = Direct(comm, "x", lambda xx: [WQ.at[zl, xx, zh, :, pl.ds(0, 256)], G5.at[zl, xx, zh]])
     qkv_b1 = Direct(comm, "z", lambda zz: [WQ.at[zz % 2, x, zz // 2, :, pl.ds(256, 256)]])
@@ -359,7 +368,7 @@
     own_tokens.forward()
     ff_y.wait()
     low, high = pl.ds(0, 256), pl.ds(256, 256)
-    low_d, high_d = pl.ds(0, 384), pl.ds(384, 384)
+    low_d, high_d = pl.ds(0, 256), pl.ds(256, 512)
     ff_a1 = Direct(
         comm, "x", lambda xx: [W1.at[zl, xx, zh, :, :, low], WD.at[zl, xx, zh, :, :, low_d]]
     )
@@ -396,12 +405,13 @@
             pl.when(here & (y < 3))(keep.start)
             pl.when(jnp.logical_not(here) & (y < 3))(cp.start)
             comm.pending.append((cp, here | (y == 3)))
-    total = jnp.zeros((8, 1024), F32)
+    total = jnp.zeros((8, 256), F32)
     for a in range(2):
         for b in range(4):
             for e in range(2):
                 total += G5[a, b, e]
-    r["GS"][...] = total
+    total = unfold_rows(total)
+    r["GS"][0:2, :] = total
     h0 = first_head(t)
     table_row = jnp.concatenate([total[0:1, 768:1024], total[1:2, 768:896]], axis=1)
     table_row = jnp.broadcast_to(table_row, (8, 384))
@@ -916,7 +926,9 @@
     VEC[0:1, 768:1024] = spread[0:1, 0:256]
     VEC[1:2, 768:896] = spread[0:1, 256:384]
 
-    v_z = Scatter(comm, "z", lambda zz: [VEC], [r["V1"]])
+    VP = r["VP"]
+    VP[...] = fold_rows(VEC[0:2, :])
+    v_z = Scatter(comm, "z", lambda zz: [VP], [r["V1"]])
     q_rb.start()
     v_z.start()
     pass_on(3)
@@ -961,7 +973,7 @@
         add_low([DWQ.at[zl, i, zh, :, low]], [r["QA1"].at[:, i]])
         add_low([DWQ.at[i // 2, x, i % 2, :, high]], [r["QB1"].at[:, i // 2, i % 2]])
     VE2 = r["VE2"]
-    VE2[...] = VEC[...] + r["V1"][0] + r["V1"][1] + r["V1"][2]
+    VE2[...] = VP[...] + r["V1"][0] + r["V1"][1] + r["V1"][2]
     q_ra2 = Scatter(comm, "x", lambda xx: [DWQ.at[zl, xx, zh, :, low]], [r["QA2"]])
     q_rb2 = Scatter(comm, "z", lambda zz: [DWQ.at[zz % 2, x, zz // 2, :, high]], [r["QB2"]])
     v_x = Scatter(comm, "x", lambda xx: [VE2], [r["V2"]])
@@ -1023,7 +1035,7 @@
         for k in range(3):
             total += cast_up(buf[k])
         asm[:, cols] = total
-    sums = VE2[...] + r["V2"][0] + r["V2"][1] + r["V2"][2]
+    sums = unfold_rows(VE2[...] + r["V2"][0] + r["V2"][1] + r["V2"][2])
     W2R = r["W2R"]
     base_h = comm.take(8)
     base_hr = comm.take(8)
@@ -1087,7 +1099,7 @@
     ("W1", ((2, 4, 2, 4, 48, 512), BF)),
     ("WD", ((2, 4, 2, 4, 16, 768), BF)),
     ("WQ", ((2, 4, 2, 48, 512), BF)),
-    ("G5", ((2, 4, 2, 8, 1024), F32)),
+    ("G5", ((2, 4, 2, 8, 256), F32)),
     ("T5", ((4, 2, 2, 128, 768), BF)),
     ("TK", ((2, 2, 128, 768), BF)),
     ("CT", ((2, 2, 128, 768), BF)),
@@ -1146,9 +1158,10 @@
     ("QB1", ((3, 2, 2, 48, 256), BF)),
     ("QB2", ((3, 48, 256), BF)),
     ("VEC", ((8, 1024), F32)),
-    ("V1", ((3, 8, 1024), F32)),
-    ("V2", ((3, 8, 1024), F32)),
-    ("VE2", ((8, 1024), F32)),
+    ("V1", ((3, 8, 256), F32)),
+    ("V2", ((3, 8, 256), F32)),
+    ("VE2", ((8, 256), F32)),
+    ("VP", ((8, 256), F32)),
     ("W2R", ((8, 8, 1024), F32)),
     ("WDG", ((16, 768), F32)),
     ("dwd_in", ((16, 768), F32)),

time: 155 us -> 147 us (0.948)
  Pallas kernels: 153 us -> 146 us
    pallas_call x1, Pallas kernels: 150 us -> 143 us  [call_mega(): pl.pallas_call(mega, out_shape=[jax.ShapeDtypeStruct(s[0], s[1]) for _, s...]
where the time goes in v5:
time: 147 us
  Pallas kernels  146 us (99%)
    pallas_call x1, Pallas kernels, call_mega(): pl.pallas_call(mega, out_shape=[jax.ShapeDtypeStruct(s[0], s[1]) for _, s...  143 us
    pallas_call x1, Pallas kernels, hand_out(): pl.pallas_call(hand_out_kernel, out_shape=shapes, in_specs=[smem] + [hbm]...  3.56 us

profile of v5, /device:TPU:1, one launch (start us, length us, event | category | flops | bytes accessed | tf_op | source)
XLA Modules:
  0.0 147.2 jit_solution(5937112258522273002)
XLA Ops:
  0.6 142.9 %layer.1 = (bf16[2,128,768]{2,1,0:T(8,128)(2,1)}, f32[2,128,768]{2,1,0:T(8,128)}, f32[6,768]{1,0:T(8,128)}, f32[6,768]{1,0:T(8,128)}, f32[6,768]{1,0:T(8,128)}, ...) custom-call(s32[2]{0:T(128)} %refs_0_.1, f32[6]{0:T(128)} %refs_1_.1, ...), custom_call_target="tpu_custom_call" | custom-call | tf_op jit(solution)/shard_map/layer/pallas_call | solution.py:1216
  143.5 3.6 %hand_out.1 = (bf16[2,128,768]{2,1,0:T(8,128)(2,1)}, f32[2,128,768]{2,1,0:T(8,128)}, f32[6,768]{1,0:T(8,128)}, f32[6,768]{1,0:T(8,128)}, f32[6,768]{1,0:T(8,128)...) custom-call(f32[8,128]{1,0:T(8,128)} %get-tuple-element.22.refs_0_, ...), custom_call_target="tpu_custom_call" | custom-call | tf_op jit(solution)/shard_map/hand_out/pallas_call | solution.py:1285

commit v6 on v5

--- a/solution.py
+++ b/solution.py
@@ -580,10 +580,10 @@
     single = (3 * t + 1) % 2
     top_now = lax.fori_loop(0, 2, attend, first_scores(0))
     give(single, 0)
-    top_now = lax.fori_loop(2, 3, attend, top_now)
+    top_now = lax.fori_loop(2, 4, attend, top_now)
     ff_a2.forward()
     ff_b2.forward()
-    lax.fori_loop(3, STEPS // 2, attend, top_now)
+    lax.fori_loop(4, STEPS // 2, attend, top_now)
     give(1 - single, 1)
     for yy in range(4):
         for hh in range(2):

time: 147 us -> 146 us (level)
    pallas_call x1, Pallas kernels: 143 us -> 141 us  [call_mega(): pl.pallas_call(mega, out_shape=[jax.ShapeDtypeStruct(s[0], s[1]) for _, s...]
where the time goes in v6:
time: 146 us
  Pallas kernels  145 us (99%)
    pallas_call x1, Pallas kernels, call_mega(): pl.pallas_call(mega, out_shape=[jax.ShapeDtypeStruct(s[0], s[1]) for _, s...  141 us
    pallas_call x1, Pallas kernels, hand_out(): pl.pallas_call(hand_out_kernel, out_shape=shapes, in_specs=[smem] + [hbm]...  3.56 us

profile of v6, /device:TPU:1, one launch (start us, length us, event | category | flops | bytes accessed | tf_op | source)
XLA Modules:
  0.0 145.6 jit_solution(14386015828673246361)
XLA Ops:
  0.6 141.2 %layer.1 = (bf16[2,128,768]{2,1,0:T(8,128)(2,1)}, f32[2,128,768]{2,1,0:T(8,128)}, f32[6,768]{1,0:T(8,128)}, f32[6,768]{1,0:T(8,128)}, f32[6,768]{1,0:T(8,128)}, ...) custom-call(s32[2]{0:T(128)} %refs_0_.1, f32[6]{0:T(128)} %refs_1_.1, ...), custom_call_target="tpu_custom_call" | custom-call | tf_op jit(solution)/shard_map/layer/pallas_call | solution.py:1216
  141.8 3.6 %hand_out.1 = (bf16[2,128,768]{2,1,0:T(8,128)(2,1)}, f32[2,128,768]{2,1,0:T(8,128)}, f32[6,768]{1,0:T(8,128)}, f32[6,768]{1,0:T(8,128)}, f32[6,768]{1,0:T(8,128)...) custom-call(f32[8,128]{1,0:T(8,128)} %get-tuple-element.22.refs_0_, ...), custom_call_target="tpu_custom_call" | custom-call | tf_op jit(solution)/shard_map/hand_out/pallas_call | solution.py:1285
